TPU v7x, 32 devices: a whole 2x2x4 slice. The times are simulated.
32 devices in a mesh: term: 8 (over y, x, core), sector: 4 (over z).
Axes of the slice: x: 2, y: 2, z: 4, core: 2. Of those that a mesh axis runs over, the one named last changes fastest.
Arguments:
- psi: float32 [8, 384, 4, 384], P('sector'), may hold values from -6 to 6
- precond: bfloat16 [8, 384, 4, 384], P('sector'), may hold values from 1 to 10
- left_environment_block: float32 [16, 8, 384, 384], P('term', 'sector'), may hold values from -0.3125 to 0.3125
- right_env: float32 [16, 8, 384, 384], P('term', 'sector'), may hold values from -0.3125 to 0.3125
- term_operators: float32 [16, 4, 4], P('term'), may hold values from -3 to 3
- term_charge: int32 [16], P('term'), may hold values from -1 to 1, as said below
- sector_sizes: int32 [8], P('sector'), may hold values from 128 to 384, as said below
- sector_energy: float32 [8], P('sector'), may hold values from 2 to 20
Outputs:
- psi_next: float32 [8, 384, 4, 384], P('sector', 'term')
- energies: float32 [1], replicated
Inputs may be any that keep to these rules, and one draw needn't show every extreme that they name: `term_charge`: every value -1, 0 and 1 occurs. `sector_sizes`: some sector has exactly 384 states and some exactly 128.
All inputs are finite; a program needn't handle non-finite values.
Results may differ from a plain program's by a relative error of at most 0.0003.
Values sent between devices are 32-bit elements; how exact they have to be, the bound alone decides.
No kernel may reach another device: no remote copies, remote signals or barrier semaphores. Data moves between devices by JAX's collectives and lax.ppermute only.
A program may use at most 128 MiB of HBM per device.

v0:
```python
import jax
import jax.numpy as jnp
from jax import lax
from jax.sharding import PartitionSpec as P

EPSILON = 1e-06
TOP_LEVEL = lax.Precision.HIGHEST


def with_halo(block, sides, width):
    for axis, dim in sides:
        count = lax.axis_size(axis)
        forward = [(i, i + 1) for i in range(count - 1)]
        backward = [(target, source) for source, target in forward]
        low = lax.ppermute(
            lax.slice_in_dim(block, block.shape[dim] - width, None, axis=dim), axis, forward
        )
        high = lax.ppermute(lax.slice_in_dim(block, 0, width, axis=dim), axis, backward)
        block = jnp.concatenate([low, block, high], axis=dim)
    return block


def term_partials(state, left_environment_block, right_env, term_operators, term_charge):
    sec_local = state.shape[0]
    extended = with_halo(state, (("sector", 0),), 1)

    def single_term(total, inputs):
        left_side, right, operator, charge = inputs
        source_sector = lax.dynamic_slice_in_dim(extended, 1 - charge, sec_local, 0)
        leading_item = jnp.einsum("qom,qmsg->qosg", left_side, source_sector, precision=TOP_LEVEL)
        second = jnp.einsum("pr,tarb->tapb", operator, leading_item, precision=TOP_LEVEL)
        third = jnp.einsum("tape,teb->tapb", second, right, precision=TOP_LEVEL)
        return (total + third, None)

    total, _ = lax.scan(
        single_term,
        jnp.zeros_like(state),
        (left_environment_block, right_env, term_operators, term_charge),
    )
    return total


def body(
    psi,
    precond,
    left_environment_block,
    right_env,
    term_operators,
    term_charge,
    sector_sizes,
    sector_energy,
):
    sec_local, block_size, phys, _ = psi.shape
    shared_rows = block_size // lax.axis_size("term")
    numel = sec_local * lax.axis_size("sector") * block_size * phys * block_size
    positions = jnp.arange(block_size, dtype=jnp.int32)
    inside = positions[None, :] < sector_sizes[:, None]
    valid_mask = (inside[:, :, None, None] & inside[:, None, None, :]).astype(jnp.float32)
    energy_col = sector_energy[:, None, None, None]
    row_start = lax.axis_index("term") * shared_rows
    state = psi * valid_mask
    partial_sum = term_partials(
        state, left_environment_block, right_env, term_operators, term_charge
    )
    total = lax.psum(partial_sum, "term")
    image = (total + energy_col * state) * valid_mask
    correlation, weight = lax.psum((jnp.sum(state * image), jnp.sum(state * state)), "sector")
    energy = correlation / weight
    moved = state - (image - energy * state) / precond.astype(jnp.float32)
    square = lax.psum(jnp.sum(moved * moved), "sector")
    state = moved * lax.rsqrt(square / numel + EPSILON)
    result = lax.dynamic_slice_in_dim(state, row_start, shared_rows, 1)
    return (result, jnp.stack([energy]))


def solution(mesh):
    in_specs = (
        P("sector", None, None, None),
        P("sector", None, None, None),
        P("term", "sector", None, None),
        P("term", "sector", None, None),
        P("term", None, None),
        P("term"),
        P("sector"),
        P("sector"),
    )
    out_specs = (P("sector", "term", None, None), P())
    return jax.shard_map(body, mesh=mesh, in_specs=in_specs, out_specs=out_specs, check_vma=False)
```

profile of v0, /device:TPU:0, one launch (start us, length us, event | category | flops | bytes accessed | tf_op | source)
XLA Modules:
  0.0 301.8 jit_solution(121484640755926830)
XLA Ops:
  7.2 0.0 all-reduce.3.cloned.1.call-start
  7.2 0.7 iota_compare_fusion
  7.9 0.2 and_convert_fusion
  8.1 3.6 %broadcast_multiply_fusion = f32[2,384,4,384]{3,2,1,0:T(4,128)S(1)} fusion(f32[2,384,4,384]{3,2,1,0:T(4,128)} %param.10, f32[2,384,384]{2,1,0:T(8,128)S(1)} %and_convert_fusion), kind=kLoop, calls=%fused_computation.24 | loop fusion | flops 1179648 | bytes 10616832 | tf_op jit(solution)/shard_map/mul | solution.py:61
  11.7 0.0 copy-start
  11.7 3.4 %fusion.18 = (f32[1,384,4,384]{3,2,1,0:T(4,128)}, f32[1,384,4,384]{3,2,1,0:T(4,128)}) fusion(f32[2,384,4,384]{3,2,1,0:T(4,128)S(1)} %broadcast_multiply_fusion), kind=kLoop, calls=%fused_computation.28 | loop fusion | bytes 9437184 | tf_op jit(solution)/shard_map/slice | solution.py:16
  15.1 0.2 copy-done
  15.3 6.4 %collective-permute-start = (f32[1,384,4,384]{3,2,1,0:T(4,128)}, f32[1,384,4,384]{3,2,1,0:T(4,128)}, u32[]{:S(2)}, u32[]{:S(2)}) collective-permute-start(f32[1,384,4,384]{3,2,1,0:T(4,128)} %get-tuple-element.136), channel_id=1, source_target_pairs={{0,1},{1,2},{2,3},{4,5},{5,6},{6,7},{8,9},{9,10},{10,11},{12,13},{... | collective-permute-start | bytes 7077896 | tf_op jit(solution)/shard_map/ppermute | solution.py:15
  21.7 1.3 collective-permute-start.1
  22.9 0.0 copy-start.1
  23.0 0.0 copy-start.3
  23.0 0.0 copy-start.5
  23.0 48.0 %collective-permute-done = f32[1,384,4,384]{3,2,1,0:T(4,128)} collective-permute-done((f32[1,384,4,384]{3,2,1,0:T(4,128)}, f32[1,384,4,384]{3,2,1,0:T(4,128)}, u32[]{:S(2)}, u32[]{:S(2)}) %collective-permute-start) | collective-permute-done | bytes 2359328 | tf_op jit(solution)/shard_map/ppermute | solution.py:15
  71.0 5.6 %collective-permute-done.1 = f32[1,384,4,384]{3,2,1,0:T(4,128)} collective-permute-done((f32[1,384,4,384]{3,2,1,0:T(4,128)}, f32[1,384,4,384]{3,2,1,0:T(4,128)}, u32[]{:S(2)}, u32[]{:S(2)}) %collective-permute-start.1) | collective-permute-done | bytes 2359328 | tf_op jit(solution)/shard_map/ppermute | solution.py:18
  76.6 9.8 %pad_maximum_fusion = f32[4,384,4,384]{3,2,1,0:T(4,128)} fusion(f32[1,384,4,384]{3,2,1,0:T(4,128)} %collective-permute-done.1, f32[2,384,4,384]{3,2,1,0:T(4,128)} %copy-done, f32[1,384,4,384]{3,2,1,0:T(4,128)} %collective-permute-done), kind=kLoop, calls=%fused_computation.18 | loop fusion | flops 4718592 | bytes 18874368 | tf_op jit(solution)/shard_map/concatenate | solution.py:19
  86.3 0.0 copy-done.1
  86.3 0.0 copy-done.3
  86.3 0.0 copy-done.5
  86.3 73.2 %while.13 = (s32[]{:T(128)}, f32[2,384,4,384]{3,1,2,0:T(8,128)}, f32[2,2,384,384]{3,2,1,0:T(8,128)S(1)}, s32[2]{0:T(128)S(1)}, f32[4,384,4,384]{3,2,1,0:T(4,128)...) while((s32[]{:T(128)}, f32[2,384,4,384]{3,1,2,0:T(8,128)}, ...), condition=%wide.region_1.2_spmd.clone, body=%wide.region_0.1_spmd.clone.sunk | while | flops 10930618368 | bytes 44829372 | solution.py:35
  86.5 0.6 dynamic_slice.66
  88.4 3.2 %constant_dynamic-slice_fusion.2 = f32[2,384,4,384]{3,2,1,0:T(4,128)S(1)} fusion(f32[4,384,4,384]{3,2,1,0:T(4,128)} %get-tuple-element.207, s32[]{:T(128)S(6)} %select_n.12), kind=kLoop, calls=%fused_computation.16.clone.1 | loop fusion | bytes 9437188 | tf_op jit(solution)/shard_map/while/body/eval_jaxpr/dynamic_slice | solution.py:29
  91.6 7.7 %fusion.33 = f32[2,384,4,384]{3,1,2,0:T(8,128)S(1)} fusion(f32[2,384,4,384]{3,2,1,0:T(4,128)S(1)} %constant_dynamic-slice_fusion.2, f32[2,2,384,384]{3,2,1,0:T(8,128)S(1)} %get-tuple-element.205, s32[]{:T(128)} %get-tuple-element.192), kind=kOutput, calls=%fused_computation.5.clone.1 | convolution fusion | flops 5435817984 | bytes 10616836 | tf_op jit(solution)/shard_map/while/body/eval_jaxpr/qom,qmsg->qosg/dot_general | solution.py:30
  99.3 10.8 %fusion.34 = f32[2,384,384,4]{2,3,1,0:T(4,128)} fusion(f32[2,384,4,384]{3,1,2,0:T(8,128)S(1)} %fusion.33, f32[2,4,4]{2,1,0:T(4,128)S(1)} %get-tuple-element.208, s32[]{:T(128)} %get-tuple-element.192), kind=kOutput, calls=%fused_computation.3.clone.1 | convolution fusion | flops 56623104 | bytes 9439236 | tf_op jit(solution)/shard_map/while/body/eval_jaxpr/pr,tarb->tapb/dot_general | solution.py:31
  110.1 12.6 %select_add_fusion.2 = f32[2,384,4,384]{3,1,2,0:T(8,128)} fusion(f32[2,384,4,384]{3,1,2,0:T(8,128)} %get-tuple-element.193, pred[]{:T(512)S(6)} %compare.3, f32[2,384,384,4]{2,3,1,0:T(4,128)} %fusion.34, f32[2,2,384,384]{3,2,1,0:T(8,128)} %get-tuple-element.209, s32[]{:T(128)} %get-tuple-element.192), kind=kOutput, calls=%fused_computation.7.clone.1 | convolution fusion | flops 5438177280 | bytes 15335937 | tf_op jit(solution)/shard_map/while/body/eval_jaxpr/tape,teb->tapb/dot_general | solution.py:32
  122.8 0.6 dynamic_slice.66
  124.7 3.2 %constant_dynamic-slice_fusion.2 = f32[2,384,4,384]{3,2,1,0:T(4,128)S(1)} fusion(f32[4,384,4,384]{3,2,1,0:T(4,128)} %get-tuple-element.207, s32[]{:T(128)S(6)} %select_n.12), kind=kLoop, calls=%fused_computation.16.clone.1 | loop fusion | bytes 9437188 | tf_op jit(solution)/shard_map/while/body/eval_jaxpr/dynamic_slice | solution.py:29
  127.8 7.7 %fusion.33 = f32[2,384,4,384]{3,1,2,0:T(8,128)S(1)} fusion(f32[2,384,4,384]{3,2,1,0:T(4,128)S(1)} %constant_dynamic-slice_fusion.2, f32[2,2,384,384]{3,2,1,0:T(8,128)S(1)} %get-tuple-element.205, s32[]{:T(128)} %get-tuple-element.192), kind=kOutput, calls=%fused_computation.5.clone.1 | convolution fusion | flops 5435817984 | bytes 10616836 | tf_op jit(solution)/shard_map/while/body/eval_jaxpr/qom,qmsg->qosg/dot_general | solution.py:30
  135.6 10.8 %fusion.34 = f32[2,384,384,4]{2,3,1,0:T(4,128)} fusion(f32[2,384,4,384]{3,1,2,0:T(8,128)S(1)} %fusion.33, f32[2,4,4]{2,1,0:T(4,128)S(1)} %get-tuple-element.208, s32[]{:T(128)} %get-tuple-element.192), kind=kOutput, calls=%fused_computation.3.clone.1 | convolution fusion | flops 56623104 | bytes 9439236 | tf_op jit(solution)/shard_map/while/body/eval_jaxpr/pr,tarb->tapb/dot_general | solution.py:31
  146.4 13.1 %select_add_fusion.2 = f32[2,384,4,384]{3,1,2,0:T(8,128)} fusion(f32[2,384,4,384]{3,1,2,0:T(8,128)} %get-tuple-element.193, pred[]{:T(512)S(6)} %compare.3, f32[2,384,384,4]{2,3,1,0:T(4,128)} %fusion.34, f32[2,2,384,384]{3,2,1,0:T(8,128)} %get-tuple-element.209, s32[]{:T(128)} %get-tuple-element.192), kind=kOutput, calls=%fused_computation.7.clone.1 | convolution fusion | flops 5438177280 | bytes 15335937 | tf_op jit(solution)/shard_map/while/body/eval_jaxpr/tape,teb->tapb/dot_general | solution.py:32
  159.5 7.5 %copy.10 = f32[2,384,4,384]{3,2,1,0:T(4,128)} copy(f32[2,384,4,384]{3,1,2,0:T(8,128)} %get-tuple-element.91) | data formatting | bytes 9437184 | tf_op jit(solution)/shard_map/while | solution.py:35
  167.0 0.0 copy-start.4
  167.0 0.0 all-reduce.3.cloned.1.call-update
  167.1 0.0 copy-start.2
  167.1 85.7 %all-reduce.3.cloned.1.call-done = f32[2,384,4,384]{3,2,1,0:T(4,128)} async-done(((f32[2,384,4,384]{3,2,1,0:T(4,128)}), f32[2,384,4,384]{3,2,1,0:T(4,128)}) %all-reduce.3.cloned.1.call-update) | async-done | bytes 4718608 | tf_op jit(solution)/shard_map/psum | solution.py:65
  252.8 0.0 copy-done.4
  252.8 6.5 %multiply_reduce_fusion.1 = (f32[]{:T(128)}, f32[]{:T(128)}) fusion(f32[2,384,384]{2,1,0:T(8,128)S(1)} %and_convert_fusion, f32[2,384,4,384]{3,2,1,0:T(4,128)} %all-reduce.3.cloned.1.call-done, f32[2]{0:T(128)S(1)} %copy-done.4, f32[2,384,4,384]{3,2,1,0:T(4,128)} %param.10), kind=kLoop, calls=%fused_computation.21 | loop fusion | flops 9437182 | bytes 10616848 | tf_op jit(solution)/shard_map/reduce_sum | solution.py:67
  259.3 12.3 %all-reduce = (f32[]{:T(128)}, f32[]{:T(128)}) all-reduce(f32[]{:T(128)} %get-tuple-element.117, f32[]{:T(128)} %get-tuple-element.116), channel_id=1, replica_groups=mesh['term'=8,'sector'=4] {'sector'}, use_global_device_ids=true, to_apply=%region_4.5 | all-reduce | flops 2 | bytes 16 | tf_op jit(solution)/shard_map/psum | solution.py:67
  273.0 0.0 copy-done.2
  273.0 9.2 %multiply_reduce_fusion = (f32[]{:T(128)}, f32[2,384,4,384]{3,2,1,0:T(4,128)}) fusion(bf16[2,384,4,384]{3,2,1,0:T(4,128)(2,1)S(1)} %copy-done.2, f32[]{:T(128)} %div.9, f32[2,384,384]{2,1,0:T(8,128)S(1)} %and_convert_fusion, f32[2,384,4,384]{3,2,1,0:T(4,128)} %all-reduce.3.cloned.1.call-done, f32[2]{0:T(128)S(1)} %copy-done.4, f32[2,384,4,384]{3,2,1,0:T(4,128)} %param.10), kind=kLoop, calls=%fused_computation.19 | loop fusion | flops 12976127 | bytes 17694736 | tf_op jit(solution)/shard_map/reduce_sum | solution.py:70
  282.2 9.0 %psum.31 = f32[]{:T(128)} all-reduce(f32[]{:T(128)} %get-tuple-element.134), channel_id=1, replica_groups=mesh['term'=8,'sector'=4] {'sector'}, use_global_device_ids=true, to_apply=%region_8.9 | all-reduce | flops 1 | bytes 8 | tf_op jit(solution)/shard_map/psum | solution.py:70
  291.9 2.0 dynamic-slice_multiply_fusion
  (1 shorter events, 0.0 us)
Async XLA Ops:
  7.2 245.7 %all-reduce.3.cloned.1.call-start = ((), (), s32[]{:S(2)}) async-start(), calls=%async_computation | async-start | bytes 9437184 | tf_op jit(solution)/shard_map/psum | solution.py:65
  11.7 3.6 %copy-start = (f32[2,384,4,384]{3,2,1,0:T(4,128)}, f32[2,384,4,384]{3,2,1,0:T(4,128)S(1)}, u32[]{:S(2)}) copy-start(f32[2,384,4,384]{3,2,1,0:T(4,128)S(1)} %broadcast_multiply_fusion) | copy-start | bytes 14155780
  15.3 55.7 %collective-permute-start = (f32[1,384,4,384]{3,2,1,0:T(4,128)}, f32[1,384,4,384]{3,2,1,0:T(4,128)}, u32[]{:S(2)}, u32[]{:S(2)}) collective-permute-start(f32[1,384,4,384]{3,2,1,0:T(4,128)} %get-tuple-element.136), channel_id=1, source_target_pairs={{0,1},{1,2},{2,3},{4,5},{5,6},{6,7},{8,9},{9,10},{10,11},{12,13},{... | collective-permute-start | bytes 7077896 | tf_op jit(solution)/shard_map/ppermute | solution.py:15
  21.7 54.9 %collective-permute-start.1 = (f32[1,384,4,384]{3,2,1,0:T(4,128)}, f32[1,384,4,384]{3,2,1,0:T(4,128)}, u32[]{:S(2)}, u32[]{:S(2)}) collective-permute-start(f32[1,384,4,384]{3,2,1,0:T(4,128)} %get-tuple-element.137), channel_id=1, source_target_pairs={{1,0},{2,1},{3,2},{5,4},{6,5},{7,6},{9,8},{10,9},{11,10},{13,12},{... | collective-permute-start | bytes 7077896 | tf_op jit(solution)/shard_map/ppermute | solution.py:18
  22.9 63.4 %copy-start.1 = (f32[2,2,384,384]{3,2,1,0:T(8,128)S(1)}, f32[2,2,384,384]{3,2,1,0:T(8,128)}, u32[]{:S(2)}) copy-start(f32[2,2,384,384]{3,2,1,0:T(8,128)} %param.12) | copy-start | bytes 7077892
  23.0 63.4 %copy-start.3 = (f32[2,4,4]{2,1,0:T(4,128)S(1)}, f32[2,4,4]{2,1,0:T(4,128)}, u32[]{:S(2)}) copy-start(f32[2,4,4]{2,1,0:T(4,128)} %param.14) | copy-start | bytes 388
  23.0 63.4 %copy-start.5 = (s32[2]{0:T(128)S(1)}, s32[2]{0:T(128)}, u32[]{:S(2)}) copy-start(s32[2]{0:T(128)} %param.15) | copy-start | bytes 28
  167.0 85.8 %copy-start.4 = (f32[2]{0:T(128)S(1)}, f32[2]{0:T(128)}, u32[]{:S(2)}) copy-start(f32[2]{0:T(128)} %param.17) | copy-start | bytes 28
  167.1 105.9 %copy-start.2 = (bf16[2,384,4,384]{3,2,1,0:T(4,128)(2,1)S(1)}, bf16[2,384,4,384]{3,2,1,0:T(4,128)(2,1)}, u32[]{:S(2)}) copy-start(bf16[2,384,4,384]{3,2,1,0:T(4,128)(2,1)} %param.11) | copy-start | bytes 7077892
Sparse Core Ops, SparseCore 0:
  167.2 85.5 all-reduce.2
where the time goes:
time: 302 us
  waiting for transfers between devices  139 us (46%)
  matrix products  62.9 us (21%)
  other arithmetic  31.9 us (11%)
  blocking collectives  21.3 us (7%)
  local copies, waits for them, and re-layouts  18.6 us (6%)
  between operations  17.3 us (6%)
  starting transfers between devices  7.69 us (3%)
    psum x1, waiting for transfers between devices, body(): total = lax.psum(partial_sum, 'term')  85.7 us
    ppermute x1, waiting for transfers between devices, with_halo(): lax.ppermute(lax.slice_in_dim(block, block.shape[dim] - width, None, axis...  48 us
    dot_general x2, matrix products, single_term(): third = jnp.einsum('tape,teb->tapb', second, right, precision=TOP_LEVEL)  25.7 us
    dot_general x2, matrix products, single_term(): jnp.einsum('pr,tarb->tapb', operator, leading_item, precision=TOP_LEVEL)  21.6 us
    dot_general x2, matrix products, single_term(): jnp.einsum('qom,qmsg->qosg', left_side, source_sector, precision=TOP_LEVEL)  15.5 us
    psum x1, blocking collectives, body(): lax.psum((jnp.sum(state * image), jnp.sum(state * state)), 'sector')  12.3 us
    concatenate x1, other arithmetic, with_halo(): block = jnp.concatenate([low, block, high], axis=dim)  9.77 us
    reduce_sum x1, other arithmetic, body(): square = lax.psum(jnp.sum(moved * moved), 'sector')  9.23 us
  transfers between devices with their start and end apart: 3, of which 3 were waited for; matrix products, arithmetic and copies ran while one was open for 0% of the time, Pallas kernels for 0%

commit v1 on v0

v1 whole, which is shorter than its diff:
```python
import functools

import jax
import jax.numpy as jnp
from jax import lax
from jax.experimental import pallas as pl
from jax.experimental.pallas import tpu as pltpu
from jax.sharding import PartitionSpec as P

EPSILON = 1e-06
F32 = jnp.float32
BF16 = jnp.bfloat16
VMEM_BYTES = 56 * 1024 * 1024


def split(x):
    high = x.astype(BF16)
    return high, (x - high.astype(F32)).astype(BF16)


def dot(a, b):
    return jnp.dot(a, b, preferred_element_type=F32)


def row_tile(rows):
    return next(size for size in (64, 32, 16, 8) if rows % size == 0)


def split_into(src, high, low, first, rows, offset):
    tile = row_tile(rows)

    @pl.loop(0, rows // tile)
    def _(i):
        at = pl.ds(pl.multiple_of(first + i * tile, tile), tile)
        to = pl.ds(pl.multiple_of(offset + i * tile, tile), tile)
        a, b = split(src[at, :])
        high[to, :] = a
        low[to, :] = b


def pair_product(phys, operators, term, source, left, right, target, scratch):
    high, low = source
    stacked, product, mixed = scratch
    size = left.shape[0]
    part = right.shape[1]
    a, b = split(right[...])
    stacked[0:size, :] = a
    stacked[size : 2 * size, :] = b
    stacked[2 * size : 3 * size, :] = a

    @pl.loop(0, phys)
    def _(r):
        rows = pl.ds(pl.multiple_of(r * size, size), size)
        x, y = high[rows, :], low[rows, :]
        product[rows, :] = dot(jnp.concatenate([x, x, y], axis=1), stacked[...])

    tile = row_tile(size)

    @pl.loop(0, size // tile)
    def _(i):
        pieces = [
            product[pl.ds(pl.multiple_of(r * size + i * tile, tile), tile), :] for r in range(phys)
        ]
        for p in range(phys):
            total = operators[term, p * phys] * pieces[0]
            for r in range(1, phys):
                total = total + operators[term, p * phys + r] * pieces[r]
            x, y = split(total)
            cols = slice(p * part, (p + 1) * part)
            for place, value in enumerate((x, y, x)):
                at = pl.ds(pl.multiple_of(place * size + i * tile, tile), tile)
                mixed[at, cols] = value

    x, y = split(left[...])
    target[...] += dot(jnp.concatenate([x, x, y], axis=1), mixed[...])


def near_kernel(
    phys, charges, operators, own, left_a, left_b, right_a, right_b, out,
    raw, left, right, high, low, stacked, product, mixed, total, sems,
):
    sectors = own.shape[0]
    count = left_a.shape[0]
    loads = [
        pltpu.make_async_copy(own, raw, sems.at[0]),
        pltpu.make_async_copy(left_a, left.at[pl.ds(0, count)], sems.at[1]),
        pltpu.make_async_copy(right_a, right.at[pl.ds(0, count)], sems.at[2]),
        pltpu.make_async_copy(left_b, left.at[pl.ds(count, count)], sems.at[3]),
        pltpu.make_async_copy(right_b, right.at[pl.ds(count, count)], sems.at[4]),
    ]
    for load in loads:
        load.start()
    total[...] = jnp.zeros_like(total)
    loads[0].wait()
    for t in range(sectors):
        split_into(raw.at[t], high.at[t], low.at[t], 0, raw.shape[1], 0)
    for load in loads[1:]:
        load.wait()

    @pl.loop(0, 2 * count * sectors)
    def _(i):
        w = i // sectors
        t = i % sectors
        source = t - charges[w]

        @pl.when((source >= 0) & (source < sectors))
        def _():
            at = jnp.clip(source, 0, sectors - 1)
            pair_product(
                phys, operators, w, (high.at[at], low.at[at]), left.at[w, t], right.at[w, t],
                total.at[t], (stacked, product, mixed),
            )

    store = pltpu.make_async_copy(total, out, sems.at[0])
    store.start()
    store.wait()


def far_kernel(
    phys, chips, info, charges, operators, low_a, high_a, low_b, high_b, left_a, left_b, right_a,
    right_b, state, near, *refs,
):
    outs, products = refs[:chips], refs[chips]
    raw, left, right, high, low, stacked, product, mixed, total, here, sems, out_sems = refs[chips + 1 :]
    sectors = near.shape[0]
    count = left_a.shape[0]
    size = near.shape[1]
    half = size // 2
    rows = outs[0].shape[2]
    chip, core = info[0], info[1]
    loads = [
        pltpu.make_async_copy(low_a, raw.at[0, 0], sems.at[0]),
        pltpu.make_async_copy(high_a, raw.at[1, 0], sems.at[1]),
        pltpu.make_async_copy(low_b, raw.at[0, 1], sems.at[2]),
        pltpu.make_async_copy(high_b, raw.at[1, 1], sems.at[3]),
        pltpu.make_async_copy(left_a, left.at[pl.ds(0, count)], sems.at[4]),
        pltpu.make_async_copy(right_a, right.at[pl.ds(0, count)], sems.at[5]),
        pltpu.make_async_copy(left_b, left.at[pl.ds(count, count)], sems.at[6]),
        pltpu.make_async_copy(right_b, right.at[pl.ds(count, count)], sems.at[7]),
        pltpu.make_async_copy(near, total, sems.at[8]),
        pltpu.make_async_copy(state, here, sems.at[9]),
    ]
    for load in loads:
        load.start()
    for place in range(2):
        for side in range(2):
            loads[2 * place + side].wait()
            offset = (core if place == 0 else 1 - core) * half
            for r in range(phys):
                split_into(
                    raw.at[side, place], high.at[side], low.at[side], r * half, half, r * size + offset
                )
    for load in loads[4:]:
        load.wait()

    @pl.loop(0, 2 * count)
    def _(w):
        charge = charges[w]

        @pl.when(charge != 0)
        def _():
            side = jnp.where(charge > 0, 0, 1)
            t = jnp.where(charge > 0, 0, sectors - 1)
            pair_product(
                phys, operators, w, (high.at[side], low.at[side]), left.at[w, t], right.at[w, t],
                total.at[t], (stacked, product, mixed),
            )

    stores = []
    for j in range(chips):
        for c in range(2):
            first = pl.multiple_of((2 * (chip ^ j) + (core ^ c)) * rows, rows)
            stores.append(
                pltpu.make_async_copy(
                    total.at[:, pl.ds(first, rows), :], outs[j].at[:, c], out_sems.at[2 * j + c]
                )
            )
    for store in stores:
        store.start()
    tile = row_tile(size)
    products[...] = jnp.zeros_like(products)
    for t in range(sectors):

        @pl.loop(0, size // tile)
        def _(i):
            at = pl.ds(pl.multiple_of(i * tile, tile), tile)
            x = total[t, at, :] * here[t, at, :]
            products[...] += jnp.sum(x.reshape(tile // 8, 8, x.shape[1]), axis=0)

    for store in stores:
        store.wait()


def swap_cores(x, count):
    return lax.ppermute(x, "term", [(i, i ^ 1) for i in range(count)])


def sum_everywhere(x, axes):
    for axis in axes:
        count = lax.axis_size(axis)
        if count & (count - 1):
            x = lax.psum(x, axis)
            continue
        bit = 1
        while bit < count:
            x = x + lax.ppermute(x, axis, [(i, i ^ bit) for i in range(count)])
            bit *= 2
    return x


def body(
    psi, precond, left_environment_block, right_env, term_operators, term_charge, sector_sizes,
    sector_energy,
):
    sectors, size, phys, _ = psi.shape
    terms = term_charge.shape[0]
    count, planes = lax.axis_size("term"), lax.axis_size("sector")
    chips = count // 2
    rows = size // count
    half = size // 2
    lanes = phys * half
    numel = sectors * planes * size * phys * size
    me = lax.axis_index("term")
    chip, core = me // 2, me % 2

    positions = jnp.arange(size, dtype=jnp.int32)
    inside = positions[None, :] < sector_sizes[:, None]

    def masked(x, row_first, row_count, col_first, col_count):
        x = lax.dynamic_slice(x, (0, row_first, 0, col_first), (sectors, row_count, phys, col_count))
        a = lax.dynamic_slice(inside, (0, row_first), (sectors, row_count))
        b = lax.dynamic_slice(inside, (0, col_first), (sectors, col_count))
        return jnp.where(a[:, :, None, None] & b[:, None, None, :], x, 0)

    sent = masked(psi, core * half, half, 0, size)
    forward = [(i, i + 1) for i in range(planes - 1)]
    backward = [(b, a) for a, b in forward]

    def flat(x):
        return jnp.transpose(x, (1, 0, 2)).reshape(phys * half, size)

    low_a = lax.ppermute(flat(sent[sectors - 1]), "sector", forward)
    high_a = lax.ppermute(flat(sent[0]), "sector", backward)
    low_b = swap_cores(low_a, count)
    high_b = swap_cores(high_a, count)

    left_a = left_environment_block
    left_b = swap_cores(left_a, count)
    right_a = lax.dynamic_slice_in_dim(right_env, core * half, half, 3)
    right_b = swap_cores(lax.dynamic_slice_in_dim(right_env, (1 - core) * half, half, 3), count)
    small = jnp.concatenate(
        [term_operators.reshape(terms, phys * phys), term_charge.astype(F32)[:, None]], axis=1
    )
    small = jnp.concatenate([small, swap_cores(small, count)], axis=0)
    operators = small[:, : phys * phys]
    charges = small[:, phys * phys].astype(jnp.int32)

    own = jnp.transpose(masked(psi, 0, size, 0, size), (0, 2, 1, 3)).reshape(sectors, phys * size, size)
    state_half = masked(psi, 0, size, core * half, half).reshape(sectors, size, lanes)

    any_spec = pl.BlockSpec(memory_space=pl.ANY)
    smem = pl.BlockSpec(memory_space=pltpu.SMEM)
    pair_scratch = [
        pltpu.VMEM((3 * size, half), BF16),
        pltpu.VMEM((phys * size, half), F32),
        pltpu.VMEM((3 * size, lanes), BF16),
        pltpu.VMEM((sectors, size, lanes), F32),
    ]
    env_scratch = [
        pltpu.VMEM((2 * terms, sectors, size, size), F32),
        pltpu.VMEM((2 * terms, sectors, size, half), F32),
    ]
    params = pltpu.CompilerParams(vmem_limit_bytes=VMEM_BYTES)
    near = pl.pallas_call(
        functools.partial(near_kernel, phys),
        out_shape=jax.ShapeDtypeStruct((sectors, size, lanes), F32),
        in_specs=[smem] * 2 + [any_spec] * 5,
        out_specs=any_spec,
        scratch_shapes=[
            pltpu.VMEM((sectors, phys * size, size), F32),
            *env_scratch,
            pltpu.VMEM((sectors, phys * size, size), BF16),
            pltpu.VMEM((sectors, phys * size, size), BF16),
            *pair_scratch,
            pltpu.SemaphoreType.DMA((5,)),
        ],
        compiler_params=params,
        cost_estimate=pl.CostEstimate(
            flops=12 * terms * sectors * size * size * lanes, bytes_accessed=16 << 20, transcendentals=0
        ),
        name="near_terms",
    )(charges, operators, own, left_a, left_b, right_a, right_b)

    info = jnp.stack([chip, core]).astype(jnp.int32)
    block = jax.ShapeDtypeStruct((sectors, 2, rows, lanes), F32)
    results = pl.pallas_call(
        functools.partial(far_kernel, phys, chips),
        out_shape=[block] * chips + [jax.ShapeDtypeStruct((8, lanes), F32)],
        in_specs=[smem] * 3 + [any_spec] * 10,
        out_specs=[any_spec] * chips + [pl.BlockSpec(memory_space=pltpu.VMEM)],
        scratch_shapes=[
            pltpu.VMEM((2, 2, phys * half, size), F32),
            *env_scratch,
            pltpu.VMEM((2, phys * size, size), BF16),
            pltpu.VMEM((2, phys * size, size), BF16),
            *pair_scratch,
            pltpu.VMEM((sectors, size, lanes), F32),
            pltpu.SemaphoreType.DMA((10,)),
            pltpu.SemaphoreType.DMA((2 * chips,)),
        ],
        compiler_params=params,
        cost_estimate=pl.CostEstimate(
            flops=6 * terms * sectors * size * size * lanes, bytes_accessed=16 << 20, transcendentals=0
        ),
        name="far_terms",
    )(
        info, charges, operators, low_a, high_a, low_b, high_b, left_a, left_b, right_a, right_b,
        state_half, near,
    )
    parts, overlap = results[:chips], results[chips]

    def share(x):
        x = x.reshape(sectors, 2, rows, lanes)
        return jnp.where(core == 0, x, x[:, ::-1])

    first = chip * 2 * rows
    state = share(masked(psi, first, 2 * rows, core * half, half))
    scale = share(masked(1.0 / precond.astype(F32), first, 2 * rows, core * half, half))
    squares = jnp.sum(state * state, axis=(1, 2, 3))
    sums = jnp.stack(
        [
            jnp.sum(overlap) + jnp.sum(sector_energy * squares),
            jnp.sum(squares),
        ]
    )
    sums = sum_everywhere(sums, ("term", "sector"))
    energy = sums[0] / sums[1]

    total = parts[0]
    for j in range(1, chips):
        total = total + lax.ppermute(parts[j], "term", [(i, i ^ (2 * j)) for i in range(count)])
    shift = sector_energy - energy
    moved = state - (total + shift[:, None, None, None] * state) * scale
    square = sum_everywhere(jnp.sum(moved * moved), ("term", "sector"))

    mine = moved[:, 0].reshape(sectors, rows, phys, half)
    other = swap_cores(moved[:, 1], count).reshape(sectors, rows, phys, half)
    both = jnp.where(
        core == 0, jnp.concatenate([mine, other], axis=3), jnp.concatenate([other, mine], axis=3)
    )
    return both * lax.rsqrt(square / numel + EPSILON), jnp.stack([energy])


def solution(mesh):
    in_specs = (
        P("sector", None, None, None),
        P("sector", None, None, None),
        P("term", "sector", None, None),
        P("term", "sector", None, None),
        P("term", None, None),
        P("term"),
        P("sector"),
        P("sector"),
    )
    out_specs = (P("sector", "term", None, None), P())
    return jax.shard_map(body, mesh=mesh, in_specs=in_specs, out_specs=out_specs, check_vma=False)
```

time: 302 us -> 181 us (0.60)
  waiting for transfers between devices: 139 us -> 48.9 us
  matrix products: 62.9 us -> 0 us
  Pallas kernels: 0 us -> 45.2 us
  blocking collectives: 21.3 us -> 0 us
  starting transfers between devices: 7.69 us -> 27.6 us
  between operations: 17.3 us -> 7.92 us
  local copies, waits for them, and re-layouts: 18.6 us -> 26.3 us
  other arithmetic: 31.9 us -> 24.6 us
    psum x1 -> x0, waiting for transfers between devices: 85.7 us -> none  [body(): total = lax.psum(partial_sum, 'term')]
    dot_general x6 -> x0, matrix products: 62.9 us -> none  [the longest x2 25.7 us: single_term(): third = jnp.einsum('tape,teb->tapb', second, right, precision=TOP_LEVEL)]
    pallas_call x0 -> x2, Pallas kernels: none -> 45.2 us  [the longest x1 29 us: body(): pl.pallas_call(functools.partial(near_kernel, phys), out_shape=jax.ShapeD...]
    psum x2 -> x0, blocking collectives: 21.3 us -> none  [the longest x1 12.3 us: body(): lax.psum((jnp.sum(state * image), jnp.sum(state * state)), 'sector')]
    ppermute x2 -> x21, starting transfers between devices: 7.65 us -> 27.6 us  [the longest x10 16.1 us: sum_everywhere(): x = x + lax.ppermute(x, axis, [(i, i ^ bit) for i in range(count)])]
    reduce_sum x2 -> x4, other arithmetic: 15.7 us -> 4.61 us  [the longest x1 1.93 us: body(): square = sum_everywhere(jnp.sum(moved * moved), ('term', 'sector'))]
    concatenate x1 -> x2, other arithmetic: 9.77 us -> 0.15 us  [the longest x1 0.08 us: body(): jnp.concatenate([term_operators.reshape(terms, phys * phys), term_charge....]
    while x1 -> x0, local copies, waits for them, and re-layouts: 7.54 us -> none  [term_partials(): lax.scan(single_term, jnp.zeros_like(state), (left_environment_block, rig...]
  transfers between devices with their start and end apart: 3 -> 21, of which waited for: 3 -> 12; matrix products, arithmetic and copies ran while one was open for 0% -> 23% of each run, Pallas kernels for 0% -> 16%
where the time goes in v1:
time: 181 us
  waiting for transfers between devices  48.9 us (27%)
  Pallas kernels  45.2 us (25%)
  starting transfers between devices  27.6 us (15%)
  local copies, waits for them, and re-layouts  26.3 us (15%)
  other arithmetic  24.6 us (14%)
  between operations  7.92 us (4%)
    ppermute x10, waiting for transfers between devices, sum_everywhere(): x = x + lax.ppermute(x, axis, [(i, i ^ bit) for i in range(count)])  33.8 us
    pallas_call x1, Pallas kernels, body(): pl.pallas_call(functools.partial(near_kernel, phys), out_shape=jax.ShapeD...  29 us
    pallas_call x1, Pallas kernels, body(): pl.pallas_call(functools.partial(far_kernel, phys, chips), out_shape=[blo...  16.3 us
    ppermute x10, starting transfers between devices, sum_everywhere(): x = x + lax.ppermute(x, axis, [(i, i ^ bit) for i in range(count)])  16.1 us
    ppermute x1, waiting for transfers between devices, body(): low_a = lax.ppermute(flat(sent[sectors - 1]), 'sector', forward)  8.78 us
    select_n x3, other arithmetic, masked(): return jnp.where(a[:, :, None, None] & b[:, None, None, :], x, 0)  7.52 us
    ppermute x1, waiting for transfers between devices, body(): high_a = lax.ppermute(flat(sent[0]), 'sector', backward)  6.25 us
    transpose x1, other arithmetic, body(): jnp.transpose(masked(psi, 0, size, 0, size), (0, 2, 1, 3))  6.15 us
  transfers between devices with their start and end apart: 21, of which 12 were waited for; matrix products, arithmetic and copies ran while one was open for 23% of the time, Pallas kernels for 16%

profile of v1, /device:TPU:0, one launch (start us, length us, event | category | flops | bytes accessed | tf_op | source)
XLA Modules:
  0.0 180.5 jit_solution(13785600741032733266)
XLA Ops:
  0.7 4.2 %constant_dynamic-slice_fusion.1 = (f32[2,2,384,192]{3,2,1,0:T(8,128)S(1)}, f32[2,2,384,192]{3,2,1,0:T(8,128)}) fusion(f32[2,2,384,384]{3,2,1,0:T(8,128)} %param.11, s32[]{:T(128)S(6)} %select_n.79, s32[]{:T(128)S(6)} %select_n.75), kind=kLoop, calls=%fused_computation.25 | loop fusion | bytes 4718600 | tf_op jit(solution)/shard_map/dynamic_slice | solution.py:250
  4.9 1.5 copy.29
  6.4 0.4 collective-permute-start.6
  6.8 0.1 copy.20
  7.1 0.4 collective-permute-start.5
  7.7 0.1 broadcast_and_fusion.2
  7.9 2.6 %dynamic-slice_select_fusion = f32[2,192,4,384]{3,2,1,0:T(4,128)S(1)} fusion(f32[2,384,4,384]{3,2,1,0:T(4,128)} %param.8, s32[]{:T(128)S(6)} %select_n.75, pred[2,192,384]{2,1,0:T(8,128)(4,1)S(1)} %broadcast_and_fusion.2), kind=kLoop, calls=%fused_computation.1 | loop fusion | flops 589824 | bytes 4866052 | tf_op jit(solution)/shard_map/jit(_where)/select_n | solution.py:233
  10.5 0.4 slice_bitcast_fusion
  11.0 1.1 copy.21
  12.1 5.6 %collective-permute-start.1 = (f32[768,384]{1,0:T(8,128)}, f32[768,384]{1,0:T(8,128)}, u32[]{:S(2)}, u32[]{:S(2)}) collective-permute-start(f32[768,384]{1,0:T(8,128)} %bitcast.5), channel_id=1, source_target_pairs={{0,1},{1,2},{2,3},{4,5},{5,6},{6,7},{8,9},{9,10},{10,11},{12,13},{... | collective-permute-start | bytes 3538952 | tf_op jit(solution)/shard_map/ppermute | solution.py:242
  17.7 1.1 copy.22
  18.8 1.3 collective-permute-start.2
  20.1 0.2 broadcast_and_fusion
  20.3 0.8 broadcast_and_fusion.1
  21.1 1.7 constant_dynamic-slice_fusion
  22.8 3.0 %copy.30 = f32[2,384,4,192]{1,3,2,0:T(8,128)} copy(f32[2,384,4,192]{3,2,1,0:T(4,128)S(1)} %constant_dynamic-slice_fusion) | data formatting | bytes 4718592
  25.8 1.9 %broadcast_select_fusion = f32[2,384,4,192]{1,3,2,0:T(8,128)S(1)} fusion(f32[2,384,4,192]{1,3,2,0:T(8,128)} %copy.30, pred[2,384,192]{1,2,0:T(8,128)(4,1)} %broadcast_and_fusion.1), kind=kLoop, calls=%fused_computation.4 | loop fusion | flops 589824 | bytes 4866048 | tf_op jit(solution)/shard_map/jit(_where)/select_n | solution.py:233
  27.7 6.1 %select_bitcast_fusion = f32[2,4,384,384]{3,1,2,0:T(4,128)} fusion(f32[2,384,4,384]{3,2,1,0:T(4,128)} %param.8, pred[2,384,384]{2,1,0:T(8,128)(4,1)S(1)} %broadcast_and_fusion), kind=kLoop, calls=%fused_computation | loop fusion | flops 1179648 | bytes 9732096 | tf_op jit(solution)/shard_map/transpose | solution.py:258
  33.9 0.1 broadcast_and_fusion.3
  34.0 8.8 %collective-permute-done.1.low_a = f32[768,384]{1,0:T(8,128)} collective-permute-done((f32[768,384]{1,0:T(8,128)}, f32[768,384]{1,0:T(8,128)}, u32[]{:S(2)}, u32[]{:S(2)}) %collective-permute-start.1) | collective-permute-done | bytes 1179680 | tf_op jit(solution)/shard_map/ppermute | solution.py:242
  42.8 6.3 %collective-permute-done.2.high_a = f32[768,384]{1,0:T(8,128)} collective-permute-done((f32[768,384]{1,0:T(8,128)}, f32[768,384]{1,0:T(8,128)}, u32[]{:S(2)}, u32[]{:S(2)}) %collective-permute-start.2) | collective-permute-done | bytes 1179680 | tf_op jit(solution)/shard_map/ppermute | solution.py:243
  49.0 3.0 %dynamic-slice_select_fusion.1 = (f32[2,96,4,192]{3,2,1,0:T(4,128)}, f32[2,96,4,192]{3,2,1,0:T(4,128)S(1)}) fusion(f32[2,384,4,384]{3,2,1,0:T(4,128)} %param.8, s32[]{:T(128)S(6)} %select_n.74, s32[]{:T(128)S(6)} %select_n.75, pred[2,96,192]{2,1,0:T(8,128)(4,1)S(1)} %broadcast_and_fusion.3, bf16[2,384,4,384]{3,2,1,0:T(4,128)(2,1)} %param.9), kind=kLoop, calls=%fused_computation.8 | loop fusion | flops 589824 | bytes 2101256 | tf_op jit(solution)/shard_map/jit(_where)/select_n | solution.py:233
  52.0 4.8 %copy.25 = f32[2,4,384,384]{3,2,1,0:T(8,128)} copy(f32[2,4,384,384]{3,1,2,0:T(4,128)} %select_bitcast_fusion) | data formatting | bytes 9437184 | tf_op jit(solution)/shard_map/transpose | solution.py:258
  56.8 2.0 %copy.28.state = f32[2,384,768]{2,1,0:T(8,128)} copy(f32[2,384,768]{1,2,0:T(8,128)S(1)} %bitcast.28) | data formatting | bytes 4718592 | tf_op jit(solution)/shard_map/reshape | solution.py:259
  58.8 1.6 reshape.94
  60.4 0.6 pad_add_fusion.info
  61.1 0.8 multiply_reduce_fusion.2
  61.9 0.6 multiply_reduce_fusion.3
  62.4 0.5 reshape.100
  63.0 0.8 convert_reduce_fusion.charges
  63.8 2.9 %copy.27.right_b = f32[2,2,384,192]{3,2,1,0:T(8,128)} copy(f32[2,2,384,192]{2,3,1,0:T(8,128)} %collective-permute-done.6) | data formatting | bytes 2359296 | tf_op jit(solution)/shard_map/ppermute | solution.py:195
  66.7 29.0 %near_terms.1.near = f32[2,384,768]{2,1,0:T(8,128)} custom-call(s32[4]{0:T(128)} %convert_reduce_fusion.charges, f32[4,16]{1,0:T(4,128)} %bitcast.30, f32[2,1536,384]{2,1,0:T(8,128)} %bitcast.29, f32[2,2,384,384]{3,2,1,0:T(8,128)} %left_a.3, f32[2,2,384,384]{3,2,1,0:T(8,128)} %collective-permute-done.5.left_b, f32[2,2,384,192]{3,2,1,0:T(8,128)} %get-tuple-element.17.right_a, ...), custom_call_target="tpu_custom_call" | custom-call | flops 5435817984 | bytes 16777216 | tf_op jit(solution)/shard_map/near_terms/pallas_call | solution.py:274
  95.7 16.3 %far_terms.1 = (f32[2,2,48,768]{3,2,1,0:T(8,128)}, f32[2,2,48,768]{3,2,1,0:T(8,128)}, f32[2,2,48,768]{3,2,1,0:T(8,128)}, f32[2,2,48,768]{3,2,1,0:T(8,128)}, f32[8,768]{1,0:T(8,128)}) custom-call(s32[2]{0:T(128)} %pad_add_fusion.info, s32[4]{0:T(128)} %convert_reduce_fusion.charges, f32[4,16]{1,0:T(4,128)} %bitcast.31, ...), custom_call_target="tpu_custom_call" | custom-call | flops 2717908992 | bytes 16777216 | tf_op jit(solution)/shard_map/far_terms/pallas_call | solution.py:296
  112.0 1.5 collective-permute-start.7
  113.5 1.5 collective-permute-start.8
  115.0 0.5 collective-permute-start.9
  115.5 1.3 reduce_sum.45
  117.9 0.7 pad_maximum_fusion.2
  118.7 1.1 collective-permute-done.10
  119.8 0.7 fusion.6
  120.5 1.5 collective-permute-start.11
  122.0 18.5 %collective-permute-done.11 = f32[2]{0:T(128)S(1)} collective-permute-done((f32[2]{0:T(128)S(1)}, f32[2]{0:T(128)S(1)}, u32[]{:S(2)}, u32[]{:S(2)}) %collective-permute-start.11) | collective-permute-done | bytes 40 | tf_op jit(solution)/shard_map/ppermute | solution.py:206
  140.5 0.7 fusion.7
  141.2 1.5 collective-permute-start.12
  142.7 2.0 %collective-permute-done.12 = f32[2]{0:T(128)S(1)} collective-permute-done((f32[2]{0:T(128)S(1)}, f32[2]{0:T(128)S(1)}, u32[]{:S(2)}, u32[]{:S(2)}) %collective-permute-start.12) | collective-permute-done | bytes 40 | tf_op jit(solution)/shard_map/ppermute | solution.py:206
  144.7 0.5 collective-permute-start.13
  145.3 3.0 %collective-permute-done.13 = f32[2]{0:T(128)S(1)} collective-permute-done((f32[2]{0:T(128)S(1)}, f32[2]{0:T(128)S(1)}, u32[]{:S(2)}, u32[]{:S(2)}) %collective-permute-start.13) | collective-permute-done | bytes 40 | tf_op jit(solution)/shard_map/ppermute | solution.py:206
  148.3 1.5 collective-permute-start.14
  149.8 2.9 %collective-permute-done.14 = f32[2]{0:T(128)S(1)} collective-permute-done((f32[2]{0:T(128)S(1)}, f32[2]{0:T(128)S(1)}, u32[]{:S(2)}, u32[]{:S(2)}) %collective-permute-start.14) | collective-permute-done | bytes 40 | tf_op jit(solution)/shard_map/ppermute | solution.py:206
  152.7 0.6 fusion.5
  154.6 1.9 %multiply_reduce_fusion = (f32[]{:T(128)}, f32[2,2,48,768]{3,2,1,0:T(8,128)S(1)}) fusion(f32[2,2,48,768]{3,2,1,0:T(8,128)S(1)} %reshape.100, f32[2]{0:T(128)S(1)} %broadcast_subtract_fusion, f32[2,2,48,768]{3,2,1,0:T(8,128)S(1)} %collective-permute-done.9, f32[2,2,48,768]{3,2,1,0:T(8,128)S(1)} %collective-permute-done.8, ...), kind=kLoop, calls=%fused_computation.13 | loop fusion | flops 1622015 | bytes 4128781 | tf_op jit(solution)/shard_map/reduce_sum | solution.py:344
  156.7 0.5 collective-permute-start.16
  157.2 0.3 reshape_squeeze.3
  157.5 1.1 collective-permute-done.16
  159.8 2.9 %collective-permute-start.17 = (f32[]{:T(128)}, f32[]{:T(128)}, u32[]{:S(2)}, u32[]{:S(2)}) collective-permute-start(f32[]{:T(128)} %add.87), channel_id=1, source_target_pairs={{0,8},{4,12},{8,0},{12,4},{16,24},{20,28},{24,16},{28,20},{1,9},{5... | collective-permute-start | bytes 20 | tf_op jit(solution)/shard_map/ppermute | solution.py:206
  162.6 0.8 collective-permute-done.17
  164.0 2.9 %collective-permute-start.18 = (f32[]{:T(128)}, f32[]{:T(128)}, u32[]{:S(2)}, u32[]{:S(2)}) collective-permute-start(f32[]{:T(128)} %add.88), channel_id=1, source_target_pairs={{0,16},{4,20},{8,24},{12,28},{16,0},{20,4},{24,8},{28,12},{1,17},{... | collective-permute-start | bytes 20 | tf_op jit(solution)/shard_map/ppermute | solution.py:206
  166.9 0.8 collective-permute-done.18
  168.3 1.9 %collective-permute-start.19 = (f32[]{:T(128)}, f32[]{:T(128)}, u32[]{:S(2)}, u32[]{:S(2)}) collective-permute-start(f32[]{:T(128)} %add.89), channel_id=1, source_target_pairs={{0,1},{1,0},{2,3},{3,2},{4,5},{5,4},{6,7},{7,6},{8,9},{9,8},{10,11... | collective-permute-start | bytes 20 | tf_op jit(solution)/shard_map/ppermute | solution.py:206
  170.2 1.8 %collective-permute-done.19 = f32[]{:T(128)} collective-permute-done((f32[]{:T(128)}, f32[]{:T(128)}, u32[]{:S(2)}, u32[]{:S(2)}) %collective-permute-start.19) | collective-permute-done | bytes 36 | tf_op jit(solution)/shard_map/ppermute | solution.py:206
  172.6 2.9 %collective-permute-start.20 = (f32[]{:T(128)}, f32[]{:T(128)}, u32[]{:S(2)}, u32[]{:S(2)}) collective-permute-start(f32[]{:T(128)} %add.90), channel_id=1, source_target_pairs={{0,2},{1,3},{2,0},{3,1},{4,6},{5,7},{6,4},{7,5},{8,10},{9,11},{10,... | collective-permute-start | bytes 20 | tf_op jit(solution)/shard_map/ppermute | solution.py:206
  175.5 1.7 collective-permute-done.20
  177.8 0.3 reshape.101
  178.1 1.3 fusion.2
  (41 shorter events, 0.7 us)
Async XLA Ops:
  4.9 1.9 %copy-start.3 = (s32[2]{0:T(128)S(1)}, s32[2]{0:T(128)}, u32[]{:S(2)}) copy-start(s32[2]{0:T(128)} %param.13) | copy-start | bytes 28
  4.9 2.0 %copy-start.1 = (f32[2,4,4]{2,1,0:T(4,128)S(1)}, f32[2,4,4]{2,1,0:T(4,128)}, u32[]{:S(2)}) copy-start(f32[2,4,4]{2,1,0:T(4,128)} %param.12) | copy-start | bytes 388
  4.9 2.7 %copy-start.2 = (s32[2]{0:T(128)S(1)}, s32[2]{0:T(128)}, u32[]{:S(2)}) copy-start(s32[2]{0:T(128)} %param.14) | copy-start | bytes 28
  6.4 57.4 %collective-permute-start.6 = (f32[2,2,384,192]{2,3,1,0:T(8,128)}, f32[2,2,384,192]{2,3,1,0:T(8,128)}, u32[]{:S(2)}, u32[]{:S(2)}) collective-permute-start(f32[2,2,384,192]{2,3,1,0:T(8,128)} %copy.29), channel_id=1, source_target_pairs={{0,4},{4,0},{8,12},{12,8},{16,20},{20,16},{24,28},{28,24},{1,5},{5... | collective-permute-start | bytes 3538952 | tf_op jit(solution)/shard_map/ppermute | solution.py:195
  7.1 55.9 %collective-permute-start = (f32[2,17]{1,0:T(2,128)S(1)}, f32[2,17]{1,0:T(2,128)S(1)}, u32[]{:S(2)}, u32[]{:S(2)}) collective-permute-start(f32[2,17]{1,0:T(2,128)S(1)} %pad_maximum_fusion.1), channel_id=1, source_target_pairs={{0,4},{4,0},{8,12},{12,8},{16,20},{20,16},{24,28},{28,24},{1,5},{5... | collective-permute-start | bytes 416 | tf_op jit(solution)/shard_map/ppermute | solution.py:195
  7.1 59.6 %collective-permute-start.5 = (f32[2,2,384,384]{3,2,1,0:T(8,128)}, f32[2,2,384,384]{3,2,1,0:T(8,128)}, u32[]{:S(2)}, u32[]{:S(2)}) collective-permute-start(f32[2,2,384,384]{3,2,1,0:T(8,128)} %left_a.3), channel_id=1, source_target_pairs={{0,4},{4,0},{8,12},{12,8},{16,20},{20,16},{24,28},{28,24},{1,5},{5... | collective-permute-start | bytes 7077896 | tf_op jit(solution)/shard_map/ppermute | solution.py:195
  7.9 13.2 %slice-start = ((s8[4718592]{0:T(1024)(128)(4,1)}), s8[4194304]{0:T(1024)(128)(4,1)S(1)}, s32[]{:S(2)}) async-start(s8[4718592]{0:T(1024)(128)(4,1)} %bitcast.26), calls=%async_computation | async-start | bytes 8388608
  10.5 10.6 %slice-start.1 = ((s8[4718592]{0:T(1024)(128)(4,1)}), s8[524288]{0:T(1024)(128)(4,1)S(1)}, s32[]{:S(2)}) async-start(s8[4718592]{0:T(1024)(128)(4,1)} %bitcast.26), calls=%async_computation.1 | async-start | bytes 1048576
  12.1 30.7 %collective-permute-start.1 = (f32[768,384]{1,0:T(8,128)}, f32[768,384]{1,0:T(8,128)}, u32[]{:S(2)}, u32[]{:S(2)}) collective-permute-start(f32[768,384]{1,0:T(8,128)} %bitcast.5), channel_id=1, source_target_pairs={{0,1},{1,2},{2,3},{4,5},{5,6},{6,7},{8,9},{9,10},{10,11},{12,13},{... | collective-permute-start | bytes 3538952 | tf_op jit(solution)/shard_map/ppermute | solution.py:242
  18.8 30.2 %collective-permute-start.2 = (f32[768,384]{1,0:T(8,128)}, f32[768,384]{1,0:T(8,128)}, u32[]{:S(2)}, u32[]{:S(2)}) collective-permute-start(f32[768,384]{1,0:T(8,128)} %bitcast.8), channel_id=1, source_target_pairs={{1,0},{2,1},{3,2},{5,4},{6,5},{7,6},{9,8},{10,9},{11,10},{13,12},{... | collective-permute-start | bytes 3538952 | tf_op jit(solution)/shard_map/ppermute | solution.py:243
  42.8 52.9 %collective-permute-start.3 = (f32[768,384]{1,0:T(8,128)}, f32[768,384]{1,0:T(8,128)}, u32[]{:S(2)}, u32[]{:S(2)}) collective-permute-start(f32[768,384]{1,0:T(8,128)} %collective-permute-done.1.low_a), channel_id=1, source_target_pairs={{0,4},{4,0},{8,12},{12,8},{16,20},{20,16},{24,28},{28,24},{1,5},{5... | collective-permute-start | bytes 3538952 | tf_op jit(solution)/shard_map/ppermute | solution.py:195
  49.0 46.7 %collective-permute-start.4 = (f32[768,384]{1,0:T(8,128)}, f32[768,384]{1,0:T(8,128)}, u32[]{:S(2)}, u32[]{:S(2)}) collective-permute-start(f32[768,384]{1,0:T(8,128)} %collective-permute-done.2.high_a), channel_id=1, source_target_pairs={{0,4},{4,0},{8,12},{12,8},{16,20},{20,16},{24,28},{28,24},{1,5},{5... | collective-permute-start | bytes 3538952 | tf_op jit(solution)/shard_map/ppermute | solution.py:195
  56.8 5.1 %copy-start.4 = (f32[2]{0:T(128)S(1)}, f32[2]{0:T(128)}, u32[]{:S(2)}) copy-start(f32[2]{0:T(128)} %param.15) | copy-start | bytes 28
  63.0 3.7 %copy-start = (f32[4,17]{1,0:T(4,128)}, f32[4,17]{1,0:T(4,128)S(1)}, u32[]{:S(2)}) copy-start(f32[4,17]{1,0:T(4,128)S(1)} %pad_maximum_fusion) | copy-start | bytes 820
  112.0 42.6 %collective-permute-start.7 = (f32[2,2,48,768]{3,2,1,0:T(8,128)}, f32[2,2,48,768]{3,2,1,0:T(8,128)S(1)}, u32[]{:S(2)}, u32[]{:S(2)}) collective-permute-start(f32[2,2,48,768]{3,2,1,0:T(8,128)} %get-tuple-element.8), channel_id=1, source_target_pairs={{0,8},{4,12},{8,0},{12,4},{16,24},{20,28},{24,16},{28,20},{1,9},{5... | collective-permute-start | bytes 1769480 | tf_op jit(solution)/shard_map/ppermute | solution.py:341
  113.5 41.1 %collective-permute-start.8 = (f32[2,2,48,768]{3,2,1,0:T(8,128)}, f32[2,2,48,768]{3,2,1,0:T(8,128)S(1)}, u32[]{:S(2)}, u32[]{:S(2)}) collective-permute-start(f32[2,2,48,768]{3,2,1,0:T(8,128)} %get-tuple-element.9), channel_id=1, source_target_pairs={{0,16},{4,20},{8,24},{12,28},{16,0},{20,4},{24,8},{28,12},{1,17},{... | collective-permute-start | bytes 1769480 | tf_op jit(solution)/shard_map/ppermute | solution.py:341
  115.0 39.6 %collective-permute-start.9 = (f32[2,2,48,768]{3,2,1,0:T(8,128)}, f32[2,2,48,768]{3,2,1,0:T(8,128)S(1)}, u32[]{:S(2)}, u32[]{:S(2)}) collective-permute-start(f32[2,2,48,768]{3,2,1,0:T(8,128)} %get-tuple-element.10), channel_id=1, source_target_pairs={{0,24},{4,28},{8,16},{12,20},{16,8},{20,12},{24,0},{28,4},{1,25},{... | collective-permute-start | bytes 1769480 | tf_op jit(solution)/shard_map/ppermute | solution.py:341
  118.7 1.1 collective-permute-start.10
  120.5 20.0 %collective-permute-start.11 = (f32[2]{0:T(128)S(1)}, f32[2]{0:T(128)S(1)}, u32[]{:S(2)}, u32[]{:S(2)}) collective-permute-start(f32[2]{0:T(128)S(1)} %fusion.6), channel_id=1, source_target_pairs={{0,8},{4,12},{8,0},{12,4},{16,24},{20,28},{24,16},{28,20},{1,9},{5... | collective-permute-start | bytes 32 | tf_op jit(solution)/shard_map/ppermute | solution.py:206
  141.2 3.5 %collective-permute-start.12 = (f32[2]{0:T(128)S(1)}, f32[2]{0:T(128)S(1)}, u32[]{:S(2)}, u32[]{:S(2)}) collective-permute-start(f32[2]{0:T(128)S(1)} %fusion.7), channel_id=1, source_target_pairs={{0,16},{4,20},{8,24},{12,28},{16,0},{20,4},{24,8},{28,12},{1,17},{... | collective-permute-start | bytes 32 | tf_op jit(solution)/shard_map/ppermute | solution.py:206
  144.7 3.5 %collective-permute-start.13 = (f32[2]{0:T(128)S(1)}, f32[2]{0:T(128)S(1)}, u32[]{:S(2)}, u32[]{:S(2)}) collective-permute-start(f32[2]{0:T(128)S(1)} %add.83), channel_id=1, source_target_pairs={{0,1},{1,0},{2,3},{3,2},{4,5},{5,4},{6,7},{7,6},{8,9},{9,8},{10,11... | collective-permute-start | bytes 32 | tf_op jit(solution)/shard_map/ppermute | solution.py:206
  148.3 4.4 %collective-permute-start.14 = (f32[2]{0:T(128)S(1)}, f32[2]{0:T(128)S(1)}, u32[]{:S(2)}, u32[]{:S(2)}) collective-permute-start(f32[2]{0:T(128)S(1)} %add.84), channel_id=1, source_target_pairs={{0,2},{1,3},{2,0},{3,1},{4,6},{5,7},{6,4},{7,5},{8,10},{9,11},{10,... | collective-permute-start | bytes 32 | tf_op jit(solution)/shard_map/ppermute | solution.py:206
  156.6 21.2 %collective-permute-start.15 = (f32[2,48,768]{2,1,0:T(8,128)S(1)}, f32[2,48,768]{2,1,0:T(8,128)S(1)}, u32[]{:S(2)}, u32[]{:S(2)}) collective-permute-start(f32[2,48,768]{2,1,0:T(8,128)S(1)} %get-tuple-element.21), channel_id=1, source_target_pairs={{0,4},{4,0},{8,12},{12,8},{16,20},{20,16},{24,28},{28,24},{1,5},{5... | collective-permute-start | bytes 884744 | tf_op jit(solution)/shard_map/ppermute | solution.py:195
  156.7 1.9 %collective-permute-start.16 = (f32[]{:T(128)}, f32[]{:T(128)}, u32[]{:S(2)}, u32[]{:S(2)}) collective-permute-start(f32[]{:T(128)} %get-tuple-element.14), channel_id=1, source_target_pairs={{0,4},{4,0},{8,12},{12,8},{16,20},{20,16},{24,28},{28,24},{1,5},{5... | collective-permute-start | bytes 20 | tf_op jit(solution)/shard_map/ppermute | solution.py:206
  159.8 3.7 %collective-permute-start.17 = (f32[]{:T(128)}, f32[]{:T(128)}, u32[]{:S(2)}, u32[]{:S(2)}) collective-permute-start(f32[]{:T(128)} %add.87), channel_id=1, source_target_pairs={{0,8},{4,12},{8,0},{12,4},{16,24},{20,28},{24,16},{28,20},{1,9},{5... | collective-permute-start | bytes 20 | tf_op jit(solution)/shard_map/ppermute | solution.py:206
  164.0 3.7 %collective-permute-start.18 = (f32[]{:T(128)}, f32[]{:T(128)}, u32[]{:S(2)}, u32[]{:S(2)}) collective-permute-start(f32[]{:T(128)} %add.88), channel_id=1, source_target_pairs={{0,16},{4,20},{8,24},{12,28},{16,0},{20,4},{24,8},{28,12},{1,17},{... | collective-permute-start | bytes 20 | tf_op jit(solution)/shard_map/ppermute | solution.py:206
  168.3 3.7 %collective-permute-start.19 = (f32[]{:T(128)}, f32[]{:T(128)}, u32[]{:S(2)}, u32[]{:S(2)}) collective-permute-start(f32[]{:T(128)} %add.89), channel_id=1, source_target_pairs={{0,1},{1,0},{2,3},{3,2},{4,5},{5,4},{6,7},{7,6},{8,9},{9,8},{10,11... | collective-permute-start | bytes 20 | tf_op jit(solution)/shard_map/ppermute | solution.py:206
  172.6 4.6 %collective-permute-start.20 = (f32[]{:T(128)}, f32[]{:T(128)}, u32[]{:S(2)}, u32[]{:S(2)}) collective-permute-start(f32[]{:T(128)} %add.90), channel_id=1, source_target_pairs={{0,2},{1,3},{2,0},{3,1},{4,6},{5,7},{6,4},{7,5},{8,10},{9,11},{10,... | collective-permute-start | bytes 20 | tf_op jit(solution)/shard_map/ppermute | solution.py:206

commit v2 on v0

v2 whole, which is shorter than its diff:
```python
import functools

import jax
import jax.numpy as jnp
from jax import lax
from jax.experimental import pallas as pl
from jax.experimental.pallas import tpu as pltpu
from jax.sharding import PartitionSpec as P

EPSILON = 1e-06
F32 = jnp.float32
BF16 = jnp.bfloat16
VMEM_BYTES = 40 * 1024 * 1024


def split(x):
    high = x.astype(BF16)
    return high, (x - high.astype(F32)).astype(BF16)


def dot(a, b):
    return jnp.dot(a, b, preferred_element_type=F32)


def row_tile(rows):
    return next(size for size in (64, 32, 16, 8) if rows % size == 0)


def rows_at(first, count):
    return pl.ds(pl.multiple_of(first, count), count)


def start(copies):
    for copy in copies:
        copy.start()


def wait(copies):
    for copy in copies:
        copy.wait()


def load_blocks(src, dst, rows, sems):
    return [
        pltpu.make_async_copy(src.at[:, r, :], dst.at[pl.ds(r * rows, rows), :], sems.at[r])
        for r in range(src.shape[1])
    ]


def split_half(core, src, stacked):
    size, half = src.shape[0], stacked.shape[1]
    for side in range(2):

        @pl.when(core == side)
        def _():
            a, b = split(src[:, side * half : (side + 1) * half])
            stacked[0:size, :] = a
            stacked[size : 2 * size, :] = b
            stacked[2 * size : 3 * size, :] = a


def put_split(stacked, at, x):
    size = x.shape[1]
    a, b = split(x)
    stacked[at, 0:size] = a
    stacked[at, size : 2 * size] = a
    stacked[at, 2 * size : 3 * size] = b


def mix(operator, product, store):
    phys = len(operator)
    rows = product.shape[0] // phys
    tile = min(32, row_tile(rows))
    for first in range(0, rows, tile):
        pieces = [product[r * rows + first : r * rows + first + tile, :] for r in range(phys)]
        for p in range(phys):
            total = operator[p][0] * pieces[0]
            for r in range(1, phys):
                total = total + operator[p][r] * pieces[r]
            store(first, tile, p, *split(total))


def pick(refs, w, *at):
    count = refs[0].shape[0]
    low = jnp.minimum(w, count - 1)
    if len(refs) == 1:
        return refs[0][(low, *at)]
    high = jnp.maximum(w - count, 0)
    return jnp.where(w < count, refs[0][(low, *at)], refs[1][(high, *at)])


def run_pairs(number, phys, operators, pairs, sources, take, product, stacked, finish):
    def begin(i):
        take(i)
        product[...] = dot(sources[pairs[1, i]], stacked[...])

    def operator(i):
        w = pairs[0, i]
        return [[pick(operators, w, p, r) for r in range(phys)] for p in range(phys)]

    @pl.when(number > 0)
    def _():
        begin(0)

        @pl.loop(0, number - 1)
        def _(i):
            take(i + 1)
            store, close = finish(i)
            mix(operator(i), product, store)
            product[...] = dot(sources[pairs[1, i + 1]], stacked[...])
            close()

        store, close = finish(number - 1)
        mix(operator(number - 1), product, store)
        close()


def near_kernel(
    first_call, phys, chips, info, sizes, charges, operators, *refs,
):
    if first_call:
        energies, psi, left, right, total, share = refs[:6]
        raw, source, stacked, tall, product, mixed, pairs, sems, state = refs[6:]
    else:
        psi, left, right, base, total = refs[:5]
        raw, source, stacked, tall, product, mixed, pairs, sems = refs[5:]
    chip, core = info[0], info[1]
    sectors, size = psi.shape[0], psi.shape[1]
    count = left.shape[0]
    half = size // 2
    loads = []
    for t in range(sectors):
        loads += load_blocks(psi.at[t], raw.at[t], size, sems.at[t])
    start(loads)

    number = 0
    for w in range(count):
        for t in range(sectors):
            at = t - charges[w]
            inside = (at >= 0) & (at < sectors)
            pairs[0, number] = w
            pairs[1, number] = jnp.clip(at, 0, sectors - 1)
            pairs[2, number] = t
            number = number + inside.astype(jnp.int32)

    if not first_call:
        total[...] = base[...]
    tile = row_tile(size)
    for t in range(sectors):
        wait(loads[t * phys : (t + 1) * phys])
        limit = sizes[t]
        columns = lax.broadcasted_iota(jnp.int32, (tile, size), 1)
        lines = lax.broadcasted_iota(jnp.int32, (tile, size), 0)

        @pl.loop(0, size // tile)
        def _(i):
            keep = (columns < limit) & (lines + i * tile < limit)
            for r in range(phys):
                at = rows_at(r * size + i * tile, tile)
                x = jnp.where(keep, raw[t, at, :], 0)
                put_split(source.at[t], at, x)
                if first_call:
                    for side in range(2):

                        @pl.when(core == side)
                        def _():
                            state[t, rows_at(i * tile, tile), r * half : (r + 1) * half] = x[
                                :, side * half : (side + 1) * half
                            ]

            if first_call:
                at = rows_at(i * tile, tile)
                total[t, at, :] = state[t, at, :] * (energies[t] * (1.0 / chips))

    if first_call:
        rows = share.shape[2]
        for c in range(2):
            at = rows_at((2 * chip + (core ^ c)) * rows, rows)
            share[:, c] = state[:, at, :]

    def finish(i):
        w, t = pairs[0, i], pairs[2, i]

        def store(first, tile, p, a, b):
            cols = slice(p * half, (p + 1) * half)
            for place, value in enumerate((a, b, a)):
                mixed[place * size + first : place * size + first + tile, cols] = value

        def close():
            put_split(tall, slice(None), left[w, t])
            total[t] += dot(tall[...], mixed[...])

        return store, close

    def take(i):
        split_half(core, right.at[pairs[0, i], pairs[2, i]], stacked)

    run_pairs(number, phys, (operators,), pairs, source, take, product, stacked, finish)


def end_target(charge, sectors):
    return jnp.where(charge > 0, 0, sectors - 1)


def of_group(w, count, use):
    for group in range(2):

        @pl.when((w >= group * count) & (w < (group + 1) * count))
        def _():
            use(group, w - group * count)


def far_products(core, charges, operators, halo, right, raw, source, stacked, product, pairs, sems, finish):
    rows, phys, _ = halo[0].shape
    sectors = right[0].shape[1]
    count = charges[0].shape[0]
    loads = [load_blocks(halo[side], raw.at[side], rows, sems.at[side]) for side in range(2)]
    start(loads[0] + loads[1])
    number = 0
    for group in range(2):
        for w in range(count):
            charge = charges[group][w]
            pairs[0, number] = group * count + w
            pairs[1, number] = jnp.where(charge > 0, 0, 1)
            pairs[2, number] = end_target(charge, sectors)
            number = number + (charge != 0).astype(jnp.int32)
    lines = raw.shape[1]
    tile = row_tile(lines)
    for side in range(2):
        wait(loads[side])

        @pl.loop(0, lines // tile)
        def _(i):
            at = rows_at(i * tile, tile)
            put_split(source.at[side], at, raw[side, at, :])

    def take(i):
        t = pairs[2, i]
        of_group(pairs[0, i], count, lambda g, w: split_half(core, right[g].at[w, t], stacked))

    run_pairs(
        number, phys, operators, pairs, source, take, product, stacked,
        lambda i: (functools.partial(finish, pairs[0, i]), lambda: None),
    )
    return number


def far_first_kernel(
    info, charges_a, charges_b, operators_a, operators_b, low, high, right_a, right_b, early,
    raw, source, stacked, product, pairs, sems,
):
    half = low.shape[0]

    def store(w, first, tile, p, a, b):
        cols = slice(p * half, (p + 1) * half)
        early[w, 0, first : first + tile, cols] = a
        early[w, 1, first : first + tile, cols] = b

    far_products(
        info[1], (charges_a, charges_b), (operators_a, operators_b), (low, high), (right_a, right_b), raw,
        source, stacked, product, pairs, sems, store,
    )


def far_last_kernel(
    chips, info, charges_a, charges_b, operators_a, operators_b, low, high, right_a, right_b, left_a,
    left_b, near, early, *refs,
):
    outs = refs[:chips]
    raw, source, stacked, product, pairs, sems, tall, mixed, total = refs[chips:]
    chip, core = info[0], info[1]
    half = low.shape[0]
    size = 2 * half
    rows = outs[0].shape[2]
    count = charges_a.shape[0]

    def store(w, first, tile, p, a, b):
        cols = slice(p * half, (p + 1) * half)
        for place, value in enumerate((a, b, a)):
            at = rows_at(place * size + (1 - core) * half + first, tile)
            mixed[w, at, cols] = value

    number = far_products(
        core, (charges_a, charges_b), (operators_a, operators_b), (low, high), (right_a, right_b), raw,
        source, stacked, product, pairs, sems, store,
    )
    total[...] = near[...]

    @pl.loop(0, number)
    def _(i):
        w = pairs[0, i]
        t = pairs[2, i]
        for place, part in enumerate((0, 1, 0)):
            mixed[w, rows_at(place * size + core * half, half), :] = early[w, part]
        of_group(w, count, lambda g, v: put_split(tall, slice(None), (left_a, left_b)[g][v, t]))
        total[t] += dot(tall[...], mixed[w])

    for j in range(chips):
        for c in range(2):
            first = (2 * (chip ^ j) + (core ^ c)) * rows
            outs[j][:, c] = total[:, rows_at(first, rows), :]


def update_kernel(*refs):
    parts, (state, scale, mine, other, sums) = refs[:-5], refs[-5:]
    sectors, _, rows, lanes = state.shape
    tile = row_tile(rows)
    values = [jnp.zeros((8, lanes), F32)] * 5

    def fold(x):
        return jnp.sum(x.reshape(tile // 8, 8, lanes), axis=0)

    for t in range(sectors):
        for c in range(2):
            for first in range(0, rows, tile):
                at = (t, c, slice(first, first + tile), slice(None))
                total = parts[0][at]
                for part in parts[1:]:
                    total = total + part[at]
                s, k = state[at], scale[at]
                fixed = s - total * k
                slope = s * k
                (mine, other)[c][0, t, first : first + tile, :] = fixed
                (mine, other)[c][1, t, first : first + tile, :] = slope
                new = (s * total, s * s, fixed * fixed, fixed * slope, slope * slope)
                values = [v + fold(x) for v, x in zip(values, new)]
    column = lax.broadcasted_iota(jnp.int32, sums.shape, 1)
    result = jnp.zeros(sums.shape, F32)
    for i, v in enumerate(values):
        result = jnp.where(column == i, jnp.sum(v), result)
    sums[...] = result


def finish_kernel(numel, info, sums, mine, other, out, energies, whole, sems):
    core = info[1]
    column = lax.broadcasted_iota(jnp.int32, sums.shape, 1)
    values = [jnp.full((1, 128), jnp.sum(jnp.where(column == i, sums[...], 0)), F32) for i in range(5)]
    energy = values[0] / values[1]
    square = values[2] + 2 * energy * values[3] + energy * energy * values[4]
    factor = lax.rsqrt(jnp.maximum(square, 0) / numel + EPSILON)[0, 0]
    energy = energy[0, 0]
    energies[0] = energy
    _, sectors, rows, lanes = mine.shape
    phys = whole.shape[1]
    half = lanes // phys
    stores = []
    for t in range(sectors):
        for p in range(phys):
            cols = slice(p * half, (p + 1) * half)
            a = (mine[0, t, :, cols] + energy * mine[1, t, :, cols]) * factor
            b = (other[0, t, :, cols] + energy * other[1, t, :, cols]) * factor
            for side in range(2):

                @pl.when(core == side)
                def _():
                    whole[t, p, :, side * half : (side + 1) * half] = a
                    whole[t, p, :, (1 - side) * half : (2 - side) * half] = b

            copy = pltpu.make_async_copy(whole.at[t, p], out.at[t, :, p, :], sems.at[t, p])
            copy.start()
            stores.append(copy)
    wait(stores)


def swap_cores(x, count):
    return lax.ppermute(x, "term", [(i, i ^ 1) for i in range(count)])


def body(
    psi, precond, left_environment_block, right_env, term_operators, term_charge, sector_sizes,
    sector_energy,
):
    sectors, size, phys, _ = psi.shape
    terms = term_charge.shape[0]
    count, planes = lax.axis_size("term"), lax.axis_size("sector")
    chips = count // 2
    rows = size // count
    half = size // 2
    lanes = phys * half
    numel = sectors * planes * size * phys * size
    me = lax.axis_index("term")
    chip, core = me // 2, me % 2
    info = jnp.stack([chip, core]).astype(jnp.int32)

    positions = jnp.arange(size, dtype=jnp.int32)

    def edge(t):
        limit = sector_sizes[t]
        x = lax.dynamic_slice(psi, (t, core * half, 0, 0), (1, half, phys, size))[0]
        a = core * half + lax.broadcasted_iota(jnp.int32, x.shape, 0) < limit
        b = lax.broadcasted_iota(jnp.int32, x.shape, 2) < limit
        return jnp.where(a & b, x, 0)

    forward = [(i, i + 1) for i in range(planes - 1)]
    backward = [(b, a) for a, b in forward]
    low_a = lax.ppermute(edge(sectors - 1), "sector", forward)
    high_a = lax.ppermute(edge(0), "sector", backward)

    left_a, right_a, charges_a, operators_a = left_environment_block, right_env, term_charge, term_operators
    charges_b = swap_cores(charges_a, count)
    operators_b = swap_cores(operators_a, count)
    right_b = swap_cores(right_a, count)
    left_b = swap_cores(left_a, count)

    any_spec = pl.BlockSpec(memory_space=pl.ANY)
    smem = pl.BlockSpec(memory_space=pltpu.SMEM)
    vmem = pl.BlockSpec(memory_space=pltpu.VMEM)
    params = pltpu.CompilerParams(vmem_limit_bytes=VMEM_BYTES)
    wide = jax.ShapeDtypeStruct((sectors, size, lanes), F32)
    block = jax.ShapeDtypeStruct((sectors, 2, rows, lanes), F32)
    pair_list = pltpu.SMEM((3, 2 * terms * sectors + 1), jnp.int32)
    near_scratch = [
        pltpu.VMEM((sectors, phys * size, size), F32),
        pltpu.VMEM((sectors, phys * size, 3 * size), BF16),
        pltpu.VMEM((3 * size, half), BF16),
        pltpu.VMEM((size, 3 * size), BF16),
        pltpu.VMEM((phys * size, half), F32),
        pltpu.VMEM((3 * size, lanes), BF16),
        pair_list,
        pltpu.SemaphoreType.DMA((sectors, phys)),
    ]

    def cost(pairs):
        return pl.CostEstimate(
            flops=pairs * 3 * 4 * size * size * lanes, bytes_accessed=12 << 20, transcendentals=0
        )

    near, state = pl.pallas_call(
        functools.partial(near_kernel, True, phys, chips),
        out_shape=[wide, block],
        in_specs=[smem] * 5 + [any_spec] + [vmem] * 2,
        out_specs=[vmem] * 2,
        scratch_shapes=[*near_scratch, pltpu.VMEM((sectors, size, lanes), F32)],
        compiler_params=params,
        cost_estimate=cost(terms * sectors),
        name="near_own",
    )(info, sector_sizes, charges_a, operators_a, sector_energy, psi, left_a, right_a)
    near = pl.pallas_call(
        functools.partial(near_kernel, False, phys, chips),
        out_shape=wide,
        in_specs=[smem] * 4 + [any_spec] + [vmem] * 3,
        out_specs=vmem,
        scratch_shapes=near_scratch,
        compiler_params=params,
        cost_estimate=cost(terms * sectors),
        name="near_partner",
    )(info, sector_sizes, charges_b, operators_b, psi, left_b, right_b, near)

    low_a, high_a, near = lax.optimization_barrier((low_a, high_a, near))
    low_b = swap_cores(low_a, count)
    high_b = swap_cores(high_a, count)

    far_scratch = [
        pltpu.VMEM((2, phys * half, size), F32),
        pltpu.VMEM((2, phys * half, 3 * size), BF16),
        pltpu.VMEM((3 * size, half), BF16),
        pltpu.VMEM((phys * half, half), F32),
        pair_list,
        pltpu.SemaphoreType.DMA((2, phys)),
    ]
    early = pl.pallas_call(
        far_first_kernel,
        out_shape=jax.ShapeDtypeStruct((2 * terms, 2, half, lanes), BF16),
        in_specs=[smem] * 5 + [vmem] * 4,
        out_specs=vmem,
        scratch_shapes=far_scratch,
        compiler_params=params,
        cost_estimate=cost(terms // 2),
        name="far_first",
    )(info, charges_a, charges_b, operators_a, operators_b, low_a, high_a, right_a, right_b)

    parts = pl.pallas_call(
        functools.partial(far_last_kernel, chips),
        out_shape=[block] * chips,
        in_specs=[smem] * 5 + [vmem] * 8,
        out_specs=[vmem] * chips,
        scratch_shapes=[
            *far_scratch,
            pltpu.VMEM((size, 3 * size), BF16),
            pltpu.VMEM((2 * terms, 3 * size, lanes), BF16),
            pltpu.VMEM((sectors, size, lanes), F32),
        ],
        compiler_params=params,
        cost_estimate=cost(terms),
        name="far_last",
    )(
        info, charges_a, charges_b, operators_a, operators_b, low_b, high_b, right_a, right_b, left_a, left_b,
        near, early,
    )

    *parts, precond = lax.optimization_barrier((*parts, precond))
    parts = [parts[0]] + [
        lax.ppermute(parts[j], "term", [(i, i ^ (2 * j)) for i in range(count)]) for j in range(1, chips)
    ]

    first = chip * 2 * rows
    inside = positions[None, :] < sector_sizes[:, None]
    scale = lax.dynamic_slice(
        precond, (0, first, 0, core * half), (sectors, 2 * rows, phys, half)
    ).astype(F32)
    a = lax.dynamic_slice(inside, (0, first), (sectors, 2 * rows))
    b = lax.dynamic_slice(inside, (0, core * half), (sectors, half))
    scale = jnp.where(a[:, :, None, None] & b[:, None, None, :], 1.0 / scale, 0)
    scale = scale.reshape(sectors, 2, rows, lanes)
    scale = jnp.where(core == 0, scale, scale[:, ::-1])

    devices = count * planes
    pair = jax.ShapeDtypeStruct((2, sectors, rows, lanes), F32)
    mine, other, sums = pl.pallas_call(
        update_kernel,
        out_shape=[pair, pair, jax.ShapeDtypeStruct((devices, 128), F32)],
        in_specs=[vmem] * (chips + 2),
        out_specs=[vmem] * 3,
        compiler_params=params,
        name="update",
    )(*parts, state, scale)
    other = swap_cores(other, count)
    sums = lax.all_to_all(sums, ("sector", "term"), 0, 0, tiled=True)
    return tuple(
        pl.pallas_call(
            functools.partial(finish_kernel, numel),
            out_shape=[
                jax.ShapeDtypeStruct((sectors, rows, phys, size), F32),
                jax.ShapeDtypeStruct((1,), F32),
            ],
            in_specs=[smem] + [vmem] * 3,
            out_specs=[any_spec, smem],
            scratch_shapes=[
                pltpu.VMEM((sectors, phys, rows, size), F32),
                pltpu.SemaphoreType.DMA((sectors, phys)),
            ],
            compiler_params=params,
            name="finish",
        )(info, sums, mine, other)
    )


def solution(mesh):
    in_specs = (
        P("sector", None, None, None),
        P("sector", None, None, None),
        P("term", "sector", None, None),
        P("term", "sector", None, None),
        P("term", None, None),
        P("term"),
        P("sector"),
        P("sector"),
    )
    out_specs = (P("sector", "term", None, None), P())
    return jax.shard_map(body, mesh=mesh, in_specs=in_specs, out_specs=out_specs, check_vma=False)
```

time: 302 us -> 125 us (0.41)
  waiting for transfers between devices: 139 us -> 20.6 us
  matrix products: 62.9 us -> 0 us
  Pallas kernels: 0 us -> 52.2 us
  other arithmetic: 31.9 us -> 10.8 us
  between operations: 17.3 us -> 1.01 us
  blocking collectives: 21.3 us -> 13.8 us
  local copies, waits for them, and re-layouts: 18.6 us -> 13.7 us
  starting transfers between devices: 7.69 us -> 12 us
    psum x1 -> x0, waiting for transfers between devices: 85.7 us -> none  [body(): total = lax.psum(partial_sum, 'term')]
    dot_general x6 -> x0, matrix products: 62.9 us -> none  [the longest x2 25.7 us: single_term(): third = jnp.einsum('tape,teb->tapb', second, right, precision=TOP_LEVEL)]
    pallas_call x0 -> x6, Pallas kernels: none -> 52.2 us  [the longest x1 16.4 us: body(): pl.pallas_call(functools.partial(far_last_kernel, chips), out_shape=[bloc...]
    ppermute x2 -> x12, waiting for transfers between devices: 53.6 us -> 20.6 us  [the longest x3 19.6 us: body(): lax.ppermute(parts[j], 'term', [(i, i ^ 2 * j) for i in range(count)])]
    psum x2 -> x0, blocking collectives: 21.3 us -> none  [the longest x1 12.3 us: body(): lax.psum((jnp.sum(state * image), jnp.sum(state * state)), 'sector')]
    reduce_sum x2 -> x0, other arithmetic: 15.7 us -> none  [the longest x1 9.23 us: body(): square = lax.psum(jnp.sum(moved * moved), 'sector')]
    all_to_all x0 -> x1, blocking collectives: none -> 13.8 us  [body(): sums = lax.all_to_all(sums, ('sector', 'term'), 0, 0, tiled=True)]
    concatenate x1 -> x0, other arithmetic: 9.77 us -> none  [with_halo(): block = jnp.concatenate([low, block, high], axis=dim)]
  transfers between devices with their start and end apart: 3 -> 12, of which waited for: 3 -> 4; matrix products, arithmetic and copies ran while one was open for 0% -> 12% of each run, Pallas kernels for 0% -> 26%
where the time goes in v2:
time: 125 us; the launch traced here: 124 us
  Pallas kernels  52.2 us (42%)
  waiting for transfers between devices  20.6 us (16%)
  blocking collectives  13.8 us (11%)
  local copies, waits for them, and re-layouts  13.7 us (11%)
  starting transfers between devices  12 us (10%)
  other arithmetic  10.8 us (9%)
    ppermute x3, waiting for transfers between devices, body(): lax.ppermute(parts[j], 'term', [(i, i ^ 2 * j) for i in range(count)])  19.6 us
    pallas_call x1, Pallas kernels, body(): pl.pallas_call(functools.partial(far_last_kernel, chips), out_shape=[bloc...  16.4 us
    all_to_all x1, blocking collectives, body(): sums = lax.all_to_all(sums, ('sector', 'term'), 0, 0, tiled=True)  13.8 us
    pallas_call x1, Pallas kernels, body(): pl.pallas_call(functools.partial(near_kernel, True, phys, chips), out_sha...  12.2 us
    pallas_call x1, Pallas kernels, body(): pl.pallas_call(functools.partial(near_kernel, False, phys, chips), out_sh...  12 us
    unnamed x30, local copies, waits for them, and re-layouts  9.73 us
    pallas_call x1, Pallas kernels, body(): pl.pallas_call(far_first_kernel, out_shape=jax.ShapeDtypeStruct((2 * term...  8.29 us
    ppermute x1, starting transfers between devices, body(): low_a = lax.ppermute(edge(sectors - 1), 'sector', forward)  4.97 us
  transfers between devices with their start and end apart: 12, of which 4 were waited for; matrix products, arithmetic and copies ran while one was open for 12% of the time, Pallas kernels for 26%

profile of v2, /device:TPU:0, one launch (start us, length us, event | category | flops | bytes accessed | tf_op | source)
XLA Modules:
  0.0 124.2 jit_solution(17795992830016081041)
XLA Ops:
  0.6 0.5 collective-permute-start.5
  1.1 0.1 collective-permute-start.4
  1.2 1.4 %fusion.2 = (s32[1]{0:T(128)}, s32[1]{0:T(128)}) fusion(s32[2]{0:T(128)} %sizes.3), kind=kLoop, calls=%fused_computation.14 | loop fusion | bytes 16 | tf_op jit(solution)/shard_map/slice | solution.py:388
  2.6 1.3 %fusion = (pred[192]{0:T(512)(128)(4,1)S(1)}, pred[192]{0:T(512)(128)(4,1)S(1)}) fusion(s32[]{:T(128)} %bitcast.4, s32[]{:T(128)S(6)} %mul.4, s32[]{:T(128)} %bitcast.2), kind=kLoop, calls=%fused_computation.11 | loop fusion | flops 576 | bytes 396 | tf_op jit(solution)/shard_map/lt | solution.py:390
  4.0 1.3 %iota_compare_fusion.1 = (pred[384]{0:T(512)(128)(4,1)S(1)}, pred[384]{0:T(512)(128)(4,1)S(1)}) fusion(s32[]{:T(128)} %bitcast.4, s32[]{:T(128)} %bitcast.2), kind=kLoop, calls=%fused_computation.6 | loop fusion | flops 768 | bytes 776 | tf_op jit(solution)/shard_map/lt | solution.py:391
  5.3 0.0 copy-start.10
  5.3 0.0 copy-start.8
  5.3 0.0 copy-start
  5.4 0.0 copy-start.9
  5.4 3.6 %bitcast_select_fusion = (f32[192,4,384]{2,1,0:T(4,128)}, f32[192,4,384]{2,1,0:T(4,128)}) fusion(f32[2,384,4,384]{3,2,1,0:T(4,128)} %refs_0_.3, s32[]{:T(128)S(6)} %select_n.42, pred[384]{0:T(512)(128)(4,1)S(1)} %get-tuple-element.42, pred[192]{0:T(512)(128)(4,1)S(1)} %get-tuple-element.40, pred[384]{0:T(512)(128)(4,1)S(1)} %get-tuple-element.43, ...), kind=kLoop, calls=%fused_computation | loop fusion | flops 1179648 | bytes 4719748 | tf_op jit(solution)/shard_map/jit(_where)/select_n | solution.py:392
  8.9 5.0 %collective-permute-start.2 = (f32[192,4,384]{2,1,0:T(4,128)}, f32[192,4,384]{2,1,0:T(4,128)S(1)}, u32[]{:S(2)}, u32[]{:S(2)}) collective-permute-start(f32[192,4,384]{2,1,0:T(4,128)} %get-tuple-element.37), channel_id=1, source_target_pairs={{0,1},{1,2},{2,3},{4,5},{5,6},{6,7},{8,9},{9,10},{10,11},{12,13},{... | collective-permute-start | bytes 3538952 | tf_op jit(solution)/shard_map/ppermute | solution.py:396
  13.9 1.3 %collective-permute-start.3 = (f32[192,4,384]{2,1,0:T(4,128)}, f32[192,4,384]{2,1,0:T(4,128)}, u32[]{:S(2)}, u32[]{:S(2)}) collective-permute-start(f32[192,4,384]{2,1,0:T(4,128)} %get-tuple-element.36), channel_id=1, source_target_pairs={{1,0},{2,1},{3,2},{5,4},{6,5},{7,6},{9,8},{10,9},{11,10},{13,12},{... | collective-permute-start | bytes 3538952 | tf_op jit(solution)/shard_map/ppermute | solution.py:397
  15.2 0.0 copy-done.10
  15.2 0.1 collective-permute-start
  15.3 0.1 pad_add_fusion.info
  15.4 1.0 collective-permute-done.charges.charges_b
  16.4 0.0 copy-done.8
  16.4 0.2 collective-permute-start.1
  16.6 0.0 copy-done
  16.6 0.0 copy-done.9
  16.6 1.7 %copy-done.2 = f32[2,2,384,384]{3,2,1,0:T(8,128)S(1)} copy-done((f32[2,2,384,384]{3,2,1,0:T(8,128)S(1)}, f32[2,2,384,384]{3,2,1,0:T(8,128)}, u32[]{:S(2)}) %copy-start.2) | copy-done | bytes 2359320
  18.3 2.3 %copy-done.5 = f32[2,384,4,384]{3,2,1,0:T(4,128)S(1)} copy-done((f32[2,384,4,384]{3,2,1,0:T(4,128)S(1)}, f32[2,384,4,384]{3,2,1,0:T(4,128)}, u32[]{:S(2)}) %copy-start.5) | copy-done | bytes 4718616
  20.6 0.7 copy-done.11
  21.3 0.7 copy-done.14
  21.9 12.2 %near_own.1 = (f32[2,384,768]{2,1,0:T(8,128)S(1)}, f32[2,2,48,768]{3,2,1,0:T(8,128)S(1)}) custom-call(s32[2]{0:T(128)S(1)} %pad_add_fusion.info, s32[2]{0:T(128)S(1)} %copy-done.9, s32[2]{0:T(128)S(1)} %copy-done.11, f32[2,4,4]{2,1,0:T(4,128)S(1)} %copy-done.8, f32[2]{0:T(128)S(1)} %copy-done.14, f32[2,384,4,384]{3,2,1,0:T(4,128)S(1)} %copy-done.5, ...), custom_call_target="tpu_custom_call" | custom-call | flops 5435817984 | bytes 12582912 | tf_op jit(solution)/shard_map/near_own/pallas_call | solution.py:428
  34.1 0.0 copy-start.6
  34.1 0.8 copy-done.6
  35.0 0.0 collective-permute-done.1.operators.operators_b
  35.0 0.0 collective-permute-done.5.refs_2_.right_b
  35.0 0.0 collective-permute-done.4.refs_1_.left_b
  35.0 12.0 %near_partner.1.near = f32[2,384,768]{2,1,0:T(8,128)S(1)} custom-call(s32[2]{0:T(128)S(1)} %pad_add_fusion.info, s32[2]{0:T(128)S(1)} %copy-done.9, s32[2]{0:T(128)} %collective-permute-done.charges.charges_b, f32[2,4,4]{2,1,0:T(4,128)S(1)} %collective-permute-done.1.operators.operators_b, f32[2,384,4,384]{3,2,1,0:T(4,128)S(1)} %copy-done.5, ...), custom_call_target="tpu_custom_call" | custom-call | flops 5435817984 | bytes 12582912 | tf_op jit(solution)/shard_map/near_partner/pallas_call | solution.py:438
  47.0 0.0 copy-start.4
  47.0 1.5 %copy-done.4 = f32[2,384,768]{2,1,0:T(8,128)} copy-done((f32[2,384,768]{2,1,0:T(8,128)}, f32[2,384,768]{2,1,0:T(8,128)S(1)}, u32[]{:S(2)}) %copy-start.4) | copy-done | bytes 2359320
  48.5 0.0 collective-permute-done.2.low
  48.5 0.0 collective-permute-done.3.high
  48.5 1.0 collective-permute-start.6
  49.5 0.1 collective-permute-start.7
  49.6 0.1 iota_compare_fusion
  49.7 0.1 constant_dynamic-slice_fusion.1
  49.7 0.1 constant_dynamic-slice_fusion
  49.8 0.7 copy-done.12
  50.5 8.3 %far_first.1.early = bf16[4,2,192,768]{3,2,1,0:T(8,128)(2,1)S(1)} custom-call(s32[2]{0:T(128)S(1)} %pad_add_fusion.info, s32[2]{0:T(128)S(1)} %copy-done.12, s32[2]{0:T(128)} %collective-permute-done.charges.charges_b, f32[2,4,4]{2,1,0:T(4,128)S(1)} %copy-done.8, f32[2,4,4]{2,1,0:T(4,128)S(1)} %collective-permute-done.1.operators.operators_b, ...), custom_call_target="tpu_custom_call" | custom-call | flops 1358954496 | bytes 12582912 | tf_op jit(solution)/shard_map/far_first/pallas_call | solution.py:461
  58.8 0.0 copy-start.1
  58.8 1.5 %copy-done.1 = bf16[4,2,192,768]{3,2,1,0:T(8,128)(2,1)} copy-done((bf16[4,2,192,768]{3,2,1,0:T(8,128)(2,1)}, bf16[4,2,192,768]{3,2,1,0:T(8,128)(2,1)S(1)}, u32[]{:S(2)}) %copy-start.1) | copy-done | bytes 2359320
  60.3 0.0 collective-permute-done.6.low
  60.3 0.0 collective-permute-done.7.high
  60.3 0.0 copy-done.3
  60.3 0.0 copy-done.13
  60.3 16.4 %far_last.1 = (f32[2,2,48,768]{3,2,1,0:T(8,128)S(1)}, f32[2,2,48,768]{3,2,1,0:T(8,128)}, f32[2,2,48,768]{3,2,1,0:T(8,128)S(1)}, f32[2,2,48,768]{3,2,1,0:T(8,128)}) custom-call(s32[2]{0:T(128)S(1)} %pad_add_fusion.info, s32[2]{0:T(128)S(1)} %copy-done.13, s32[2]{0:T(128)} %collective-permute-done.charges.charges_b, f32[2,4,4]{2,1,0:T(4,128)S(1)} %copy-done.8, ...), custom_call_target="tpu_custom_call" | custom-call | flops 2717908992 | bytes 12582912 | tf_op jit(solution)/shard_map/far_last/pallas_call | solution.py:472
  76.7 1.3 %collective-permute-start.10 = (f32[2,2,48,768]{3,2,1,0:T(8,128)}, f32[2,2,48,768]{3,2,1,0:T(8,128)S(1)}, u32[]{:S(2)}, u32[]{:S(2)}) collective-permute-start(f32[2,2,48,768]{3,2,1,0:T(8,128)} %get-tuple-element.30), channel_id=1, source_target_pairs={{0,24},{4,28},{8,16},{12,20},{16,8},{20,12},{24,0},{28,4},{1,25},{... | collective-permute-start | bytes 1769480 | tf_op jit(solution)/shard_map/ppermute | solution.py:493
  78.0 1.8 %collective-permute-start.8 = (f32[2,2,48,768]{3,2,1,0:T(8,128)}, f32[2,2,48,768]{3,2,1,0:T(8,128)S(1)}, u32[]{:S(2)}, u32[]{:S(2)}) collective-permute-start(f32[2,2,48,768]{3,2,1,0:T(8,128)} %get-tuple-element.28), channel_id=1, source_target_pairs={{0,8},{4,12},{8,0},{12,4},{16,24},{20,28},{24,16},{28,20},{1,9},{5... | collective-permute-start | bytes 1769480 | tf_op jit(solution)/shard_map/ppermute | solution.py:493
  79.8 0.5 collective-permute-start.9
  80.3 0.7 broadcast_and_fusion
  81.0 2.4 %divide_select_fusion = f32[2,96,4,192]{3,2,1,0:T(4,128)} fusion(bf16[2,384,4,384]{3,2,1,0:T(4,128)(2,1)} %param.9, s32[]{:T(128)S(6)} %select_n.46, s32[]{:T(128)S(6)} %select_n.42, pred[2,96,192]{2,1,0:T(8,128)(4,1)} %broadcast_and_fusion), kind=kLoop, calls=%fused_computation.3 | loop fusion | flops 442368 | bytes 921608 | tf_op jit(solution)/shard_map/jit(_where)/select_n | solution.py:503
  83.4 2.4 %reshape.18 = f32[2,2,48,768]{3,2,1,0:T(8,128)} reshape(f32[2,96,4,192]{3,2,1,0:T(4,128)} %divide_select_fusion) | data formatting | bytes 1179648 | tf_op jit(solution)/shard_map/reshape | solution.py:504
  85.9 1.3 %reverse_select_fusion.refs_5_ = f32[2,2,48,768]{3,2,1,0:T(8,128)S(1)} fusion(f32[2,2,48,768]{3,2,1,0:T(8,128)} %reshape.18, pred[]{:T(512)S(6)} %eq.5), kind=kLoop, calls=%fused_computation.2 | loop fusion | flops 147456 | bytes 1179649 | tf_op jit(solution)/shard_map/jit(_where)/select_n | solution.py:505
  87.2 6.7 %collective-permute-done.10.refs_3_ = f32[2,2,48,768]{3,2,1,0:T(8,128)S(1)} collective-permute-done((f32[2,2,48,768]{3,2,1,0:T(8,128)}, f32[2,2,48,768]{3,2,1,0:T(8,128)S(1)}, u32[]{:S(2)}, u32[]{:S(2)}) %collective-permute-start.10) | collective-permute-done | bytes 589856 | tf_op jit(solution)/shard_map/ppermute | solution.py:493
  93.9 12.7 %collective-permute-done.8.refs_1_ = f32[2,2,48,768]{3,2,1,0:T(8,128)S(1)} collective-permute-done((f32[2,2,48,768]{3,2,1,0:T(8,128)}, f32[2,2,48,768]{3,2,1,0:T(8,128)S(1)}, u32[]{:S(2)}, u32[]{:S(2)}) %collective-permute-start.8) | collective-permute-done | bytes 589856 | tf_op jit(solution)/shard_map/ppermute | solution.py:493
  106.6 0.2 collective-permute-done.9.refs_2_
  106.7 0.5 update.1
  107.3 0.2 collective-permute-start.11
  107.5 13.8 %all_to_all.11 = f32[32,1,128]{2,1,0:T(1,128)S(1)} all-to-all(f32[32,1,128]{2,1,0:T(1,128)S(1)} %bitcast.13), channel_id=1, replica_groups=mesh['term'=8,'sector'=4] {'sector','term'}, dimensions={0} | all-to-all | bytes 32768 | tf_op jit(solution)/shard_map/all_to_all | solution.py:518
  121.3 0.0 collective-permute-done.11.other
  121.3 2.7 %finish.1 = (f32[2,48,4,384]{3,2,1,0:T(4,128)}, f32[1]{0:T(128)}) custom-call(s32[2]{0:T(128)S(1)} %pad_add_fusion.info, f32[32,128]{1,0:T(8,128)S(1)} %bitcast.12, f32[2,2,48,768]{3,2,1,0:T(8,128)S(1)} %get-tuple-element.34.mine, f32[2,2,48,768]{3,2,1,0:T(8,128)S(1)} %collective-permute-done.11.other), custom_call_target="tpu_custom_call" | custom-call | tf_op jit(solution)/shard_map/finish/pallas_call | solution.py:520
  (9 shorter events, 0.0 us)
Async XLA Ops:
  0.6 34.3 %collective-permute-start.5 = (f32[2,2,384,384]{3,2,1,0:T(8,128)}, f32[2,2,384,384]{3,2,1,0:T(8,128)}, u32[]{:S(2)}, u32[]{:S(2)}) collective-permute-start(f32[2,2,384,384]{3,2,1,0:T(8,128)} %right_a.3), channel_id=1, source_target_pairs={{0,4},{4,0},{8,12},{12,8},{16,20},{20,16},{24,28},{28,24},{1,5},{5... | collective-permute-start | bytes 7077896 | tf_op jit(solution)/shard_map/ppermute | solution.py:366
  1.1 33.8 %collective-permute-start.4 = (f32[2,2,384,384]{3,2,1,0:T(8,128)}, f32[2,2,384,384]{3,2,1,0:T(8,128)}, u32[]{:S(2)}, u32[]{:S(2)}) collective-permute-start(f32[2,2,384,384]{3,2,1,0:T(8,128)} %left_a.1), channel_id=1, source_target_pairs={{0,4},{4,0},{8,12},{12,8},{16,20},{20,16},{24,28},{28,24},{1,5},{5... | collective-permute-start | bytes 7077896 | tf_op jit(solution)/shard_map/ppermute | solution.py:366
  5.3 9.9 %copy-start.10 = (s32[2]{0:T(128)S(1)}, s32[2]{0:T(128)}, u32[]{:S(2)}) copy-start(s32[2]{0:T(128)} %charges_a.3) | copy-start | bytes 28
  5.3 11.0 %copy-start.8 = (f32[2,4,4]{2,1,0:T(4,128)S(1)}, f32[2,4,4]{2,1,0:T(4,128)}, u32[]{:S(2)}) copy-start(f32[2,4,4]{2,1,0:T(4,128)} %operators_a.3) | copy-start | bytes 388
  5.3 11.3 %copy-start = (f32[2,2,384,384]{3,2,1,0:T(8,128)S(1)}, f32[2,2,384,384]{3,2,1,0:T(8,128)}, u32[]{:S(2)}) copy-start(f32[2,2,384,384]{3,2,1,0:T(8,128)} %right_a.3) | copy-start | bytes 7077892
  5.4 11.3 %copy-start.9 = (s32[2]{0:T(128)S(1)}, s32[2]{0:T(128)}, u32[]{:S(2)}) copy-start(s32[2]{0:T(128)} %sizes.3) | copy-start | bytes 28
  8.9 39.6 %collective-permute-start.2 = (f32[192,4,384]{2,1,0:T(4,128)}, f32[192,4,384]{2,1,0:T(4,128)S(1)}, u32[]{:S(2)}, u32[]{:S(2)}) collective-permute-start(f32[192,4,384]{2,1,0:T(4,128)} %get-tuple-element.37), channel_id=1, source_target_pairs={{0,1},{1,2},{2,3},{4,5},{5,6},{6,7},{8,9},{9,10},{10,11},{12,13},{... | collective-permute-start | bytes 3538952 | tf_op jit(solution)/shard_map/ppermute | solution.py:396
  13.9 34.6 %collective-permute-start.3 = (f32[192,4,384]{2,1,0:T(4,128)}, f32[192,4,384]{2,1,0:T(4,128)}, u32[]{:S(2)}, u32[]{:S(2)}) collective-permute-start(f32[192,4,384]{2,1,0:T(4,128)} %get-tuple-element.36), channel_id=1, source_target_pairs={{1,0},{2,1},{3,2},{5,4},{6,5},{7,6},{9,8},{10,9},{11,10},{13,12},{... | collective-permute-start | bytes 3538952 | tf_op jit(solution)/shard_map/ppermute | solution.py:397
  15.2 1.2 collective-permute-start
  16.4 18.6 %collective-permute-start.1 = (f32[2,4,4]{2,1,0:T(4,128)S(1)}, f32[2,4,4]{2,1,0:T(4,128)S(1)}, u32[]{:S(2)}, u32[]{:S(2)}) collective-permute-start(f32[2,4,4]{2,1,0:T(4,128)S(1)} %copy-done.8), channel_id=1, source_target_pairs={{0,4},{4,0},{8,12},{12,8},{16,20},{20,16},{24,28},{28,24},{1,5},{5... | collective-permute-start | bytes 392 | tf_op jit(solution)/shard_map/ppermute | solution.py:366
  16.6 1.7 %copy-start.2 = (f32[2,2,384,384]{3,2,1,0:T(8,128)S(1)}, f32[2,2,384,384]{3,2,1,0:T(8,128)}, u32[]{:S(2)}) copy-start(f32[2,2,384,384]{3,2,1,0:T(8,128)} %left_a.1) | copy-start | bytes 7077892
  18.3 2.3 %copy-start.5 = (f32[2,384,4,384]{3,2,1,0:T(4,128)S(1)}, f32[2,384,4,384]{3,2,1,0:T(4,128)}, u32[]{:S(2)}) copy-start(f32[2,384,4,384]{3,2,1,0:T(4,128)} %refs_0_.3) | copy-start | bytes 14155780
  20.6 0.7 copy-start.11
  21.3 0.7 copy-start.14
  34.1 0.8 copy-start.6
  47.0 1.5 %copy-start.4 = (f32[2,384,768]{2,1,0:T(8,128)}, f32[2,384,768]{2,1,0:T(8,128)S(1)}, u32[]{:S(2)}) copy-start(f32[2,384,768]{2,1,0:T(8,128)S(1)} %near_partner.1.near) | copy-start | bytes 7077892
  48.5 11.8 %collective-permute-start.6 = (f32[192,4,384]{2,1,0:T(4,128)S(1)}, f32[192,4,384]{2,1,0:T(4,128)}, u32[]{:S(2)}, u32[]{:S(2)}) collective-permute-start(f32[192,4,384]{2,1,0:T(4,128)S(1)} %collective-permute-done.2.low), channel_id=1, source_target_pairs={{0,4},{4,0},{8,12},{12,8},{16,20},{20,16},{24,28},{28,24},{1,5},{5... | collective-permute-start | bytes 3538952 | tf_op jit(solution)/shard_map/ppermute | solution.py:366
  49.5 10.7 %collective-permute-start.7 = (f32[192,4,384]{2,1,0:T(4,128)}, f32[192,4,384]{2,1,0:T(4,128)}, u32[]{:S(2)}, u32[]{:S(2)}) collective-permute-start(f32[192,4,384]{2,1,0:T(4,128)} %collective-permute-done.3.high), channel_id=1, source_target_pairs={{0,4},{4,0},{8,12},{12,8},{16,20},{20,16},{24,28},{28,24},{1,5},{5... | collective-permute-start | bytes 3538952 | tf_op jit(solution)/shard_map/ppermute | solution.py:366
  49.8 0.7 copy-start.12
  50.5 9.8 %copy-start.3 = (f32[2,2,384,384]{3,2,1,0:T(8,128)S(1)}, f32[2,2,384,384]{3,2,1,0:T(8,128)}, u32[]{:S(2)}) copy-start(f32[2,2,384,384]{3,2,1,0:T(8,128)} %left_a.1) | copy-start | bytes 7077892
  50.5 9.8 %copy-start.13 = (s32[2]{0:T(128)S(1)}, s32[2]{0:T(128)}, u32[]{:S(2)}) copy-start(s32[2]{0:T(128)} %charges_a.3) | copy-start | bytes 28
  58.8 1.5 %copy-start.1 = (bf16[4,2,192,768]{3,2,1,0:T(8,128)(2,1)}, bf16[4,2,192,768]{3,2,1,0:T(8,128)(2,1)S(1)}, u32[]{:S(2)}) copy-start(bf16[4,2,192,768]{3,2,1,0:T(8,128)(2,1)S(1)} %far_first.1.early) | copy-start | bytes 7077892
  76.7 30.0 %copy-start.7 = (f32[2,2,48,768]{3,2,1,0:T(8,128)S(1)}, f32[2,2,48,768]{3,2,1,0:T(8,128)}, u32[]{:S(2)}) copy-start(f32[2,2,48,768]{3,2,1,0:T(8,128)} %copy-done.6) | copy-start | bytes 1769476
  76.7 17.2 %collective-permute-start.10 = (f32[2,2,48,768]{3,2,1,0:T(8,128)}, f32[2,2,48,768]{3,2,1,0:T(8,128)S(1)}, u32[]{:S(2)}, u32[]{:S(2)}) collective-permute-start(f32[2,2,48,768]{3,2,1,0:T(8,128)} %get-tuple-element.30), channel_id=1, source_target_pairs={{0,24},{4,28},{8,16},{12,20},{16,8},{20,12},{24,0},{28,4},{1,25},{... | collective-permute-start | bytes 1769480 | tf_op jit(solution)/shard_map/ppermute | solution.py:493
  78.0 28.6 %collective-permute-start.8 = (f32[2,2,48,768]{3,2,1,0:T(8,128)}, f32[2,2,48,768]{3,2,1,0:T(8,128)S(1)}, u32[]{:S(2)}, u32[]{:S(2)}) collective-permute-start(f32[2,2,48,768]{3,2,1,0:T(8,128)} %get-tuple-element.28), channel_id=1, source_target_pairs={{0,8},{4,12},{8,0},{12,4},{16,24},{20,28},{24,16},{28,20},{1,9},{5... | collective-permute-start | bytes 1769480 | tf_op jit(solution)/shard_map/ppermute | solution.py:493
  79.8 27.0 %collective-permute-start.9 = (f32[2,2,48,768]{3,2,1,0:T(8,128)S(1)}, f32[2,2,48,768]{3,2,1,0:T(8,128)S(1)}, u32[]{:S(2)}, u32[]{:S(2)}) collective-permute-start(f32[2,2,48,768]{3,2,1,0:T(8,128)S(1)} %get-tuple-element.29), channel_id=1, source_target_pairs={{0,16},{4,20},{8,24},{12,28},{16,0},{20,4},{24,8},{28,12},{1,17},{... | collective-permute-start | bytes 1769480 | tf_op jit(solution)/shard_map/ppermute | solution.py:493
  107.3 14.0 %collective-permute-start.11 = (f32[2,2,48,768]{3,2,1,0:T(8,128)S(1)}, f32[2,2,48,768]{3,2,1,0:T(8,128)S(1)}, u32[]{:S(2)}, u32[]{:S(2)}) collective-permute-start(f32[2,2,48,768]{3,2,1,0:T(8,128)S(1)} %get-tuple-element.35), channel_id=1, source_target_pairs={{0,4},{4,0},{8,12},{12,8},{16,20},{20,16},{24,28},{28,24},{1,5},{5... | collective-permute-start | bytes 1769480 | tf_op jit(solution)/shard_map/ppermute | solution.py:366

commit v3 on v2

v3 whole, which is shorter than its diff:
```python
import functools

import jax
import jax.numpy as jnp
from jax import lax
from jax.experimental import pallas as pl
from jax.experimental.pallas import tpu as pltpu
from jax.sharding import PartitionSpec as P

EPSILON = 1e-06
F32 = jnp.float32
BF16 = jnp.bfloat16
VMEM_BYTES = 24 * 1024 * 1024
SEND_BYTES = 60 * 1024 * 1024


def split(x):
    high = x.astype(BF16)
    return high, (x - high.astype(F32)).astype(BF16)


def dot(a, b):
    return jnp.dot(a, b, preferred_element_type=F32)


def row_tile(rows):
    return next(size for size in (64, 32, 16, 8) if rows % size == 0)


class Window:
    def __init__(self, flat, offset, shape):
        self.flat, self.offset, self.shape = flat, offset, shape

    def __getitem__(self, at):
        place = 0
        for size, i in zip(self.shape, at if isinstance(at, tuple) else (at,)):
            place = place * size + i
        return self.flat[self.offset + place]


def unpack(ints, floats, sectors, terms, phys):
    return (
        Window(ints, 2 + sectors, (terms,)),
        Window(floats, 0, (terms, phys, phys)),
        Window(ints, 2, (sectors,)),
        Window(floats, terms * phys * phys, (sectors,)),
    )


def rows_at(first, count):
    return pl.ds(pl.multiple_of(first, count), count)


def start(copies):
    for copy in copies:
        copy.start()


def wait(copies):
    for copy in copies:
        copy.wait()


def load_blocks(src, dst, rows, sems):
    return [
        pltpu.make_async_copy(src.at[:, r, :], dst.at[pl.ds(r * rows, rows), :], sems.at[r])
        for r in range(src.shape[1])
    ]


def split_half(core, src, stacked):
    size, half = src.shape[0], stacked.shape[1]
    for side in range(2):

        @pl.when(core == side)
        def _():
            a, b = split(src[:, side * half : (side + 1) * half])
            stacked[0:size, :] = a
            stacked[size : 2 * size, :] = b
            stacked[2 * size : 3 * size, :] = a


def put_split(stacked, at, x):
    size = x.shape[1]
    a, b = split(x)
    stacked[at, 0:size] = a
    stacked[at, size : 2 * size] = a
    stacked[at, 2 * size : 3 * size] = b


def mix(operator, product, store):
    phys = len(operator)
    rows = product.shape[0] // phys
    tile = min(32, row_tile(rows))
    for first in range(0, rows, tile):
        pieces = [product[r * rows + first : r * rows + first + tile, :] for r in range(phys)]
        for p in range(phys):
            total = operator[p][0] * pieces[0]
            for r in range(1, phys):
                total = total + operator[p][r] * pieces[r]
            store(first, tile, p, *split(total))


def pick(refs, w, *at):
    count = refs[0].shape[0]
    low = jnp.minimum(w, count - 1)
    if len(refs) == 1:
        return refs[0][(low, *at)]
    high = jnp.maximum(w - count, 0)
    return jnp.where(w < count, refs[0][(low, *at)], refs[1][(high, *at)])


def run_pairs(number, phys, operators, pairs, sources, take, product, stacked, finish):
    def begin(i):
        take(i)
        product[...] = dot(sources[pairs[1, i]], stacked[...])

    def operator(i):
        w = pairs[0, i]
        return [[pick(operators, w, p, r) for r in range(phys)] for p in range(phys)]

    @pl.when(number > 0)
    def _():
        begin(0)

        @pl.loop(0, number - 1)
        def _(i):
            take(i + 1)
            store, close = finish(i)
            mix(operator(i), product, store)
            product[...] = dot(sources[pairs[1, i + 1]], stacked[...])
            close()

        store, close = finish(number - 1)
        mix(operator(number - 1), product, store)
        close()


def load_states(sizes, loads, raw, source):
    sectors, lines, size = raw.shape
    phys = lines // size
    tile = row_tile(size)
    columns = lax.broadcasted_iota(jnp.int32, (tile, size), 1)
    rows = lax.broadcasted_iota(jnp.int32, (tile, size), 0)
    for t in range(sectors):
        wait(loads[t * phys : (t + 1) * phys])

        @pl.loop(0, size // tile)
        def _(i):
            keep = (columns < sizes[t]) & (rows + i * tile < sizes[t])
            for r in range(phys):
                at = rows_at(r * size + i * tile, tile)
                put_split(source.at[t], at, jnp.where(keep, raw[t, at, :], 0))


def store_share(sizes, chip, core, raw, share):
    sectors, _, rows, lanes = share.shape
    size = raw.shape[2]
    half = size // 2
    phys = lanes // half
    columns = lax.broadcasted_iota(jnp.int32, (rows, half), 1)
    lines = lax.broadcasted_iota(jnp.int32, (rows, half), 0)
    for c in range(2):
        first = (2 * chip + (core ^ c)) * rows
        for side in range(2):

            @pl.when(core == side)
            def _():
                for t in range(sectors):
                    keep = (columns + side * half < sizes[t]) & (lines + first < sizes[t])
                    for r in range(phys):
                        x = raw[t, rows_at(r * size + first, rows), side * half : (side + 1) * half]
                        share[t, c, :, r * half : (r + 1) * half] = jnp.where(keep, x, 0)


def near_kernel(
    first_call, phys, info, ints, floats, *refs,
):
    if first_call:
        psi, left, right, total, share, source = refs[:6]
        stacked, tall, product, mixed, pairs, raw, sems = refs[6:]
    else:
        source, left, right, base, total = refs[:5]
        stacked, tall, product, mixed, pairs = refs[5:]
    chip, core = info[0], info[1]
    sectors, size = left.shape[1], left.shape[2]
    count = left.shape[0]
    half = size // 2
    charges, operators, sizes, _ = unpack(ints, floats, sectors, count, phys)
    if first_call:
        loads = []
        for t in range(sectors):
            loads += load_blocks(psi.at[t], raw.at[t], size, sems.at[t])
        start(loads)

    number = 0
    for w in range(count):
        for t in range(sectors):
            at = t - charges[w]
            inside = (at >= 0) & (at < sectors)
            pairs[0, number] = w
            pairs[1, number] = jnp.clip(at, 0, sectors - 1)
            pairs[2, number] = t
            number = number + inside.astype(jnp.int32)

    if first_call:
        load_states(sizes, loads, raw, source)
        store_share(sizes, chip, core, raw, share)
        total[...] = jnp.zeros_like(total)
    else:
        total[...] = base[...]

    def finish(i):
        w, t = pairs[0, i], pairs[2, i]

        def store(first, tile, p, a, b):
            cols = slice(p * half, (p + 1) * half)
            for place, value in enumerate((a, b, a)):
                mixed[place * size + first : place * size + first + tile, cols] = value

        def close():
            put_split(tall, slice(None), left[w, t])
            total[t] += dot(tall[...], mixed[...])

        return store, close

    def take(i):
        split_half(core, right.at[pairs[0, i], pairs[2, i]], stacked)

    run_pairs(number, phys, (operators,), pairs, source, take, product, stacked, finish)


def end_target(charge, sectors):
    return jnp.where(charge > 0, 0, sectors - 1)


def of_group(w, count, use):
    for group in range(2):

        @pl.when((w >= group * count) & (w < (group + 1) * count))
        def _():
            use(group, w - group * count)


def put_columns(core, src, stacked):
    half = src.shape[1] // 2
    for side in range(2):

        @pl.when(core == side)
        def _():
            put_split(stacked, slice(None), src[:, side * half : (side + 1) * half])


def far_kernel(
    last, chips, info, ints_a, ints_b, floats_a, floats_b, low, high, right_a, right_b, left_a,
    left_b, base, *refs,
):
    if last:
        many = chips * base.shape[0]
        outs = refs[:many]
        source, stacked, product, tall, mixed, pairs, total = refs[many:]
    else:
        total, source, stacked, product, tall, mixed, pairs = refs
    chip, core = info[0], info[1]
    part = 1 - core if last else core
    rights, lefts = (right_a, right_b), (left_a, left_b)
    lines = low.shape[0]
    half = stacked.shape[1]
    phys = lines // half
    count, sectors = left_a.shape[:2]
    views = [
        unpack(a, b, sectors, count, phys) for a, b in ((ints_a, floats_a), (ints_b, floats_b))
    ]
    charges, operators = [v[0] for v in views], [v[1] for v in views]
    number = 0
    for group in range(2):
        for w in range(count):
            charge = charges[group][w]
            pairs[0, number] = group * count + w
            pairs[1, number] = jnp.where(charge > 0, 0, 1)
            pairs[2, number] = end_target(charge, sectors)
            number = number + (charge != 0).astype(jnp.int32)
    tile = row_tile(lines)
    for side, halo in enumerate((low, high)):

        @pl.loop(0, lines // tile)
        def _(i):
            at = rows_at(i * tile, tile)
            put_split(source.at[side], at, halo[at, :])

    total[...] = base[...]

    def take(i):
        t = pairs[2, i]
        of_group(pairs[0, i], count, lambda g, w: split_half(core, rights[g].at[w, t], stacked))

    def finish(i):
        t = pairs[2, i]
        of_group(pairs[0, i], count, lambda g, w: put_columns(part, lefts[g].at[w, t], tall))

        def store(first, rows, p, a, b):
            cols = slice(p * half, (p + 1) * half)
            for place, value in enumerate((a, b, a)):
                mixed[place * half + first : place * half + first + rows, cols] = value

        def close():
            total[t] += dot(tall[...], mixed[...])

        return store, close

    run_pairs(number, phys, operators, pairs, source, take, product, stacked, finish)
    if last:
        rows = outs[0].shape[1]
        for j in range(chips):
            for c in range(2):
                first = (2 * (chip ^ j) + (core ^ c)) * rows
                for t in range(sectors):
                    outs[j * sectors + t][c] = total[t, rows_at(first, rows), :]


def send_kernel(info, ints, psi, up, down, sems):
    sectors, size, phys, _ = psi.shape
    half = size // 2
    sizes = Window(ints, 2, (sectors,))
    first = info[1] * half
    work = ((sectors - 1, up), (0, down))
    loads = [
        load_blocks(psi.at[t, rows_at(first, half)], out, half, sems.at[side])
        for side, (t, out) in enumerate(work)
    ]
    start(loads[0] + loads[1])
    tile = row_tile(half)
    columns = lax.broadcasted_iota(jnp.int32, (tile, size), 1)
    rows = lax.broadcasted_iota(jnp.int32, (tile, size), 0)
    for side, (t, out) in enumerate(work):
        wait(loads[side])

        @pl.loop(0, half // tile)
        def _(i):
            keep = (columns < sizes[t]) & (rows + (first + i * tile) < sizes[t])
            for r in range(phys):
                at = rows_at(r * half + i * tile, tile)
                out[at, :] = jnp.where(keep, out[at, :], 0)


def update_kernel(phys, terms, floats, *refs):
    parts, (state, scale, mine, other, sums) = refs[:-5], refs[-5:]
    sectors, _, rows, lanes = state.shape
    tile = row_tile(rows)
    values = [jnp.zeros((8, lanes), F32)] * 5
    energies = Window(floats, terms * phys * phys, (sectors,))
    count = len(parts) // sectors

    def fold(x):
        return jnp.sum(x.reshape(tile // 8, 8, lanes), axis=0)

    for t in range(sectors):
        for c in range(2):
            for first in range(0, rows, tile):
                at = (t, c, slice(first, first + tile), slice(None))
                s, k = state[at], scale[at]
                total = energies[t] * s
                for part in parts[t * count : (t + 1) * count]:
                    total = total + part[at[1:]]
                fixed = s - total * k
                slope = s * k
                (mine, other)[c][0, t, first : first + tile, :] = fixed
                (mine, other)[c][1, t, first : first + tile, :] = slope
                new = (s * total, s * s, fixed * fixed, fixed * slope, slope * slope)
                values = [v + fold(x) for v, x in zip(values, new)]
    column = lax.broadcasted_iota(jnp.int32, sums.shape, 1)
    result = jnp.zeros(sums.shape, F32)
    for i, v in enumerate(values):
        result = jnp.where(column == i, jnp.sum(v), result)
    sums[...] = result


def finish_kernel(numel, info, sums, mine, other, out, energies, whole, sems):
    core = info[1]
    column = lax.broadcasted_iota(jnp.int32, sums.shape, 1)
    values = [jnp.full((1, 128), jnp.sum(jnp.where(column == i, sums[...], 0)), F32) for i in range(5)]
    energy = values[0] / values[1]
    square = values[2] + 2 * energy * values[3] + energy * energy * values[4]
    factor = lax.rsqrt(jnp.maximum(square, 0) / numel + EPSILON)[0, 0]
    energy = energy[0, 0]
    energies[0] = energy
    _, sectors, rows, lanes = mine.shape
    phys = whole.shape[1]
    half = lanes // phys
    stores = []
    for t in range(sectors):
        for p in range(phys):
            cols = slice(p * half, (p + 1) * half)
            a = (mine[0, t, :, cols] + energy * mine[1, t, :, cols]) * factor
            b = (other[0, t, :, cols] + energy * other[1, t, :, cols]) * factor
            for side in range(2):

                @pl.when(core == side)
                def _():
                    whole[t, p, :, side * half : (side + 1) * half] = a
                    whole[t, p, :, (1 - side) * half : (2 - side) * half] = b

            copy = pltpu.make_async_copy(whole.at[t, p], out.at[t, :, p, :], sems.at[t, p])
            copy.start()
            stores.append(copy)
    wait(stores)


def swap_cores(x, count):
    return lax.ppermute(x, "term", [(i, i ^ 1) for i in range(count)])


def sum_chips(parts, count, backward):
    chips = len(parts)
    bits = [1 << i for i in range(chips.bit_length() - 1)]
    if backward:
        bits.reverse()
    parts = dict(enumerate(parts))
    arrived = [parts[0]]
    for step, bit in enumerate(bits):
        going = [j for j in parts if j & bit]
        later = sum(bits[step + 1 :])
        for j in sorted(going, key=lambda j: not (j & later)):
            part = lax.ppermute(parts.pop(j), "term", [(i, i ^ (2 * bit)) for i in range(count)])
            if j == bit:
                arrived.append(part)
            else:
                parts[j ^ bit] = parts[j ^ bit] + part
    return arrived


def body(
    psi, precond, left_environment_block, right_env, term_operators, term_charge, sector_sizes,
    sector_energy,
):
    sectors, size, phys, _ = psi.shape
    terms = term_charge.shape[0]
    count, planes = lax.axis_size("term"), lax.axis_size("sector")
    chips = count // 2
    rows = size // count
    half = size // 2
    lanes = phys * half
    numel = sectors * planes * size * phys * size
    me = lax.axis_index("term")
    chip, core = me // 2, me % 2
    info = jnp.concatenate([jnp.stack([chip, core]).astype(jnp.int32), sector_sizes, term_charge])
    ints_a = info
    floats_a = jnp.concatenate([term_operators.reshape(-1), sector_energy])

    positions = jnp.arange(size, dtype=jnp.int32)

    any_spec = pl.BlockSpec(memory_space=pl.ANY)
    smem = pl.BlockSpec(memory_space=pltpu.SMEM)
    vmem = pl.BlockSpec(memory_space=pltpu.VMEM)
    params = pltpu.CompilerParams(vmem_limit_bytes=VMEM_BYTES)

    edge = jax.ShapeDtypeStruct((phys * half, size), F32)
    up, down = pl.pallas_call(
        send_kernel,
        out_shape=[edge] * 2,
        in_specs=[smem] * 2 + [any_spec],
        out_specs=[vmem] * 2,
        scratch_shapes=[pltpu.SemaphoreType.DMA((2, phys))],
        compiler_params=pltpu.CompilerParams(vmem_limit_bytes=SEND_BYTES),
        name="send",
    )(info, ints_a, psi)
    forward = [(i, i + 1) for i in range(planes - 1)]
    backward = [(b, a) for a, b in forward]
    low_a = lax.ppermute(up, "sector", forward)
    high_a = lax.ppermute(down, "sector", backward)

    left_a, right_a = left_environment_block, right_env
    ints_b = swap_cores(ints_a, count)
    floats_b = swap_cores(floats_a, count)
    right_b = swap_cores(right_a, count)
    left_b = swap_cores(left_a, count)

    wide = jax.ShapeDtypeStruct((sectors, size, lanes), F32)
    block = jax.ShapeDtypeStruct((sectors, 2, rows, lanes), F32)
    piece = jax.ShapeDtypeStruct((2, rows, lanes), F32)
    pair_list = pltpu.SMEM((3, 2 * terms * sectors + 1), jnp.int32)
    splits = (sectors, phys * size, 3 * size)
    near_scratch = [
        pltpu.VMEM((3 * size, half), BF16),
        pltpu.VMEM((size, 3 * size), BF16),
        pltpu.VMEM((phys * size, half), F32),
        pltpu.VMEM((3 * size, lanes), BF16),
        pair_list,
    ]

    def cost(pairs):
        return pl.CostEstimate(
            flops=pairs * 3 * 4 * size * size * lanes, bytes_accessed=12 << 20, transcendentals=0
        )

    near, state, source = pl.pallas_call(
        functools.partial(near_kernel, True, phys),
        out_shape=[wide, block, jax.ShapeDtypeStruct(splits, BF16)],
        in_specs=[smem] * 3 + [any_spec] + [vmem] * 2,
        out_specs=[vmem] * 3,
        scratch_shapes=[
            *near_scratch,
            pltpu.VMEM((sectors, phys * size, size), F32),
            pltpu.SemaphoreType.DMA((sectors, phys)),
        ],
        compiler_params=params,
        cost_estimate=cost(terms * sectors),
        name="near_own",
    )(info, ints_a, floats_a, psi, left_a, right_a)
    near = pl.pallas_call(
        functools.partial(near_kernel, False, phys),
        out_shape=wide,
        in_specs=[smem] * 3 + [vmem] * 4,
        out_specs=vmem,
        scratch_shapes=near_scratch,
        compiler_params=params,
        cost_estimate=cost(terms * sectors),
        name="near_partner",
    )(info, ints_b, floats_b, source, left_b, right_b, near)

    low_a, high_a, near = lax.optimization_barrier((low_a, high_a, near))
    low_b = swap_cores(low_a, count)
    high_b = swap_cores(high_a, count)

    def far(last, low, high, base):
        return pl.pallas_call(
            functools.partial(far_kernel, last, chips),
            out_shape=[piece] * (chips * sectors) if last else wide,
            in_specs=[smem] * 5 + [vmem] * 7,
            out_specs=[vmem] * (chips * sectors) if last else vmem,
            scratch_shapes=[
                pltpu.VMEM((2, phys * half, 3 * size), BF16),
                pltpu.VMEM((3 * size, half), BF16),
                pltpu.VMEM((phys * half, half), F32),
                pltpu.VMEM((size, 3 * half), BF16),
                pltpu.VMEM((3 * half, lanes), BF16),
                pair_list,
            ]
            + [pltpu.VMEM((sectors, size, lanes), F32)] * last,
            compiler_params=params,
            cost_estimate=cost(terms // 2),
            name="far_last" if last else "far_first",
        )(
            info, ints_a, ints_b, floats_a, floats_b, low, high, right_a, right_b, left_a, left_b,
            base,
        )

    parts = far(True, low_b, high_b, far(False, low_a, high_a, near))

    *parts, precond, sector_sizes = lax.optimization_barrier((*parts, precond, sector_sizes))
    parts = [sum_chips(parts[t::sectors], count, t % 2 == 1) for t in range(sectors)]

    first = chip * 2 * rows
    inside = positions[None, :] < sector_sizes[:, None]
    scale = lax.dynamic_slice(
        precond, (0, first, 0, core * half), (sectors, 2 * rows, phys, half)
    ).astype(F32)
    a = lax.dynamic_slice(inside, (0, first), (sectors, 2 * rows))
    b = lax.dynamic_slice(inside, (0, core * half), (sectors, half))
    scale = jnp.where(a[:, :, None, None] & b[:, None, None, :], 1.0 / scale, 0)
    scale = scale.reshape(sectors, 2, rows, lanes)
    scale = jnp.where(core == 0, scale, scale[:, ::-1])

    devices = count * planes
    pair = jax.ShapeDtypeStruct((2, sectors, rows, lanes), F32)
    mine, other, sums = pl.pallas_call(
        functools.partial(update_kernel, phys, terms),
        out_shape=[pair, pair, jax.ShapeDtypeStruct((devices, 128), F32)],
        in_specs=[smem] + [vmem] * (sum(map(len, parts)) + 2),
        out_specs=[vmem] * 3,
        compiler_params=params,
        name="update",
    )(floats_a, *sum(parts, []), state, scale)
    other = swap_cores(other, count)
    sums = lax.all_to_all(sums, ("sector", "term"), 0, 0, tiled=True)
    return tuple(
        pl.pallas_call(
            functools.partial(finish_kernel, numel),
            out_shape=[
                jax.ShapeDtypeStruct((sectors, rows, phys, size), F32),
                jax.ShapeDtypeStruct((1,), F32),
            ],
            in_specs=[smem] + [vmem] * 3,
            out_specs=[any_spec, smem],
            scratch_shapes=[
                pltpu.VMEM((sectors, phys, rows, size), F32),
                pltpu.SemaphoreType.DMA((sectors, phys)),
            ],
            compiler_params=params,
            name="finish",
        )(info, sums, mine, other)
    )


def solution(mesh):
    in_specs = (
        P("sector", None, None, None),
        P("sector", None, None, None),
        P("term", "sector", None, None),
        P("term", "sector", None, None),
        P("term", None, None),
        P("term"),
        P("sector"),
        P("sector"),
    )
    out_specs = (P("sector", "term", None, None), P())
    return jax.shard_map(body, mesh=mesh, in_specs=in_specs, out_specs=out_specs, check_vma=False)
```

time: 125 us -> 106 us (0.85)
  waiting for transfers between devices: 20.6 us -> 10.5 us
  Pallas kernels: 52.2 us -> 44.9 us
  starting transfers between devices: 12 us -> 16.9 us
  other arithmetic: 10.8 us -> 6.14 us
  local copies, waits for them, and re-layouts: 13.7 us -> 11.4 us
    ppermute x5 -> x8, waiting for transfers between devices: 19.6 us -> 10.2 us  [the longest x6 10.2 us: sum_chips(): lax.ppermute(parts.pop(j), 'term', [(i, i ^ 2 * bit) for i in range(count)])]
    pallas_call x5 -> x6, Pallas kernels: 49.5 us -> 42.2 us  [the longest x2 14.3 us: far(): pl.pallas_call(functools.partial(far_kernel, last, chips), out_shape=[pie...]
    ppermute x5 -> x8, starting transfers between devices: 9.81 us -> 14.5 us  [the longest x6 8.19 us: sum_chips(): lax.ppermute(parts.pop(j), 'term', [(i, i ^ 2 * bit) for i in range(count)])]
    select_n x1 -> x0, other arithmetic: 3.55 us -> none  [edge(): return jnp.where(a & b, x, 0)]
    lt x2 -> x0, other arithmetic: 2.68 us -> none  [the longest x1 1.34 us: edge(): b = lax.broadcasted_iota(jnp.int32, x.shape, 2) < limit]
    concatenate x0 -> x2, other arithmetic: none -> 1.99 us  [the longest x1 1.26 us: body(): jnp.concatenate([jnp.stack([chip, core]).astype(jnp.int32), sector_sizes,...]
    add x0 -> x2, other arithmetic: none -> 1.51 us  [sum_chips(): parts[j ^ bit] = parts[j ^ bit] + part]
    slice x1 -> x0, local copies, waits for them, and re-layouts: 1.39 us -> none  [edge(): limit = sector_sizes[t]]
  transfers between devices with their start and end apart: 12 -> 15, of which waited for: 4 -> 3; matrix products, arithmetic and copies ran while one was open for 12% -> 8% of each run, Pallas kernels for 26% -> 28%
where the time goes in v3:
time: 106 us; the launch traced here: 105 us
  Pallas kernels  44.9 us (42%)
  starting transfers between devices  16.9 us (16%)
  blocking collectives  14.2 us (13%)
  local copies, waits for them, and re-layouts  11.4 us (11%)
  waiting for transfers between devices  10.5 us (10%)
  other arithmetic  6.14 us (6%)
    pallas_call x2, Pallas kernels, far(): pl.pallas_call(functools.partial(far_kernel, last, chips), out_shape=[pie...  14.3 us
    all_to_all x1, blocking collectives, body(): sums = lax.all_to_all(sums, ('sector', 'term'), 0, 0, tiled=True)  14.2 us
    pallas_call x1, Pallas kernels, body(): pl.pallas_call(functools.partial(near_kernel, True, phys), out_shape=[wid...  12.7 us
    ppermute x6, waiting for transfers between devices, sum_chips(): lax.ppermute(parts.pop(j), 'term', [(i, i ^ 2 * bit) for i in range(count)])  10.2 us
    pallas_call x1, Pallas kernels, body(): pl.pallas_call(functools.partial(near_kernel, False, phys), out_shape=wid...  10.1 us
    unnamed x22, local copies, waits for them, and re-layouts  9.6 us
    ppermute x6, starting transfers between devices, sum_chips(): lax.ppermute(parts.pop(j), 'term', [(i, i ^ 2 * bit) for i in range(count)])  8.19 us
    ppermute x1, starting transfers between devices, body(): low_a = lax.ppermute(up, 'sector', forward)  4.98 us
  transfers between devices with their start and end apart: 15, of which 3 were waited for; matrix products, arithmetic and copies ran while one was open for 8% of the time, Pallas kernels for 28%

profile of v3, /device:TPU:0, one launch (start us, length us, event | category | flops | bytes accessed | tf_op | source)
XLA Modules:
  0.0 105.2 jit_solution(11431393049167970355)
XLA Ops:
  0.6 0.5 collective-permute-start.4
  1.1 0.1 collective-permute-start.5
  1.2 1.3 %pad_add_fusion.info.ints.ints_a = s32[6]{0:T(128)} fusion(s32[2]{0:T(128)} %param.13, s32[2]{0:T(128)} %param.14, s32[1]{0:T(128)} %bitcast.1, s32[1]{0:T(128)} %bitcast), kind=kLoop, calls=%fused_computation.6 | loop fusion | flops 18 | bytes 48 | tf_op jit(solution)/shard_map/concatenate | solution.py:446
  2.5 0.0 copy-start.8
  2.5 4.1 %send.1 = (f32[768,384]{1,0:T(8,128)}, f32[768,384]{1,0:T(8,128)}) custom-call(s32[6]{0:T(128)} %pad_add_fusion.info.ints.ints_a, s32[6]{0:T(128)} %pad_add_fusion.info.ints.ints_a, f32[2,384,4,384]{3,2,1,0:T(4,128)} %refs_0_.1), custom_call_target="tpu_custom_call" | custom-call | tf_op jit(solution)/shard_map/send/pallas_call | solution.py:458
  6.6 5.0 %collective-permute-start.2 = (f32[768,384]{1,0:T(8,128)}, f32[768,384]{1,0:T(8,128)S(1)}, u32[]{:S(2)}, u32[]{:S(2)}) collective-permute-start(f32[768,384]{1,0:T(8,128)} %get-tuple-element.31), channel_id=1, source_target_pairs={{0,1},{1,2},{2,3},{4,5},{5,6},{6,7},{8,9},{9,10},{10,11},{12,13},{... | collective-permute-start | bytes 3538952 | tf_op jit(solution)/shard_map/ppermute | solution.py:469
  11.6 1.3 %collective-permute-start.3 = (f32[768,384]{1,0:T(8,128)}, f32[768,384]{1,0:T(8,128)}, u32[]{:S(2)}, u32[]{:S(2)}) collective-permute-start(f32[768,384]{1,0:T(8,128)} %get-tuple-element.32), channel_id=1, source_target_pairs={{1,0},{2,1},{3,2},{5,4},{6,5},{7,6},{9,8},{10,9},{11,10},{13,12},{... | collective-permute-start | bytes 3538952 | tf_op jit(solution)/shard_map/ppermute | solution.py:470
  12.9 0.0 copy-done.8
  12.9 0.1 collective-permute-start
  13.0 0.0 copy-done.9
  13.0 0.1 reshape.21
  13.1 0.7 pad_maximum_fusion.floats.floats_a
  13.8 0.3 collective-permute-done.ints.ints_b
  14.1 0.2 collective-permute-start.1
  14.3 0.0 copy-done
  14.3 1.7 %copy-done.1 = f32[2,2,384,384]{3,2,1,0:T(8,128)S(1)} copy-done((f32[2,2,384,384]{3,2,1,0:T(8,128)S(1)}, f32[2,2,384,384]{3,2,1,0:T(8,128)}, u32[]{:S(2)}) %copy-start.1) | copy-done | bytes 2359320
  16.0 2.3 %copy-done.3 = f32[2,384,4,384]{3,2,1,0:T(4,128)S(1)} copy-done((f32[2,384,4,384]{3,2,1,0:T(4,128)S(1)}, f32[2,384,4,384]{3,2,1,0:T(4,128)}, u32[]{:S(2)}) %copy-start.3) | copy-done | bytes 4718616
  18.3 12.7 %near_own.1 = (f32[2,384,768]{2,1,0:T(8,128)S(1)}, f32[2,2,48,768]{3,2,1,0:T(8,128)S(1)}, bf16[2,1536,1152]{2,1,0:T(8,128)(2,1)S(1)}) custom-call(s32[6]{0:T(128)S(1)} %copy-done.8, s32[6]{0:T(128)S(1)} %copy-done.8, f32[34]{0:T(128)S(1)} %pad_maximum_fusion.floats.floats_a, f32[2,384,4,384]{3,2,1,0:T(4,128)S(1)} %copy-done.3, ...), custom_call_target="tpu_custom_call" | custom-call | flops 5435817984 | bytes 12582912 | tf_op jit(solution)/shard_map/near_own/pallas_call | solution.py:496
  31.0 0.0 copy-start.6
  31.0 0.8 copy-done.6
  31.8 0.0 collective-permute-done.1.floats.floats_b
  31.8 0.0 collective-permute-done.4.refs_1_.left_b
  31.8 0.0 collective-permute-done.5.refs_2_.right_b
  31.8 10.1 %near_partner.1.base = f32[2,384,768]{2,1,0:T(8,128)S(1)} custom-call(s32[6]{0:T(128)S(1)} %copy-done.8, s32[6]{0:T(128)S(1)} %collective-permute-done.ints.ints_b, f32[34]{0:T(128)S(1)} %collective-permute-done.1.floats.floats_b, bf16[2,1536,1152]{2,1,0:T(8,128)(2,1)S(1)} %get-tuple-element.33.refs_0_, ...), custom_call_target="tpu_custom_call" | custom-call | flops 5435817984 | bytes 12582912 | tf_op jit(solution)/shard_map/near_partner/pallas_call | solution.py:510
  42.0 0.0 copy-start.4
  42.0 1.4 %copy-done.4 = f32[2,384,768]{2,1,0:T(8,128)} copy-done((f32[2,384,768]{2,1,0:T(8,128)}, f32[2,384,768]{2,1,0:T(8,128)S(1)}, u32[]{:S(2)}) %copy-start.4) | copy-done | bytes 2359320
  43.4 0.0 collective-permute-done.2.low
  43.4 0.0 collective-permute-done.3.high
  43.4 1.3 %collective-permute-start.6 = (f32[768,384]{1,0:T(8,128)S(1)}, f32[768,384]{1,0:T(8,128)}, u32[]{:S(2)}, u32[]{:S(2)}) collective-permute-start(f32[768,384]{1,0:T(8,128)S(1)} %collective-permute-done.2.low), channel_id=1, source_target_pairs={{0,4},{4,0},{8,12},{12,8},{16,20},{20,16},{24,28},{28,24},{1,5},{5... | collective-permute-start | bytes 3538952 | tf_op jit(solution)/shard_map/ppermute | solution.py:410
  44.7 0.1 collective-permute-start.7
  44.7 1.7 %copy-done.2 = f32[2,2,384,384]{3,2,1,0:T(8,128)S(1)} copy-done((f32[2,2,384,384]{3,2,1,0:T(8,128)S(1)}, f32[2,2,384,384]{3,2,1,0:T(8,128)}, u32[]{:S(2)}) %copy-start.2) | copy-done | bytes 2359320
  46.4 1.7 %copy-done.5 = f32[2,384,768]{2,1,0:T(8,128)S(1)} copy-done((f32[2,384,768]{2,1,0:T(8,128)S(1)}, f32[2,384,768]{2,1,0:T(8,128)}, u32[]{:S(2)}) %copy-start.5) | copy-done | bytes 2359320
  48.1 6.7 %far_first.1.base = f32[2,384,768]{2,1,0:T(8,128)S(1)} custom-call(s32[6]{0:T(128)S(1)} %copy-done.8, s32[6]{0:T(128)S(1)} %copy-done.8, s32[6]{0:T(128)S(1)} %collective-permute-done.ints.ints_b, f32[34]{0:T(128)S(1)} %pad_maximum_fusion.floats.floats_a, f32[34]{0:T(128)S(1)} %collective-permute-done.1.floats.floats_b, ...), custom_call_target="tpu_custom_call" | custom-call | flops 1358954496 | bytes 12582912 | tf_op jit(solution)/shard_map/far_first/pallas_call | solution.py:526
  54.8 0.0 copy-start.10
  54.8 0.0 collective-permute-done.6.low
  54.8 0.0 collective-permute-done.7.high
  54.8 7.6 %far_last.1 = (f32[2,48,768]{2,1,0:T(8,128)S(1)}, f32[2,48,768]{2,1,0:T(8,128)S(1)}, f32[2,48,768]{2,1,0:T(8,128)S(1)}, f32[2,48,768]{2,1,0:T(8,128)S(1)}, f32[2...) custom-call(s32[6]{0:T(128)S(1)} %copy-done.8, ...), custom_call_target="tpu_custom_call" | custom-call | flops 1358954496 | bytes 12582912 | tf_op jit(solution)/shard_map/far_last/pallas_call | solution.py:526
  62.4 0.0 copy-done.10
  62.4 0.1 iota_compare_fusion
  62.5 1.5 %collective-permute-start.12 = (f32[2,48,768]{2,1,0:T(8,128)S(1)}, f32[2,48,768]{2,1,0:T(8,128)S(1)}, u32[]{:S(2)}, u32[]{:S(2)}) collective-permute-start(f32[2,48,768]{2,1,0:T(8,128)S(1)} %get-tuple-element.53), channel_id=1, source_target_pairs={{0,16},{4,20},{8,24},{12,28},{16,0},{20,4},{24,8},{28,12},{1,17},{... | collective-permute-start | bytes 884744 | tf_op jit(solution)/shard_map/ppermute | solution.py:424
  64.0 2.3 %collective-permute-start.9 = (f32[2,48,768]{2,1,0:T(8,128)S(1)}, f32[2,48,768]{2,1,0:T(8,128)S(1)}, u32[]{:S(2)}, u32[]{:S(2)}) collective-permute-start(f32[2,48,768]{2,1,0:T(8,128)S(1)} %get-tuple-element.49), channel_id=1, source_target_pairs={{0,8},{4,12},{8,0},{12,4},{16,24},{20,28},{24,16},{28,20},{1,9},{5... | collective-permute-start | bytes 884744 | tf_op jit(solution)/shard_map/ppermute | solution.py:424
  66.4 0.5 collective-permute-start.11
  66.9 0.0 collective-permute-start.8
  66.9 0.1 constant_dynamic-slice_fusion
  66.9 0.1 constant_dynamic-slice_fusion.1
  67.0 0.1 broadcast_and_fusion
  67.1 5.2 %collective-permute-done.12 = f32[2,48,768]{2,1,0:T(8,128)S(1)} collective-permute-done((f32[2,48,768]{2,1,0:T(8,128)S(1)}, f32[2,48,768]{2,1,0:T(8,128)S(1)}, u32[]{:S(2)}, u32[]{:S(2)}) %collective-permute-start.12) | collective-permute-done | bytes 294944 | tf_op jit(solution)/shard_map/ppermute | solution.py:424
  72.4 0.7 add.21
  73.1 2.3 %collective-permute-start.13 = (f32[2,48,768]{2,1,0:T(8,128)}, f32[2,48,768]{2,1,0:T(8,128)S(1)}, u32[]{:S(2)}, u32[]{:S(2)}) collective-permute-start(f32[2,48,768]{2,1,0:T(8,128)} %add.21), channel_id=1, source_target_pairs={{0,8},{4,12},{8,0},{12,4},{16,24},{20,28},{24,16},{28,20},{1,9},{5... | collective-permute-start | bytes 884744 | tf_op jit(solution)/shard_map/ppermute | solution.py:424
  75.4 0.0 collective-permute-done.9
  75.4 0.8 add.20
  76.2 1.5 %collective-permute-start.10 = (f32[2,48,768]{2,1,0:T(8,128)}, f32[2,48,768]{2,1,0:T(8,128)S(1)}, u32[]{:S(2)}, u32[]{:S(2)}) collective-permute-start(f32[2,48,768]{2,1,0:T(8,128)} %add.20), channel_id=1, source_target_pairs={{0,16},{4,20},{8,24},{12,28},{16,0},{20,4},{24,8},{28,12},{1,17},{... | collective-permute-start | bytes 884744 | tf_op jit(solution)/shard_map/ppermute | solution.py:424
  77.7 2.4 %divide_select_fusion = f32[2,96,4,192]{3,2,1,0:T(4,128)} fusion(bf16[2,384,4,384]{3,2,1,0:T(4,128)(2,1)} %param.9, s32[]{:T(128)S(6)} %select_n.34, s32[]{:T(128)S(6)} %select_n.35, pred[2,96,192]{2,1,0:T(8,128)(4,1)S(1)} %broadcast_and_fusion), kind=kLoop, calls=%fused_computation.1 | loop fusion | flops 442368 | bytes 921608 | tf_op jit(solution)/shard_map/jit(_where)/select_n | solution.py:560
  80.1 1.6 %reshape.22 = f32[2,2,48,768]{3,2,1,0:T(8,128)S(1)} reshape(f32[2,96,4,192]{3,2,1,0:T(4,128)} %divide_select_fusion) | data formatting | bytes 1179648 | tf_op jit(solution)/shard_map/reshape | solution.py:561
  81.8 0.0 collective-permute-done.11.refs_4_
  81.8 0.0 collective-permute-done.8.refs_1_
  81.8 5.0 %collective-permute-done.13.refs_5_ = f32[2,48,768]{2,1,0:T(8,128)S(1)} collective-permute-done((f32[2,48,768]{2,1,0:T(8,128)}, f32[2,48,768]{2,1,0:T(8,128)S(1)}, u32[]{:S(2)}, u32[]{:S(2)}) %collective-permute-start.13) | collective-permute-done | bytes 294944 | tf_op jit(solution)/shard_map/ppermute | solution.py:424
  86.8 0.0 collective-permute-done.10.refs_2_
  86.8 0.0 copy-done.7
  86.8 1.1 %update.1 = (f32[2,2,48,768]{3,2,1,0:T(8,128)S(1)}, f32[2,2,48,768]{3,2,1,0:T(8,128)S(1)}, f32[32,128]{1,0:T(8,128)S(1)}) custom-call(f32[34]{0:T(128)S(1)} %pad_maximum_fusion.floats.floats_a, f32[2,48,768]{2,1,0:T(8,128)S(1)} %get-tuple-element.46.refs_0_, f32[2,48,768]{2,1,0:T(8,128)S(1)} %collective-permute-done.8.refs_1_, ...), custom_call_target="tpu_custom_call" | custom-call | tf_op jit(solution)/shard_map/update/pallas_call | solution.py:566
  87.9 0.2 collective-permute-start.14
  88.1 14.2 %all_to_all.11 = f32[32,1,128]{2,1,0:T(1,128)S(1)} all-to-all(f32[32,1,128]{2,1,0:T(1,128)S(1)} %bitcast.7), channel_id=1, replica_groups=mesh['term'=8,'sector'=4] {'sector','term'}, dimensions={0} | all-to-all | bytes 32768 | tf_op jit(solution)/shard_map/all_to_all | solution.py:575
  102.3 0.0 collective-permute-done.14.other
  102.3 2.7 %finish.1 = (f32[2,48,4,384]{3,2,1,0:T(4,128)}, f32[1]{0:T(128)}) custom-call(s32[6]{0:T(128)S(1)} %copy-done.8, f32[32,128]{1,0:T(8,128)S(1)} %bitcast.6, f32[2,2,48,768]{3,2,1,0:T(8,128)S(1)} %get-tuple-element.58.mine, f32[2,2,48,768]{3,2,1,0:T(8,128)S(1)} %collective-permute-done.14.other), custom_call_target="tpu_custom_call" | custom-call | tf_op jit(solution)/shard_map/finish/pallas_call | solution.py:577
  (8 shorter events, 0.1 us)
Async XLA Ops:
  0.6 31.2 %collective-permute-start.4 = (f32[2,2,384,384]{3,2,1,0:T(8,128)}, f32[2,2,384,384]{3,2,1,0:T(8,128)}, u32[]{:S(2)}, u32[]{:S(2)}) collective-permute-start(f32[2,2,384,384]{3,2,1,0:T(8,128)} %left_a.3), channel_id=1, source_target_pairs={{0,4},{4,0},{8,12},{12,8},{16,20},{20,16},{24,28},{28,24},{1,5},{5... | collective-permute-start | bytes 7077896 | tf_op jit(solution)/shard_map/ppermute | solution.py:410
  1.1 30.7 %collective-permute-start.5 = (f32[2,2,384,384]{3,2,1,0:T(8,128)}, f32[2,2,384,384]{3,2,1,0:T(8,128)}, u32[]{:S(2)}, u32[]{:S(2)}) collective-permute-start(f32[2,2,384,384]{3,2,1,0:T(8,128)} %right_a.3), channel_id=1, source_target_pairs={{0,4},{4,0},{8,12},{12,8},{16,20},{20,16},{24,28},{28,24},{1,5},{5... | collective-permute-start | bytes 7077896 | tf_op jit(solution)/shard_map/ppermute | solution.py:410
  2.5 10.4 %copy-start.8 = (s32[6]{0:T(128)S(1)}, s32[6]{0:T(128)}, u32[]{:S(2)}) copy-start(s32[6]{0:T(128)} %pad_add_fusion.info.ints.ints_a) | copy-start | bytes 76
  2.5 10.5 %copy-start.9 = (f32[2,4,4]{2,1,0:T(4,128)S(1)}, f32[2,4,4]{2,1,0:T(4,128)}, u32[]{:S(2)}) copy-start(f32[2,4,4]{2,1,0:T(4,128)} %param.12) | copy-start | bytes 388
  2.5 11.8 %copy-start = (f32[2,2,384,384]{3,2,1,0:T(8,128)S(1)}, f32[2,2,384,384]{3,2,1,0:T(8,128)}, u32[]{:S(2)}) copy-start(f32[2,2,384,384]{3,2,1,0:T(8,128)} %right_a.3) | copy-start | bytes 7077892
  6.6 36.8 %collective-permute-start.2 = (f32[768,384]{1,0:T(8,128)}, f32[768,384]{1,0:T(8,128)S(1)}, u32[]{:S(2)}, u32[]{:S(2)}) collective-permute-start(f32[768,384]{1,0:T(8,128)} %get-tuple-element.31), channel_id=1, source_target_pairs={{0,1},{1,2},{2,3},{4,5},{5,6},{6,7},{8,9},{9,10},{10,11},{12,13},{... | collective-permute-start | bytes 3538952 | tf_op jit(solution)/shard_map/ppermute | solution.py:469
  11.6 31.8 %collective-permute-start.3 = (f32[768,384]{1,0:T(8,128)}, f32[768,384]{1,0:T(8,128)}, u32[]{:S(2)}, u32[]{:S(2)}) collective-permute-start(f32[768,384]{1,0:T(8,128)} %get-tuple-element.32), channel_id=1, source_target_pairs={{1,0},{2,1},{3,2},{5,4},{6,5},{7,6},{9,8},{10,9},{11,10},{13,12},{... | collective-permute-start | bytes 3538952 | tf_op jit(solution)/shard_map/ppermute | solution.py:470
  12.9 1.2 %collective-permute-start = (s32[6]{0:T(128)S(1)}, s32[6]{0:T(128)S(1)}, u32[]{:S(2)}, u32[]{:S(2)}) collective-permute-start(s32[6]{0:T(128)S(1)} %copy-done.8), channel_id=1, source_target_pairs={{0,4},{4,0},{8,12},{12,8},{16,20},{20,16},{24,28},{28,24},{1,5},{5... | collective-permute-start | bytes 80 | tf_op jit(solution)/shard_map/ppermute | solution.py:410
  14.1 17.7 %collective-permute-start.1 = (f32[34]{0:T(128)S(1)}, f32[34]{0:T(128)S(1)}, u32[]{:S(2)}, u32[]{:S(2)}) collective-permute-start(f32[34]{0:T(128)S(1)} %pad_maximum_fusion.floats.floats_a), channel_id=1, source_target_pairs={{0,4},{4,0},{8,12},{12,8},{16,20},{20,16},{24,28},{28,24},{1,5},{5... | collective-permute-start | bytes 416 | tf_op jit(solution)/shard_map/ppermute | solution.py:410
  14.3 1.7 %copy-start.1 = (f32[2,2,384,384]{3,2,1,0:T(8,128)S(1)}, f32[2,2,384,384]{3,2,1,0:T(8,128)}, u32[]{:S(2)}) copy-start(f32[2,2,384,384]{3,2,1,0:T(8,128)} %left_a.3) | copy-start | bytes 7077892
  16.0 2.3 %copy-start.3 = (f32[2,384,4,384]{3,2,1,0:T(4,128)S(1)}, f32[2,384,4,384]{3,2,1,0:T(4,128)}, u32[]{:S(2)}) copy-start(f32[2,384,4,384]{3,2,1,0:T(4,128)} %refs_0_.1) | copy-start | bytes 14155780
  31.0 0.8 copy-start.6
  42.0 1.4 %copy-start.4 = (f32[2,384,768]{2,1,0:T(8,128)}, f32[2,384,768]{2,1,0:T(8,128)S(1)}, u32[]{:S(2)}) copy-start(f32[2,384,768]{2,1,0:T(8,128)S(1)} %near_partner.1.base) | copy-start | bytes 7077892
  43.4 11.4 %collective-permute-start.6 = (f32[768,384]{1,0:T(8,128)S(1)}, f32[768,384]{1,0:T(8,128)}, u32[]{:S(2)}, u32[]{:S(2)}) collective-permute-start(f32[768,384]{1,0:T(8,128)S(1)} %collective-permute-done.2.low), channel_id=1, source_target_pairs={{0,4},{4,0},{8,12},{12,8},{16,20},{20,16},{24,28},{28,24},{1,5},{5... | collective-permute-start | bytes 3538952 | tf_op jit(solution)/shard_map/ppermute | solution.py:410
  44.7 10.1 %collective-permute-start.7 = (f32[768,384]{1,0:T(8,128)}, f32[768,384]{1,0:T(8,128)}, u32[]{:S(2)}, u32[]{:S(2)}) collective-permute-start(f32[768,384]{1,0:T(8,128)} %collective-permute-done.3.high), channel_id=1, source_target_pairs={{0,4},{4,0},{8,12},{12,8},{16,20},{20,16},{24,28},{28,24},{1,5},{5... | collective-permute-start | bytes 3538952 | tf_op jit(solution)/shard_map/ppermute | solution.py:410
  44.7 1.7 %copy-start.2 = (f32[2,2,384,384]{3,2,1,0:T(8,128)S(1)}, f32[2,2,384,384]{3,2,1,0:T(8,128)}, u32[]{:S(2)}) copy-start(f32[2,2,384,384]{3,2,1,0:T(8,128)} %left_a.3) | copy-start | bytes 7077892
  46.4 1.7 %copy-start.5 = (f32[2,384,768]{2,1,0:T(8,128)S(1)}, f32[2,384,768]{2,1,0:T(8,128)}, u32[]{:S(2)}) copy-start(f32[2,384,768]{2,1,0:T(8,128)} %copy-done.4) | copy-start | bytes 7077892
  54.8 7.6 %copy-start.10 = (s32[2]{0:T(128)S(1)}, s32[2]{0:T(128)}, u32[]{:S(2)}) copy-start(s32[2]{0:T(128)} %param.14) | copy-start | bytes 28
  62.5 9.9 %collective-permute-start.12 = (f32[2,48,768]{2,1,0:T(8,128)S(1)}, f32[2,48,768]{2,1,0:T(8,128)S(1)}, u32[]{:S(2)}, u32[]{:S(2)}) collective-permute-start(f32[2,48,768]{2,1,0:T(8,128)S(1)} %get-tuple-element.53), channel_id=1, source_target_pairs={{0,16},{4,20},{8,24},{12,28},{16,0},{20,4},{24,8},{28,12},{1,17},{... | collective-permute-start | bytes 884744 | tf_op jit(solution)/shard_map/ppermute | solution.py:424
  64.0 11.4 %collective-permute-start.9 = (f32[2,48,768]{2,1,0:T(8,128)S(1)}, f32[2,48,768]{2,1,0:T(8,128)S(1)}, u32[]{:S(2)}, u32[]{:S(2)}) collective-permute-start(f32[2,48,768]{2,1,0:T(8,128)S(1)} %get-tuple-element.49), channel_id=1, source_target_pairs={{0,8},{4,12},{8,0},{12,4},{16,24},{20,28},{24,16},{28,20},{1,9},{5... | collective-permute-start | bytes 884744 | tf_op jit(solution)/shard_map/ppermute | solution.py:424
  66.4 15.4 %collective-permute-start.11 = (f32[2,48,768]{2,1,0:T(8,128)S(1)}, f32[2,48,768]{2,1,0:T(8,128)S(1)}, u32[]{:S(2)}, u32[]{:S(2)}) collective-permute-start(f32[2,48,768]{2,1,0:T(8,128)S(1)} %get-tuple-element.51), channel_id=1, source_target_pairs={{0,16},{4,20},{8,24},{12,28},{16,0},{20,4},{24,8},{28,12},{1,17},{... | collective-permute-start | bytes 884744 | tf_op jit(solution)/shard_map/ppermute | solution.py:424
  66.9 14.9 %collective-permute-start.8 = (f32[2,48,768]{2,1,0:T(8,128)S(1)}, f32[2,48,768]{2,1,0:T(8,128)S(1)}, u32[]{:S(2)}, u32[]{:S(2)}) collective-permute-start(f32[2,48,768]{2,1,0:T(8,128)S(1)} %get-tuple-element.47), channel_id=1, source_target_pairs={{0,8},{4,12},{8,0},{12,4},{16,24},{20,28},{24,16},{28,20},{1,9},{5... | collective-permute-start | bytes 884744 | tf_op jit(solution)/shard_map/ppermute | solution.py:424
  73.1 13.7 %copy-start.7 = (f32[2,2,48,768]{3,2,1,0:T(8,128)S(1)}, f32[2,2,48,768]{3,2,1,0:T(8,128)}, u32[]{:S(2)}) copy-start(f32[2,2,48,768]{3,2,1,0:T(8,128)} %copy-done.6) | copy-start | bytes 1769476
  73.1 13.7 %collective-permute-start.13 = (f32[2,48,768]{2,1,0:T(8,128)}, f32[2,48,768]{2,1,0:T(8,128)S(1)}, u32[]{:S(2)}, u32[]{:S(2)}) collective-permute-start(f32[2,48,768]{2,1,0:T(8,128)} %add.21), channel_id=1, source_target_pairs={{0,8},{4,12},{8,0},{12,4},{16,24},{20,28},{24,16},{28,20},{1,9},{5... | collective-permute-start | bytes 884744 | tf_op jit(solution)/shard_map/ppermute | solution.py:424
  76.2 10.6 %collective-permute-start.10 = (f32[2,48,768]{2,1,0:T(8,128)}, f32[2,48,768]{2,1,0:T(8,128)S(1)}, u32[]{:S(2)}, u32[]{:S(2)}) collective-permute-start(f32[2,48,768]{2,1,0:T(8,128)} %add.20), channel_id=1, source_target_pairs={{0,16},{4,20},{8,24},{12,28},{16,0},{20,4},{24,8},{28,12},{1,17},{... | collective-permute-start | bytes 884744 | tf_op jit(solution)/shard_map/ppermute | solution.py:424
  87.9 14.4 %collective-permute-start.14 = (f32[2,2,48,768]{3,2,1,0:T(8,128)S(1)}, f32[2,2,48,768]{3,2,1,0:T(8,128)S(1)}, u32[]{:S(2)}, u32[]{:S(2)}) collective-permute-start(f32[2,2,48,768]{3,2,1,0:T(8,128)S(1)} %get-tuple-element.59), channel_id=1, source_target_pairs={{0,4},{4,0},{8,12},{12,8},{16,20},{20,16},{24,28},{28,24},{1,5},{5... | collective-permute-start | bytes 1769480 | tf_op jit(solution)/shard_map/ppermute | solution.py:410

commit v4 on v3

--- a/solution.py
+++ b/solution.py
@@ -318,11 +318,10 @@
                     outs[j * sectors + t][c] = total[t, rows_at(first, rows), :]
 
 
-def send_kernel(info, ints, psi, up, down, sems):
+def send_kernel(sizes, psi, up, down, sems):
     sectors, size, phys, _ = psi.shape
     half = size // 2
-    sizes = Window(ints, 2, (sectors,))
-    first = info[1] * half
+    first = lax.rem(lax.axis_index("term"), 2) * half
     work = ((sectors - 1, up), (0, down))
     loads = [
         load_blocks(psi.at[t, rows_at(first, half)], out, half, sems.at[side])
@@ -458,12 +457,15 @@
     up, down = pl.pallas_call(
         send_kernel,
         out_shape=[edge] * 2,
-        in_specs=[smem] * 2 + [any_spec],
+        in_specs=[smem, any_spec],
         out_specs=[vmem] * 2,
         scratch_shapes=[pltpu.SemaphoreType.DMA((2, phys))],
         compiler_params=pltpu.CompilerParams(vmem_limit_bytes=SEND_BYTES),
         name="send",
-    )(info, ints_a, psi)
+    )(sector_sizes, psi)
+    up, down, left_late, right_late = lax.optimization_barrier(
+        (up, down, left_environment_block, right_env)
+    )
     forward = [(i, i + 1) for i in range(planes - 1)]
     backward = [(b, a) for a, b in forward]
     low_a = lax.ppermute(up, "sector", forward)
@@ -472,8 +474,8 @@
     left_a, right_a = left_environment_block, right_env
     ints_b = swap_cores(ints_a, count)
     floats_b = swap_cores(floats_a, count)
-    right_b = swap_cores(right_a, count)
-    left_b = swap_cores(left_a, count)
+    right_b = swap_cores(right_late, count)
+    left_b = swap_cores(left_late, count)
 
     wide = jax.ShapeDtypeStruct((sectors, size, lanes), F32)
     block = jax.ShapeDtypeStruct((sectors, 2, rows, lanes), F32)
@@ -548,7 +550,6 @@
     parts = far(True, low_b, high_b, far(False, low_a, high_a, near))
 
     *parts, precond, sector_sizes = lax.optimization_barrier((*parts, precond, sector_sizes))
-    parts = [sum_chips(parts[t::sectors], count, t % 2 == 1) for t in range(sectors)]
 
     first = chip * 2 * rows
     inside = positions[None, :] < sector_sizes[:, None]
@@ -560,6 +561,13 @@
     scale = jnp.where(a[:, :, None, None] & b[:, None, None, :], 1.0 / scale, 0)
     scale = scale.reshape(sectors, 2, rows, lanes)
     scale = jnp.where(core == 0, scale, scale[:, ::-1])
+
+    if chips > 1:
+        direct = [(chips // 2 if t % 2 else 1) * sectors + t for t in range(sectors)]
+        *late, scale = lax.optimization_barrier((*(parts[i] for i in direct), scale))
+        for i, part in zip(direct, late):
+            parts[i] = part
+    parts = [sum_chips(parts[t::sectors], count, t % 2 == 1) for t in range(sectors)]
 
     devices = count * planes
     pair = jax.ShapeDtypeStruct((2, sectors, rows, lanes), F32)

time: 106 us -> 107 us (level); the launches traced: 105 us -> 107 us
  starting transfers between devices: 16.9 us -> 13 us
  Pallas kernels: 44.9 us -> 47.9 us
  waiting for transfers between devices: 10.5 us -> 13.1 us
  local copies, waits for them, and re-layouts: 11.4 us -> 13.1 us
  blocking collectives: 14.2 us -> 13 us
    pallas_call x2, Pallas kernels: 14.3 us -> 21.7 us  [far(): pl.pallas_call(functools.partial(far_kernel, last, chips), out_shape=[pie...]
    ppermute x6, starting transfers between devices: 8.19 us -> 5.1 us  [sum_chips(): lax.ppermute(parts.pop(j), 'term', [(i, i ^ 2 * bit) for i in range(count)])]
    pallas_call x1, Pallas kernels: 10.1 us -> 7.88 us  [body(): pl.pallas_call(functools.partial(near_kernel, False, phys), out_shape=wid...]
    pallas_call x1, Pallas kernels: 12.7 us -> 10.5 us  [body(): pl.pallas_call(functools.partial(near_kernel, True, phys), out_shape=[wid...]
    ppermute x1, waiting for transfers between devices: 0.01 us -> 1.96 us  [body(): high_a = lax.ppermute(down, 'sector', backward)]
    unnamed x22 -> x34, local copies, waits for them, and re-layouts: 9.6 us -> 11.1 us
    select_n x1, other arithmetic: 0.04 us -> 1.33 us  [body(): scale = jnp.where(core == 0, scale, scale[:, ::-1])]
    all_to_all x1, blocking collectives: 14.2 us -> 13 us  [body(): sums = lax.all_to_all(sums, ('sector', 'term'), 0, 0, tiled=True)]
  transfers between devices with their start and end apart: 15 -> 15, of which waited for: 3 -> 5; matrix products, arithmetic and copies ran while one was open for 8% -> 7% of each run, Pallas kernels for 28% -> 26%
where the time goes in v4:
time: 107 us
  Pallas kernels  47.9 us (45%)
  local copies, waits for them, and re-layouts  13.1 us (12%)
  waiting for transfers between devices  13.1 us (12%)
  starting transfers between devices  13 us (12%)
  blocking collectives  13 us (12%)
  other arithmetic  5.88 us (5%)
  between operations  1.11 us (1%)
    pallas_call x2, Pallas kernels, far(): pl.pallas_call(functools.partial(far_kernel, last, chips), out_shape=[pie...  21.7 us
    all_to_all x1, blocking collectives, body(): sums = lax.all_to_all(sums, ('sector', 'term'), 0, 0, tiled=True)  13 us
    ppermute x6, waiting for transfers between devices, sum_chips(): lax.ppermute(parts.pop(j), 'term', [(i, i ^ 2 * bit) for i in range(count)])  11.2 us
    unnamed x34, local copies, waits for them, and re-layouts  11.1 us
    pallas_call x1, Pallas kernels, body(): pl.pallas_call(functools.partial(near_kernel, True, phys), out_shape=[wid...  10.5 us
    pallas_call x1, Pallas kernels, body(): pl.pallas_call(functools.partial(near_kernel, False, phys), out_shape=wid...  7.88 us
    ppermute x6, starting transfers between devices, sum_chips(): lax.ppermute(parts.pop(j), 'term', [(i, i ^ 2 * bit) for i in range(count)])  5.1 us
    ppermute x1, starting transfers between devices, body(): low_a = lax.ppermute(up, 'sector', forward)  4.96 us
  transfers between devices with their start and end apart: 15, of which 5 were waited for; matrix products, arithmetic and copies ran while one was open for 7% of the time, Pallas kernels for 26%

profile of v4, /device:TPU:0, one launch (start us, length us, event | category | flops | bytes accessed | tf_op | source)
XLA Modules:
  0.0 107.2 jit_solution(1674515215432114877)
XLA Ops:
  0.6 0.0 copy-start.13
  0.6 0.0 copy-start
  0.7 0.0 copy-start.16
  0.7 4.1 %send.1 = (f32[768,384]{1,0:T(8,128)}, f32[768,384]{1,0:T(8,128)}) custom-call(s32[2]{0:T(128)} %sizes.1, f32[2,384,4,384]{3,2,1,0:T(4,128)} %refs_0_.1), custom_call_target="tpu_custom_call" | custom-call | tf_op jit(solution)/shard_map/send/pallas_call | solution.py:457
  4.8 0.5 collective-permute-start.4
  5.3 0.1 collective-permute-start.5
  5.4 5.0 %collective-permute-start.2 = (f32[768,384]{1,0:T(8,128)}, f32[768,384]{1,0:T(8,128)S(1)}, u32[]{:S(2)}, u32[]{:S(2)}) collective-permute-start(f32[768,384]{1,0:T(8,128)} %get-tuple-element.40), channel_id=1, source_target_pairs={{0,1},{1,2},{2,3},{4,5},{5,6},{6,7},{8,9},{9,10},{10,11},{12,13},{... | collective-permute-start | bytes 3538952 | tf_op jit(solution)/shard_map/ppermute | solution.py:471
  10.3 1.3 %collective-permute-start.3 = (f32[768,384]{1,0:T(8,128)}, f32[768,384]{1,0:T(8,128)}, u32[]{:S(2)}, u32[]{:S(2)}) collective-permute-start(f32[768,384]{1,0:T(8,128)} %get-tuple-element.41), channel_id=1, source_target_pairs={{1,0},{2,1},{3,2},{5,4},{6,5},{7,6},{9,8},{10,9},{11,10},{13,12},{... | collective-permute-start | bytes 3538952 | tf_op jit(solution)/shard_map/ppermute | solution.py:472
  11.7 0.1 pad_add_fusion.info.ints.ints_a
  11.8 0.0 collective-permute-start
  11.8 0.6 reshape.21
  12.4 0.7 pad_maximum_fusion.floats.floats_a
  13.1 0.0 collective-permute-done.ints.ints_b
  13.1 0.5 collective-permute-start.1
  13.6 1.7 %copy-done.1 = f32[2,2,384,384]{3,2,1,0:T(8,128)S(1)} copy-done((f32[2,2,384,384]{3,2,1,0:T(8,128)S(1)}, f32[2,2,384,384]{3,2,1,0:T(8,128)}, u32[]{:S(2)}) %copy-start.1) | copy-done | bytes 2359320
  15.3 2.3 %copy-done.4 = f32[2,384,4,384]{3,2,1,0:T(4,128)S(1)} copy-done((f32[2,384,4,384]{3,2,1,0:T(4,128)S(1)}, f32[2,384,4,384]{3,2,1,0:T(4,128)}, u32[]{:S(2)}) %copy-start.4) | copy-done | bytes 4718616
  17.6 10.5 %near_own.1 = (f32[2,384,768]{2,1,0:T(8,128)S(1)}, f32[2,2,48,768]{3,2,1,0:T(8,128)S(1)}, bf16[2,1536,1152]{2,1,0:T(8,128)(2,1)S(1)}) custom-call(s32[6]{0:T(128)S(1)} %pad_add_fusion.info.ints.ints_a, s32[6]{0:T(128)S(1)} %pad_add_fusion.info.ints.ints_a, f32[34]{0:T(128)S(1)} %pad_maximum_fusion.floats.floats_a, f32[2,384,4,384]{3,2,1,0:T(4,128)S(1)} %copy-done.4, ...), custom_call_target="tpu_custom_call" | custom-call | flops 5435817984 | bytes 12582912 | tf_op jit(solution)/shard_map/near_own/pallas_call | solution.py:498
  28.1 0.0 copy-start.7
  28.1 0.8 copy-done.7
  28.9 0.0 collective-permute-done.1.floats.floats_b
  28.9 0.0 collective-permute-done.4.refs_1_.left_b
  28.9 0.0 collective-permute-done.5.refs_2_.right_b
  28.9 7.9 %near_partner.1.base = f32[2,384,768]{2,1,0:T(8,128)S(1)} custom-call(s32[6]{0:T(128)S(1)} %pad_add_fusion.info.ints.ints_a, s32[6]{0:T(128)S(1)} %collective-permute-done.ints.ints_b, f32[34]{0:T(128)S(1)} %collective-permute-done.1.floats.floats_b, bf16[2,1536,1152]{2,1,0:T(8,128)(2,1)S(1)} %get-tuple-element.42.refs_0_, ...), custom_call_target="tpu_custom_call" | custom-call | flops 5435817984 | bytes 12582912 | tf_op jit(solution)/shard_map/near_partner/pallas_call | solution.py:512
  36.8 1.4 %copy-done.5 = f32[2,384,768]{2,1,0:T(8,128)} copy-done((f32[2,384,768]{2,1,0:T(8,128)}, f32[2,384,768]{2,1,0:T(8,128)S(1)}, u32[]{:S(2)}) %copy-start.5) | copy-done | bytes 2359320
  38.3 0.0 collective-permute-done.2.low
  38.3 2.0 %collective-permute-done.3.high = f32[768,384]{1,0:T(8,128)} collective-permute-done((f32[768,384]{1,0:T(8,128)}, f32[768,384]{1,0:T(8,128)}, u32[]{:S(2)}, u32[]{:S(2)}) %collective-permute-start.3) | collective-permute-done | bytes 1179680 | tf_op jit(solution)/shard_map/ppermute | solution.py:472
  40.2 0.0 collective-permute-start.6
  40.2 0.5 collective-permute-start.7
  40.8 1.7 %copy-done.2 = f32[2,2,384,384]{3,2,1,0:T(8,128)S(1)} copy-done((f32[2,2,384,384]{3,2,1,0:T(8,128)S(1)}, f32[2,2,384,384]{3,2,1,0:T(8,128)}, u32[]{:S(2)}) %copy-start.2) | copy-done | bytes 2359320
  42.4 1.7 %copy-done.6 = f32[2,384,768]{2,1,0:T(8,128)S(1)} copy-done((f32[2,384,768]{2,1,0:T(8,128)S(1)}, f32[2,384,768]{2,1,0:T(8,128)}, u32[]{:S(2)}) %copy-start.6) | copy-done | bytes 2359320
  44.1 9.9 %far_first.1.base = f32[2,384,768]{2,1,0:T(8,128)S(1)} custom-call(s32[6]{0:T(128)S(1)} %pad_add_fusion.info.ints.ints_a, s32[6]{0:T(128)S(1)} %pad_add_fusion.info.ints.ints_a, s32[6]{0:T(128)S(1)} %collective-permute-done.ints.ints_b, f32[34]{0:T(128)S(1)} %pad_maximum_fusion.floats.floats_a, f32[34]{0:T(128)S(1)} %collective-permute-done.1.floats.floats_b, ...), custom_call_target="tpu_custom_call" | custom-call | flops 1358954496 | bytes 12582912 | tf_op jit(solution)/shard_map/far_first/pallas_call | solution.py:528
  54.0 0.0 copy-start.14
  54.1 0.0 collective-permute-done.6.low
  54.1 0.0 collective-permute-done.7.high
  54.1 11.8 %far_last.1 = (f32[2,48,768]{2,1,0:T(8,128)S(1)}, f32[2,48,768]{2,1,0:T(8,128)S(1)}, f32[2,48,768]{2,1,0:T(8,128)S(1)}, f32[2,48,768]{2,1,0:T(8,128)S(1)}, f32[2...) custom-call(s32[6]{0:T(128)S(1)} %pad_add_fusion.info.ints.ints_a, ...), custom_call_target="tpu_custom_call" | custom-call | flops 1358954496 | bytes 12582912 | tf_op jit(solution)/shard_map/far_last/pallas_call | solution.py:528
  65.8 0.7 copy-done.9
  66.6 0.7 copy-done.11
  67.3 0.1 iota_compare_fusion
  67.4 0.1 constant_dynamic-slice_fusion
  67.5 0.1 constant_dynamic-slice_fusion.1
  67.5 0.0 collective-permute-start.9
  67.6 0.4 collective-permute-start.12
  67.9 0.1 broadcast_and_fusion
  68.0 1.6 %divide_select_fusion = f32[2,96,4,192]{3,2,1,0:T(4,128)S(1)} fusion(bf16[2,384,4,384]{3,2,1,0:T(4,128)(2,1)} %param.9, s32[]{:T(128)S(6)} %select_n.34, s32[]{:T(128)S(6)} %select_n.35, pred[2,96,192]{2,1,0:T(8,128)(4,1)S(1)} %broadcast_and_fusion), kind=kLoop, calls=%fused_computation.1 | loop fusion | flops 442368 | bytes 921608 | tf_op jit(solution)/shard_map/jit(_where)/select_n | solution.py:561
  69.6 0.0 copy-start.8
  69.6 1.3 %reshape.22 = f32[2,2,48,768]{3,2,1,0:T(8,128)} reshape(f32[2,96,4,192]{3,2,1,0:T(4,128)S(1)} %divide_select_fusion) | data formatting | bytes 1179648 | tf_op jit(solution)/shard_map/reshape | solution.py:562
  70.9 1.3 %reverse_select_fusion.refs_7_ = f32[2,2,48,768]{3,2,1,0:T(8,128)S(1)} fusion(f32[2,2,48,768]{3,2,1,0:T(8,128)} %reshape.22, pred[]{:T(512)S(6)} %eq.5), kind=kLoop, calls=%fused_computation | loop fusion | flops 147456 | bytes 1179649 | tf_op jit(solution)/shard_map/jit(_where)/select_n | solution.py:563
  72.3 1.7 %collective-permute-start.8 = (f32[2,48,768]{2,1,0:T(8,128)S(1)}, f32[2,48,768]{2,1,0:T(8,128)S(1)}, u32[]{:S(2)}, u32[]{:S(2)}) collective-permute-start(f32[2,48,768]{2,1,0:T(8,128)S(1)} %copy-done.12), channel_id=1, source_target_pairs={{0,8},{4,12},{8,0},{12,4},{16,24},{20,28},{24,16},{28,20},{1,9},{5... | collective-permute-start | bytes 884744 | tf_op jit(solution)/shard_map/ppermute | solution.py:423
  74.0 2.0 %collective-permute-start.11 = (f32[2,48,768]{2,1,0:T(8,128)S(1)}, f32[2,48,768]{2,1,0:T(8,128)S(1)}, u32[]{:S(2)}, u32[]{:S(2)}) collective-permute-start(f32[2,48,768]{2,1,0:T(8,128)S(1)} %copy-done.10), channel_id=1, source_target_pairs={{0,16},{4,20},{8,24},{12,28},{16,0},{20,4},{24,8},{28,12},{1,17},{... | collective-permute-start | bytes 884744 | tf_op jit(solution)/shard_map/ppermute | solution.py:423
  76.0 1.8 %collective-permute-done.9 = f32[2,48,768]{2,1,0:T(8,128)} collective-permute-done((f32[2,48,768]{2,1,0:T(8,128)}, f32[2,48,768]{2,1,0:T(8,128)}, u32[]{:S(2)}, u32[]{:S(2)}) %collective-permute-start.9) | collective-permute-done | bytes 294944 | tf_op jit(solution)/shard_map/ppermute | solution.py:423
  77.7 1.0 add.22
  78.7 0.1 collective-permute-start.10
  78.8 0.0 collective-permute-done.12
  78.8 1.0 add.23
  79.8 0.9 collective-permute-start.13
  80.8 3.2 %collective-permute-done.8.refs_1_ = f32[2,48,768]{2,1,0:T(8,128)S(1)} collective-permute-done((f32[2,48,768]{2,1,0:T(8,128)S(1)}, f32[2,48,768]{2,1,0:T(8,128)S(1)}, u32[]{:S(2)}, u32[]{:S(2)}) %collective-permute-start.8) | collective-permute-done | bytes 294944 | tf_op jit(solution)/shard_map/ppermute | solution.py:423
  84.0 0.1 collective-permute-done.11.refs_4_
  84.0 6.1 %collective-permute-done.10.refs_2_ = f32[2,48,768]{2,1,0:T(8,128)S(1)} collective-permute-done((f32[2,48,768]{2,1,0:T(8,128)S(1)}, f32[2,48,768]{2,1,0:T(8,128)S(1)}, u32[]{:S(2)}, u32[]{:S(2)}) %collective-permute-start.10) | collective-permute-done | bytes 294944 | tf_op jit(solution)/shard_map/ppermute | solution.py:423
  90.2 0.0 collective-permute-done.13.refs_5_
  90.2 1.1 %update.1 = (f32[2,2,48,768]{3,2,1,0:T(8,128)S(1)}, f32[2,2,48,768]{3,2,1,0:T(8,128)S(1)}, f32[32,128]{1,0:T(8,128)S(1)}) custom-call(f32[34]{0:T(128)S(1)} %pad_maximum_fusion.floats.floats_a, f32[2,48,768]{2,1,0:T(8,128)S(1)} %get-tuple-element.57.refs_0_, f32[2,48,768]{2,1,0:T(8,128)S(1)} %collective-permute-done.8.refs_1_, ...), custom_call_target="tpu_custom_call" | custom-call | tf_op jit(solution)/shard_map/update/pallas_call | solution.py:574
  91.3 0.1 collective-permute-start.14
  91.3 13.0 %all_to_all.11 = f32[32,1,128]{2,1,0:T(1,128)S(1)} all-to-all(f32[32,1,128]{2,1,0:T(1,128)S(1)} %bitcast.7), channel_id=1, replica_groups=mesh['term'=8,'sector'=4] {'sector','term'}, dimensions={0} | all-to-all | bytes 32768 | tf_op jit(solution)/shard_map/all_to_all | solution.py:583
  104.4 0.0 collective-permute-done.14.other
  104.4 2.7 %finish.1 = (f32[2,48,4,384]{3,2,1,0:T(4,128)}, f32[1]{0:T(128)}) custom-call(s32[6]{0:T(128)S(1)} %pad_add_fusion.info.ints.ints_a, f32[32,128]{1,0:T(8,128)S(1)} %bitcast.6, f32[2,2,48,768]{3,2,1,0:T(8,128)S(1)} %get-tuple-element.72.mine, f32[2,2,48,768]{3,2,1,0:T(8,128)S(1)} %collective-permute-done.14.other), custom_call_target="tpu_custom_call" | custom-call | tf_op jit(solution)/shard_map/finish/pallas_call | solution.py:585
  (20 shorter events, 0.0 us)
Async XLA Ops:
  0.6 11.0 %copy-start.13 = (s32[2]{0:T(128)S(1)}, s32[2]{0:T(128)}, u32[]{:S(2)}) copy-start(s32[2]{0:T(128)} %sizes.1) | copy-start | bytes 28
  0.6 4.6 %copy-start = (f32[2,2,384,384]{3,2,1,0:T(8,128)S(1)}, f32[2,2,384,384]{3,2,1,0:T(8,128)}, u32[]{:S(2)}) copy-start(f32[2,2,384,384]{3,2,1,0:T(8,128)} %right_a.3) | copy-start | bytes 7077892
  0.7 11.0 %copy-start.16 = (s32[2]{0:T(128)S(1)}, s32[2]{0:T(128)}, u32[]{:S(2)}) copy-start(s32[2]{0:T(128)} %param.13) | copy-start | bytes 28
  0.7 11.1 %copy-start.15 = (f32[2,4,4]{2,1,0:T(4,128)S(1)}, f32[2,4,4]{2,1,0:T(4,128)}, u32[]{:S(2)}) copy-start(f32[2,4,4]{2,1,0:T(4,128)} %param.12) | copy-start | bytes 388
  4.8 24.2 %collective-permute-start.4 = (f32[2,2,384,384]{3,2,1,0:T(8,128)}, f32[2,2,384,384]{3,2,1,0:T(8,128)}, u32[]{:S(2)}, u32[]{:S(2)}) collective-permute-start(f32[2,2,384,384]{3,2,1,0:T(8,128)} %left_a.3), channel_id=1, source_target_pairs={{0,4},{4,0},{8,12},{12,8},{16,20},{20,16},{24,28},{28,24},{1,5},{5... | collective-permute-start | bytes 7077896 | tf_op jit(solution)/shard_map/ppermute | solution.py:409
  5.3 23.6 %collective-permute-start.5 = (f32[2,2,384,384]{3,2,1,0:T(8,128)S(1)}, f32[2,2,384,384]{3,2,1,0:T(8,128)}, u32[]{:S(2)}, u32[]{:S(2)}) collective-permute-start(f32[2,2,384,384]{3,2,1,0:T(8,128)S(1)} %copy-done), channel_id=1, source_target_pairs={{0,4},{4,0},{8,12},{12,8},{16,20},{20,16},{24,28},{28,24},{1,5},{5... | collective-permute-start | bytes 7077896 | tf_op jit(solution)/shard_map/ppermute | solution.py:409
  5.4 32.9 %collective-permute-start.2 = (f32[768,384]{1,0:T(8,128)}, f32[768,384]{1,0:T(8,128)S(1)}, u32[]{:S(2)}, u32[]{:S(2)}) collective-permute-start(f32[768,384]{1,0:T(8,128)} %get-tuple-element.40), channel_id=1, source_target_pairs={{0,1},{1,2},{2,3},{4,5},{5,6},{6,7},{8,9},{9,10},{10,11},{12,13},{... | collective-permute-start | bytes 3538952 | tf_op jit(solution)/shard_map/ppermute | solution.py:471
  10.3 29.9 %collective-permute-start.3 = (f32[768,384]{1,0:T(8,128)}, f32[768,384]{1,0:T(8,128)}, u32[]{:S(2)}, u32[]{:S(2)}) collective-permute-start(f32[768,384]{1,0:T(8,128)} %get-tuple-element.41), channel_id=1, source_target_pairs={{1,0},{2,1},{3,2},{5,4},{6,5},{7,6},{9,8},{10,9},{11,10},{13,12},{... | collective-permute-start | bytes 3538952 | tf_op jit(solution)/shard_map/ppermute | solution.py:472
  11.8 1.4 %collective-permute-start = (s32[6]{0:T(128)S(1)}, s32[6]{0:T(128)S(1)}, u32[]{:S(2)}, u32[]{:S(2)}) collective-permute-start(s32[6]{0:T(128)S(1)} %pad_add_fusion.info.ints.ints_a), channel_id=1, source_target_pairs={{0,4},{4,0},{8,12},{12,8},{16,20},{20,16},{24,28},{28,24},{1,5},{5... | collective-permute-start | bytes 80 | tf_op jit(solution)/shard_map/ppermute | solution.py:409
  13.1 15.8 %collective-permute-start.1 = (f32[34]{0:T(128)S(1)}, f32[34]{0:T(128)S(1)}, u32[]{:S(2)}, u32[]{:S(2)}) collective-permute-start(f32[34]{0:T(128)S(1)} %pad_maximum_fusion.floats.floats_a), channel_id=1, source_target_pairs={{0,4},{4,0},{8,12},{12,8},{16,20},{20,16},{24,28},{28,24},{1,5},{5... | collective-permute-start | bytes 416 | tf_op jit(solution)/shard_map/ppermute | solution.py:409
  13.6 1.7 %copy-start.1 = (f32[2,2,384,384]{3,2,1,0:T(8,128)S(1)}, f32[2,2,384,384]{3,2,1,0:T(8,128)}, u32[]{:S(2)}) copy-start(f32[2,2,384,384]{3,2,1,0:T(8,128)} %left_a.3) | copy-start | bytes 7077892
  15.3 2.3 %copy-start.4 = (f32[2,384,4,384]{3,2,1,0:T(4,128)S(1)}, f32[2,384,4,384]{3,2,1,0:T(4,128)}, u32[]{:S(2)}) copy-start(f32[2,384,4,384]{3,2,1,0:T(4,128)} %refs_0_.1) | copy-start | bytes 14155780
  28.1 0.8 copy-start.7
  36.8 1.5 %copy-start.5 = (f32[2,384,768]{2,1,0:T(8,128)}, f32[2,384,768]{2,1,0:T(8,128)S(1)}, u32[]{:S(2)}) copy-start(f32[2,384,768]{2,1,0:T(8,128)S(1)} %near_partner.1.base) | copy-start | bytes 7077892
  40.2 13.8 %collective-permute-start.6 = (f32[768,384]{1,0:T(8,128)S(1)}, f32[768,384]{1,0:T(8,128)}, u32[]{:S(2)}, u32[]{:S(2)}) collective-permute-start(f32[768,384]{1,0:T(8,128)S(1)} %collective-permute-done.2.low), channel_id=1, source_target_pairs={{0,4},{4,0},{8,12},{12,8},{16,20},{20,16},{24,28},{28,24},{1,5},{5... | collective-permute-start | bytes 3538952 | tf_op jit(solution)/shard_map/ppermute | solution.py:409
  40.2 13.8 %collective-permute-start.7 = (f32[768,384]{1,0:T(8,128)}, f32[768,384]{1,0:T(8,128)}, u32[]{:S(2)}, u32[]{:S(2)}) collective-permute-start(f32[768,384]{1,0:T(8,128)} %collective-permute-done.3.high), channel_id=1, source_target_pairs={{0,4},{4,0},{8,12},{12,8},{16,20},{20,16},{24,28},{28,24},{1,5},{5... | collective-permute-start | bytes 3538952 | tf_op jit(solution)/shard_map/ppermute | solution.py:409
  40.8 1.7 %copy-start.2 = (f32[2,2,384,384]{3,2,1,0:T(8,128)S(1)}, f32[2,2,384,384]{3,2,1,0:T(8,128)}, u32[]{:S(2)}) copy-start(f32[2,2,384,384]{3,2,1,0:T(8,128)} %left_a.3) | copy-start | bytes 7077892
  42.4 1.7 %copy-start.6 = (f32[2,384,768]{2,1,0:T(8,128)S(1)}, f32[2,384,768]{2,1,0:T(8,128)}, u32[]{:S(2)}) copy-start(f32[2,384,768]{2,1,0:T(8,128)} %copy-done.5) | copy-start | bytes 7077892
  44.1 10.0 %copy-start.3 = (f32[2,2,384,384]{3,2,1,0:T(8,128)S(1)}, f32[2,2,384,384]{3,2,1,0:T(8,128)}, u32[]{:S(2)}) copy-start(f32[2,2,384,384]{3,2,1,0:T(8,128)} %left_a.3) | copy-start | bytes 7077892
  54.0 13.3 %copy-start.14 = (s32[2]{0:T(128)S(1)}, s32[2]{0:T(128)}, u32[]{:S(2)}) copy-start(s32[2]{0:T(128)} %sizes.1) | copy-start | bytes 28
  65.8 0.7 copy-start.9
  66.6 0.7 copy-start.11
  67.3 4.9 %copy-start.12 = (f32[2,48,768]{2,1,0:T(8,128)S(1)}, f32[2,48,768]{2,1,0:T(8,128)}, u32[]{:S(2)}) copy-start(f32[2,48,768]{2,1,0:T(8,128)} %copy-done.11) | copy-start | bytes 884740
  67.3 6.7 %copy-start.10 = (f32[2,48,768]{2,1,0:T(8,128)S(1)}, f32[2,48,768]{2,1,0:T(8,128)}, u32[]{:S(2)}) copy-start(f32[2,48,768]{2,1,0:T(8,128)} %copy-done.9) | copy-start | bytes 884740
  67.5 10.2 %collective-permute-start.9 = (f32[2,48,768]{2,1,0:T(8,128)}, f32[2,48,768]{2,1,0:T(8,128)}, u32[]{:S(2)}, u32[]{:S(2)}) collective-permute-start(f32[2,48,768]{2,1,0:T(8,128)} %get-tuple-element.64), channel_id=1, source_target_pairs={{0,8},{4,12},{8,0},{12,4},{16,24},{20,28},{24,16},{28,20},{1,9},{5... | collective-permute-start | bytes 884744 | tf_op jit(solution)/shard_map/ppermute | solution.py:423
  67.6 11.3 %collective-permute-start.12 = (f32[2,48,768]{2,1,0:T(8,128)}, f32[2,48,768]{2,1,0:T(8,128)}, u32[]{:S(2)}, u32[]{:S(2)}) collective-permute-start(f32[2,48,768]{2,1,0:T(8,128)} %get-tuple-element.68), channel_id=1, source_target_pairs={{0,16},{4,20},{8,24},{12,28},{16,0},{20,4},{24,8},{28,12},{1,17},{... | collective-permute-start | bytes 884744 | tf_op jit(solution)/shard_map/ppermute | solution.py:423
  69.6 20.6 %copy-start.8 = (f32[2,2,48,768]{3,2,1,0:T(8,128)S(1)}, f32[2,2,48,768]{3,2,1,0:T(8,128)}, u32[]{:S(2)}) copy-start(f32[2,2,48,768]{3,2,1,0:T(8,128)} %copy-done.7) | copy-start | bytes 1769476
  72.3 11.7 %collective-permute-start.8 = (f32[2,48,768]{2,1,0:T(8,128)S(1)}, f32[2,48,768]{2,1,0:T(8,128)S(1)}, u32[]{:S(2)}, u32[]{:S(2)}) collective-permute-start(f32[2,48,768]{2,1,0:T(8,128)S(1)} %copy-done.12), channel_id=1, source_target_pairs={{0,8},{4,12},{8,0},{12,4},{16,24},{20,28},{24,16},{28,20},{1,9},{5... | collective-permute-start | bytes 884744 | tf_op jit(solution)/shard_map/ppermute | solution.py:423
  74.0 10.1 %collective-permute-start.11 = (f32[2,48,768]{2,1,0:T(8,128)S(1)}, f32[2,48,768]{2,1,0:T(8,128)S(1)}, u32[]{:S(2)}, u32[]{:S(2)}) collective-permute-start(f32[2,48,768]{2,1,0:T(8,128)S(1)} %copy-done.10), channel_id=1, source_target_pairs={{0,16},{4,20},{8,24},{12,28},{16,0},{20,4},{24,8},{28,12},{1,17},{... | collective-permute-start | bytes 884744 | tf_op jit(solution)/shard_map/ppermute | solution.py:423
  78.7 11.4 %collective-permute-start.10 = (f32[2,48,768]{2,1,0:T(8,128)S(1)}, f32[2,48,768]{2,1,0:T(8,128)S(1)}, u32[]{:S(2)}, u32[]{:S(2)}) collective-permute-start(f32[2,48,768]{2,1,0:T(8,128)S(1)} %add.22), channel_id=1, source_target_pairs={{0,16},{4,20},{8,24},{12,28},{16,0},{20,4},{24,8},{28,12},{1,17},{... | collective-permute-start | bytes 884744 | tf_op jit(solution)/shard_map/ppermute | solution.py:423
  79.8 10.3 %collective-permute-start.13 = (f32[2,48,768]{2,1,0:T(8,128)S(1)}, f32[2,48,768]{2,1,0:T(8,128)S(1)}, u32[]{:S(2)}, u32[]{:S(2)}) collective-permute-start(f32[2,48,768]{2,1,0:T(8,128)S(1)} %add.23), channel_id=1, source_target_pairs={{0,8},{4,12},{8,0},{12,4},{16,24},{20,28},{24,16},{28,20},{1,9},{5... | collective-permute-start | bytes 884744 | tf_op jit(solution)/shard_map/ppermute | solution.py:423
  91.3 13.1 %collective-permute-start.14 = (f32[2,2,48,768]{3,2,1,0:T(8,128)S(1)}, f32[2,2,48,768]{3,2,1,0:T(8,128)S(1)}, u32[]{:S(2)}, u32[]{:S(2)}) collective-permute-start(f32[2,2,48,768]{3,2,1,0:T(8,128)S(1)} %get-tuple-element.73), channel_id=1, source_target_pairs={{0,4},{4,0},{8,12},{12,8},{16,20},{20,16},{24,28},{28,24},{1,5},{5... | collective-permute-start | bytes 1769480 | tf_op jit(solution)/shard_map/ppermute | solution.py:409
